TPU v7x, 32 devices: a whole 2x2x4 slice. The times are simulated.
32 devices in a mesh: dp: 8 (over z, core), seq: 4 (over y, x).
Axes of the slice: x: 2, y: 2, z: 4, core: 2. Of those that a mesh axis runs over, the one named last changes fastest.
Arguments:
- tokens: bfloat16 [8, 2048, 2048], P('dp', 'seq'), may hold values from -6 to 6
- joined_weight: bfloat16 [2048, 1920], P(('dp', 'seq')), may hold values from -0.125 to 0.125
- output_weight: bfloat16 [1280, 2048], P(None, ('dp', 'seq')), may hold values from -2.5 to 2.5
- expand_weight: bfloat16 [2048, 12288], P(('dp', 'seq')), may hold values from -0.125 to 0.125
- shrink_weight: bfloat16 [6144, 2048], P(None, ('dp', 'seq')), may hold values from -0.078125 to 0.078125
- norm_gains: bfloat16 [4224], P(('dp', 'seq')), may hold values from 0.25 to 1.75
- doc_lengths: int32 [8, 4], P('dp'), may hold values from 1 to 2045, as said below
- cotangent: bfloat16 [8, 2048, 2048], P('dp', 'seq'), may hold values from -6 to 6
Outputs:
- layer_output: bfloat16 [8, 2048, 2048], P('dp', 'seq')
- token_gradient: bfloat16 [8, 2048, 2048], P('dp', 'seq')
- joined_gradient: float32 [2048, 1920], P(('dp', 'seq'))
- output_gradient: float32 [1280, 2048], P(None, ('dp', 'seq'))
- expand_gradient: float32 [2048, 12288], P(('dp', 'seq'))
- shrink_gradient: float32 [6144, 2048], P(None, ('dp', 'seq'))
- gains_gradient: float32 [4224], P(('dp', 'seq'))
Inputs may be any that keep to these rules, and one draw needn't show every extreme that they name: `doc_lengths`: each row's lengths sum to 2048. Each row holds one document that starts within the first device's share of the row along seq and ends within the last one's; in some row that document has 2045 tokens.
All inputs are finite; a program needn't handle non-finite values.
Results may differ from a plain program's by a relative error of at most 0.015.
Values may be sent and summed in bfloat16 or wider, within the bound.
A program may use at most 384 MiB of HBM per device.

v0:
```python
import jax
import jax.numpy as jnp
from jax import lax
from jax.sharding import PartitionSpec as P

D = 2048
HEADS = 20
KV_HEADS = 5
HEAD_DIM = 64
FF = 6144
ROW_LEN = 2048


epsilon = 1e-05
masked_fill = -1e30


def rms_scale(values):
    return lax.rsqrt(jnp.mean(values * values, axis=-1, keepdims=True) + epsilon)


def norm_back(upstream, values, scaling, gain_vector):
    weighted = upstream * gain_vector
    average = jnp.mean(weighted * values, axis=-1, keepdims=True)
    return scaling * weighted - values * (scaling * scaling * scaling) * average


def rope_tables(positions):
    half_dim = HEAD_DIM // 2
    frequency = 10000.0 ** (-jnp.arange(half_dim, dtype=jnp.float32) / half_dim)
    angles = positions.astype(jnp.float32)[:, None] * frequency[None, :]
    return (jnp.cos(angles), jnp.sin(angles))


def rotate(values, cosine, sine_table):
    half_dim = values.shape[-1] // 2
    first_half = values[..., :half_dim]
    second_half = values[..., half_dim:]
    return jnp.concatenate(
        [
            first_half * cosine - second_half * sine_table,
            second_half * cosine + first_half * sine_table,
        ],
        axis=-1,
    )


def rotate_back(gradient, cosine, sine_table):
    half_dim = gradient.shape[-1] // 2
    first_half = gradient[..., :half_dim]
    second_half = gradient[..., half_dim:]
    return jnp.concatenate(
        [
            first_half * cosine + second_half * sine_table,
            second_half * cosine - first_half * sine_table,
        ],
        axis=-1,
    )


def document_ids(doc_lengths):
    bounds = jnp.cumsum(doc_lengths, axis=-1)[:, :-1]
    places = jnp.arange(ROW_LEN, dtype=jnp.int32)
    return jnp.sum((places[None, :, None] >= bounds[:, None, :]).astype(jnp.int32), axis=-1)


def contract(left, right, left_dim, right_dim):
    return lax.dot_general(
        left, right, (((left_dim,), (right_dim,)), ((), ())), preferred_element_type=jnp.float32
    )


def body(
    tokens,
    joined_weight,
    output_weight,
    expand_weight,
    shrink_weight,
    norm_gains,
    doc_lengths,
    cotangent,
):
    row_count, local_len, width = tokens.shape
    token_count = row_count * local_len
    group_size = HEADS // KV_HEADS
    query_width = HEADS * HEAD_DIM
    kv_width = KV_HEADS * HEAD_DIM
    score_scale = HEAD_DIM ** (-0.5)
    offset = lax.axis_index("seq") * local_len
    query_pos = offset + jnp.arange(local_len, dtype=jnp.int32)
    cosine, sine_table = rope_tables(query_pos)
    cosine = cosine[None, :, None, :]
    sine_table = sine_table[None, :, None, :]
    doc_index = document_ids(doc_lengths)
    query_docs = lax.dynamic_slice_in_dim(doc_index, offset, local_len, 1)

    def allowed(piece_len):
        key_pos = jnp.arange(piece_len, dtype=jnp.int32)
        same_doc = query_docs[:, :, None] == doc_index[:, None, :]
        causal = key_pos[None, :] <= query_pos[:, None]
        return (same_doc & causal[None])[:, None, None]

    joined_all, output_all, gains_all = (
        lax.all_gather(joined_weight, ("dp", "seq"), axis=0, tiled=True),
        lax.all_gather(output_weight, ("dp", "seq"), axis=1, tiled=True),
        lax.all_gather(norm_gains, ("dp", "seq"), axis=0, tiled=True),
    )
    gains_float = gains_all.astype(jnp.float32)
    gain_one = gains_float[:D]
    gain_query = gains_float[D : D + HEAD_DIM]
    gain_key = gains_float[D + HEAD_DIM : D + 2 * HEAD_DIM]
    gain_two = gains_float[D + 2 * HEAD_DIM :]
    flat = tokens.reshape(token_count, width).astype(jnp.float32)
    scale_one = rms_scale(flat)
    normed_low = (flat * scale_one * gain_one).astype(jnp.bfloat16)
    projected = jnp.dot(normed_low, joined_all, preferred_element_type=jnp.float32)
    queries = projected[:, :query_width].reshape(row_count, local_len, HEADS, HEAD_DIM)
    key_rows = projected[:, query_width : query_width + kv_width].reshape(
        row_count, local_len, KV_HEADS, HEAD_DIM
    )
    value_rows = projected[:, query_width + kv_width :].reshape(row_count, local_len, kv_width)
    scale_query = rms_scale(queries)
    scale_key = rms_scale(key_rows)
    query_low = rotate(queries * scale_query * gain_query, cosine, sine_table).astype(jnp.bfloat16)
    query_low = query_low.reshape(row_count, local_len, KV_HEADS, group_size, HEAD_DIM)
    key_low = rotate(key_rows * scale_key * gain_key, cosine, sine_table).astype(jnp.bfloat16)
    kv_stack = jnp.concatenate(
        [key_low.reshape(row_count, local_len, kv_width), value_rows.astype(jnp.bfloat16)], axis=-1
    )

    def split_piece(pieces):
        piece_len = pieces.shape[1]
        key_piece = pieces[..., :kv_width].reshape(row_count, piece_len, KV_HEADS, HEAD_DIM)
        value_piece = pieces[..., kv_width:].reshape(row_count, piece_len, KV_HEADS, HEAD_DIM)
        return (key_piece, value_piece, piece_len)

    running_max = jnp.full((row_count, KV_HEADS, group_size, local_len), masked_fill, jnp.float32)
    key_piece, value_piece, piece_len = split_piece(
        lax.all_gather(kv_stack, "seq", axis=1, tiled=True)
    )
    allowed_mask = allowed(piece_len)
    scores = (
        jnp.einsum("rqhgd,rkhd->rhgqk", query_low, key_piece, preferred_element_type=jnp.float32)
        * score_scale
    )
    scores = jnp.where(allowed_mask, scores, masked_fill)
    new_max = jnp.maximum(running_max, jnp.max(scores, axis=-1))
    expo = jnp.where(allowed_mask, jnp.exp(scores - new_max[..., None]), 0.0)
    running_sum = jnp.sum(expo, axis=-1)
    mixed = jnp.einsum(
        "rhgqk,rkhd->rqhgd",
        expo.astype(jnp.bfloat16),
        value_piece,
        preferred_element_type=jnp.float32,
    )
    weighted = mixed
    running_max, running_sum, weighted = (new_max, running_sum, weighted)
    log_total = running_max + jnp.log(running_sum)
    attended = weighted / jnp.transpose(running_sum, (0, 3, 1, 2))[..., None]
    attended_low = attended.astype(jnp.bfloat16).reshape(token_count, query_width)
    residual = flat + jnp.dot(attended_low, output_all, preferred_element_type=jnp.float32)
    scale_two = rms_scale(residual)
    normed_two = (residual * scale_two * gain_two).astype(jnp.bfloat16)
    expand_all, shrink_all = (
        lax.all_gather(expand_weight, ("dp", "seq"), axis=0, tiled=True),
        lax.all_gather(shrink_weight, ("dp", "seq"), axis=1, tiled=True),
    )
    both_pre = jnp.dot(normed_two, expand_all, preferred_element_type=jnp.float32)
    gate_pre = both_pre[:, :FF]
    up_pre = both_pre[:, FF:]
    gate_sigmoid = jax.nn.sigmoid(gate_pre)
    hidden_low = (gate_pre * gate_sigmoid * up_pre).astype(jnp.bfloat16)
    result = residual + jnp.dot(hidden_low, shrink_all, preferred_element_type=jnp.float32)
    layer_output = result.astype(jnp.bfloat16).reshape(row_count, local_len, width)
    expand_back, shrink_back = (
        lax.all_gather(expand_weight, ("dp", "seq"), axis=0, tiled=True),
        lax.all_gather(shrink_weight, ("dp", "seq"), axis=1, tiled=True),
    )
    upstream_low = cotangent.reshape(token_count, width)
    upstream = upstream_low.astype(jnp.float32)
    grad_hidden = contract(upstream_low, shrink_back, 1, 1)
    grad_gate = grad_hidden * up_pre * gate_sigmoid * (1.0 + gate_pre * (1.0 - gate_sigmoid))
    grad_up = grad_hidden * gate_pre * gate_sigmoid
    grad_both = jnp.concatenate([grad_gate, grad_up], axis=1).astype(jnp.bfloat16)
    grad_normed_two = contract(grad_both, expand_back, 1, 1)
    gain_two_grad = jnp.sum(grad_normed_two * residual * scale_two, axis=0)
    grad_residual = upstream + norm_back(grad_normed_two, residual, scale_two, gain_two)
    shrink_term = contract(hidden_low, upstream_low, 0, 0)
    expand_term = contract(normed_two, grad_both, 0, 0)
    expand_gradient, shrink_gradient = (
        lax.psum_scatter(expand_term, ("dp", "seq"), scatter_dimension=0, tiled=True),
        lax.psum_scatter(shrink_term, ("dp", "seq"), scatter_dimension=1, tiled=True),
    )
    joined_back, output_back = (
        lax.all_gather(joined_weight, ("dp", "seq"), axis=0, tiled=True),
        lax.all_gather(output_weight, ("dp", "seq"), axis=1, tiled=True),
    )
    grad_attn_low = grad_residual.astype(jnp.bfloat16)
    output_term = contract(attended_low, grad_attn_low, 0, 0)
    grad_out_low = contract(grad_attn_low, output_back, 1, 1).astype(jnp.bfloat16)
    grad_out_low = grad_out_low.reshape(row_count, local_len, KV_HEADS, group_size, HEAD_DIM)
    row_inner = jnp.sum(grad_out_low.astype(jnp.float32) * attended, axis=-1)
    row_inner = jnp.transpose(row_inner, (0, 2, 3, 1))
    key_piece, value_piece, piece_len = split_piece(
        lax.all_gather(kv_stack, "seq", axis=1, tiled=True)
    )
    allowed_mask = allowed(piece_len)
    scores = (
        jnp.einsum("rqhgd,rkhd->rhgqk", query_low, key_piece, preferred_element_type=jnp.float32)
        * score_scale
    )
    scores = jnp.where(allowed_mask, scores, masked_fill)
    probability = jnp.where(allowed_mask, jnp.exp(scores - log_total[..., None]), 0.0)
    grad_prob = jnp.einsum(
        "rqhgd,rkhd->rhgqk", grad_out_low, value_piece, preferred_element_type=jnp.float32
    )
    grad_scores = (probability * (grad_prob - row_inner[..., None])).astype(jnp.bfloat16)
    grad_query = (
        jnp.einsum("rhgqk,rkhd->rqhgd", grad_scores, key_piece, preferred_element_type=jnp.float32)
        * score_scale
    )
    key_term = (
        jnp.einsum("rhgqk,rqhgd->rkhd", grad_scores, query_low, preferred_element_type=jnp.float32)
        * score_scale
    )
    value_term = jnp.einsum(
        "rhgqk,rqhgd->rkhd",
        probability.astype(jnp.bfloat16),
        grad_out_low,
        preferred_element_type=jnp.float32,
    )
    both_terms = jnp.concatenate(
        [
            key_term.reshape(row_count, piece_len, kv_width),
            value_term.reshape(row_count, piece_len, kv_width),
        ],
        axis=-1,
    )
    grad_query, grad_kv_all = (grad_query, both_terms)
    grad_kv = lax.psum_scatter(
        grad_kv_all.astype(jnp.bfloat16), "seq", scatter_dimension=1, tiled=True
    ).astype(jnp.float32)
    grad_key_rot = grad_kv[..., :kv_width].reshape(row_count, local_len, KV_HEADS, HEAD_DIM)
    grad_values = grad_kv[..., kv_width:].reshape(token_count, kv_width)
    grad_query_rot = rotate_back(
        grad_query.reshape(row_count, local_len, HEADS, HEAD_DIM), cosine, sine_table
    )
    grad_key_norm = rotate_back(grad_key_rot, cosine, sine_table)
    gain_query_grad = jnp.sum(grad_query_rot * queries * scale_query, axis=(0, 1, 2))
    gain_key_grad = jnp.sum(grad_key_norm * key_rows * scale_key, axis=(0, 1, 2))
    grad_queries = norm_back(grad_query_rot, queries, scale_query, gain_query)
    grad_keys = norm_back(grad_key_norm, key_rows, scale_key, gain_key)
    grad_projected = jnp.concatenate(
        [
            grad_queries.reshape(token_count, query_width),
            grad_keys.reshape(token_count, kv_width),
            grad_values,
        ],
        axis=1,
    ).astype(jnp.bfloat16)
    joined_term = contract(normed_low, grad_projected, 0, 0)
    grad_normed = contract(grad_projected, joined_back, 1, 1)
    gain_one_grad = jnp.sum(grad_normed * flat * scale_one, axis=0)
    token_gradient = grad_residual + norm_back(grad_normed, flat, scale_one, gain_one)
    gains_term = jnp.concatenate([gain_one_grad, gain_query_grad, gain_key_grad, gain_two_grad])
    joined_gradient, output_gradient, gains_gradient = (
        lax.psum_scatter(joined_term, ("dp", "seq"), scatter_dimension=0, tiled=True),
        lax.psum_scatter(output_term, ("dp", "seq"), scatter_dimension=1, tiled=True),
        lax.psum_scatter(gains_term, ("dp", "seq"), scatter_dimension=0, tiled=True),
    )
    return (
        layer_output,
        token_gradient.astype(jnp.bfloat16).reshape(row_count, local_len, width),
        joined_gradient,
        output_gradient,
        expand_gradient,
        shrink_gradient,
        gains_gradient,
    )


def solution(mesh):
    placed = (
        P("dp", "seq", None),
        P(("dp", "seq"), None),
        P(None, ("dp", "seq")),
        P(("dp", "seq"), None),
        P(None, ("dp", "seq")),
        P(("dp", "seq")),
        P("dp", None),
        P("dp", "seq", None),
    )
    return jax.shard_map(
        body,
        mesh=mesh,
        in_specs=placed,
        out_specs=(
            P("dp", "seq", None),
            P("dp", "seq", None),
            P(("dp", "seq"), None),
            P(None, ("dp", "seq")),
            P(("dp", "seq"), None),
            P(None, ("dp", "seq")),
            P(("dp", "seq")),
        ),
        check_vma=False,
    )
```

profile of v0, /device:TPU:0, one launch (start us, length us, event | category | flops | bytes accessed | tf_op | source)
XLA Modules:
  0.0 2555.8 jit_solution(3590372819697121886)
XLA Ops:
  8.8 42.5 %all-reduce = bf16[4224]{0:T(1024)(128)(2,1)S(1)} all-reduce(bf16[4224]{0:T(1024)(128)(2,1)S(1)} %dynamic-update-slice), channel_id=1, replica_groups=mesh['dp'=8,'seq'=4] {'dp','seq'}, use_global_device_ids=true, to_apply=%add | all-reduce | flops 4224 | bytes 16896
  54.5 35.2 %all-gather.6.cloned.1.call-done = bf16[2048,1920]{1,0:T(8,128)(2,1)} async-done(((bf16[64,1920]{1,0:T(8,128)(2,1)}), bf16[2048,1920]{1,0:T(8,128)(2,1)}) %all-gather.6.cloned.1.call-update) | async-done | bytes 7864336 | tf_op jit(solution)/shard_map/all_gather | solution.py:104
  89.7 7.7 fusion.53
  116.2 24.8 all-gather.8.cloned.1.call-done
  146.9 31.5 %fusion.5 = (f32[5,4,512]{2,1,0:T(4,128)S(1)}, f32[5,2048,512,4]{2,1,3,0:T(8,128)}) fusion(pred[512,2048]{0,1:T(8,128)(4,1)} %fusion.27, bf16[2048,5,64,1]{0,2,3,1:T(8,128)(2,1)} %bitcast.203, bf16[512,5,4,32]{0,3,2,1:T(8,128)(2,1)} %bitcast.207, bf16[512,5,4,32]{0,3,2,1:T(8,128)(2,1)} %bitcast.205), kind=kOutput, calls=%fused_computation.9 | convolution fusion | flops 2749880320 | bytes 87597056 | tf_op jit(solution)/shard_map/rqhgd,rkhd->rhgqk/dot_general | solution.py:143
  178.4 27.6 %fusion.2 = f32[5,4,512]{2,1,0:T(4,128)S(1)} fusion(f32[5,2048,512,4]{2,1,3,0:T(8,128)} %get-tuple-element.49, f32[5,4,512]{2,1,0:T(4,128)S(1)} %broadcast_maximum_fusion, pred[512,2048]{0,1:T(8,128)(4,1)S(1)} %copy-done.9), kind=kLoop, calls=%fused_computation.6 | loop fusion | flops 104847360 | bytes 85016576 | tf_op jit(solution)/shard_map/reduce_sum | solution.py:149
  206.0 34.6 %fusion.72 = (bf16[1,512,5,4,64]{1,4,3,2,0:T(8,128)(2,1)}, f32[1,512,5,4,64]{1,4,3,2,0:T(8,128)}) fusion(f32[512,5,4]{0,2,1:T(4,128)S(1)} %bitcast.219, bf16[2048,5,64,1]{0,2,3,1:T(8,128)(2,1)} %bitcast.211, f32[5,2048,512,4]{2,1,3,0:T(8,128)} %get-tuple-element.49, f32[5,4,512]{2,1,0:T(4,128)S(1)} %broadcast_maximum_fusion, ...), kind=kOutput, calls=%fused_computation.138 | convolution fusion | flops 2790522880 | bytes 90259456 | tf_op jit(solution)/shard_map/rhgqk,rkhd->rqhgd/dot_general | solution.py:150
  240.7 8.0 multiply_reduce_fusion.2
  249.8 237.1 %all-gather.12.cloned.1.call-done = bf16[2048,12288]{1,0:T(8,128)(2,1)} async-done(((bf16[64,12288]{1,0:T(8,128)(2,1)}), bf16[2048,12288]{1,0:T(8,128)(2,1)}) %all-gather.12.cloned.1.call-update) | async-done | bytes 50331664 | tf_op jit(solution)/shard_map/all_gather | solution.py:165
  486.9 37.4 %fusion.68 = f32[512,12288]{1,0:T(8,128)} fusion(bf16[2048,12288]{1,0:T(8,128)(2,1)} %all-gather.12.cloned.1.call-done, f32[512,2048]{1,0:T(8,128)} %get-tuple-element.53, f32[2048]{0:T(1024)S(1)} %get-tuple-element.38, f32[512]{0:T(512)S(1)} %get-tuple-element.47), kind=kOutput, calls=%fused_computation.134 | convolution fusion | flops 25772949504 | bytes 79702016 | tf_op jit(solution)/shard_map/dot_general | solution.py:168
  524.3 118.2 %all-gather.14.cloned.1.call-done = bf16[6144,2048]{0,1:T(8,128)(2,1)} async-done(((bf16[6144,64]{0,1:T(8,128)(2,1)}), bf16[6144,2048]{0,1:T(8,128)(2,1)}) %all-gather.14.cloned.1.call-update) | async-done | bytes 25165840 | tf_op jit(solution)/shard_map/all_gather | solution.py:166
  642.5 31.8 %multiply_convert_fusion.1 = (bf16[512,6144]{1,0:T(8,128)(2,1)}, bf16[512,6144]{1,0:T(8,128)(2,1)}, bf16[512,6144]{1,0:T(8,128)(2,1)}) fusion(f32[512,12288]{1,0:T(8,128)} %fusion.68, bf16[6144,2048]{0,1:T(8,128)(2,1)} %all-gather.14.cloned.1.call-done, bf16[1,512,2048]{2,1,0:T(8,128)(2,1)S(1)} %copy-done.18), kind=kOutput, calls=%fused_computation.19 | convolution fusion | flops 12935233536 | bytes 71303168 | tf_op jit(solution)/shard_map/dot_general | solution.py:68
  674.4 36.4 %multiply_reduce_fusion = (f32[2048]{0:T(1024)}, f32[512]{0:T(512)S(1)}, f32[512,2048]{1,0:T(8,128)}) fusion(f32[512,2048]{1,0:T(8,128)} %get-tuple-element.53, f32[512]{0:T(512)S(1)} %get-tuple-element.47, f32[2048]{0:T(1024)S(1)} %get-tuple-element.38, bf16[2048,12288]{1,0:T(8,128)(2,1)} %all-gather.12.cloned.1.call-done, ...), kind=kOutput, calls=%fused_computation.40 | convolution fusion | flops 25801259008 | bytes 71323648 | tf_op jit(solution)/shard_map/dot_general | solution.py:68
  710.7 4.9 subtract_add_fusion
  717.6 3.9 convolution_convert_fusion
  728.1 37.8 %fusion.34 = bf16[5,64,2048]{2,1,0:T(8,128)(2,1)S(1)} fusion(bf16[512,5,4,64]{0,3,2,1:T(8,128)(2,1)} %bitcast.213, f32[5,2048,512,4]{2,1,3,0:T(8,128)} %get-tuple-element.49, f32[5,4,512]{2,1,0:T(4,128)S(1)} %copy-done.31, pred[512,2048]{0,1:T(8,128)(4,1)} %fusion.27), kind=kOutput, calls=%fused_computation.54 | convolution fusion | flops 2789867520 | bytes 87597056 | tf_op jit(solution)/shard_map/rhgqk,rqhgd->rkhd/dot_general | solution.py:226
  765.9 48.5 %fusion.8 = bf16[5,4,512,2048]{2,3,1,0:T(8,128)(2,1)} fusion(f32[5,2048,512,4]{2,1,3,0:T(8,128)} %get-tuple-element.49, f32[5,4,512]{2,1,0:T(4,128)S(1)} %bitcast.220, f32[5,4,512]{2,1,0:T(4,128)S(1)} %copy-done.31, pred[512,2048]{0,1:T(8,128)(4,1)S(1)} %copy-done.10, bf16[2048,5,64,1]{0,2,3,1:T(8,128)(2,1)} %bitcast.212, bf16[512,5,4,64]{0,3,2,1:T(8,128)(2,1)} %bitcast.214), kind=kOutput, calls=%fused_computation.12 | convolution fusion | flops 2831155200 | bytes 129581056 | tf_op jit(solution)/shard_map/rqhgd,rkhd->rhgqk/dot_general | solution.py:214
  814.4 18.1 fusion.33
  834.3 9.4 fusion.44
  849.4 17.6 convolution_multiply_fusion
  876.8 7.0 multiply_reduce_fusion.3
  890.7 9.6 fusion.51
  901.9 22.7 fusion.38
  925.3 43.9 %fusion.15 = f32[2048,12288]{1,0:T(8,128)} fusion(bf16[512,6144]{1,0:T(8,128)(2,1)} %get-tuple-element.12, bf16[512,6144]{1,0:T(8,128)(2,1)} %get-tuple-element.11, f32[512,2048]{1,0:T(8,128)} %get-tuple-element.53, f32[2048]{0:T(1024)S(1)} %copy-done.12, f32[512]{0:T(512)S(1)} %copy-done.17), kind=kOutput, calls=%fused_computation.28 | convolution fusion | flops 25798115328 | bytes 117450752 | tf_op jit(solution)/shard_map/dot_general | solution.py:68
  969.4 21.2 fusion.32
  991.0 10.8 fusion.26
  1001.8 40.1 %all-reduce.1 = f32[4224]{0:T(1024)S(1)} all-reduce(f32[4224]{0:T(1024)S(1)} %concatenate.95), channel_id=7, replica_groups=mesh['dp'=8,'seq'=4] {'dp','seq'}, use_global_device_ids=true, to_apply=%region_24.25.clone | all-reduce | flops 4224 | bytes 33792
  1042.6 6.0 fusion.37
  1048.5 55.1 %reduce-scatter.10.cloned.1.call-done = f32[1280,64]{0,1:T(8,128)} async-done(((f32[1280,2048]{0,1:T(8,128)}), f32[1280,64]{0,1:T(8,128)}) %reduce-scatter.10.cloned.1.call-update) | async-done | bytes 327696 | tf_op jit(solution)/shard_map/reduce_scatter | solution.py:268
  1103.6 178.0 %reduce-scatter.8.cloned.1.call-done = f32[64,1920]{1,0:T(8,128)} async-done(((f32[2048,1920]{1,0:T(8,128)}), f32[64,1920]{1,0:T(8,128)}) %reduce-scatter.8.cloned.1.call-update) | async-done | bytes 491536 | tf_op jit(solution)/shard_map/reduce_scatter | solution.py:267
  1281.6 437.9 %reduce-scatter.14.cloned.1.call-done = f32[6144,64]{0,1:T(8,128)} async-done(((f32[6144,2048]{0,1:T(8,128)}), f32[6144,64]{0,1:T(8,128)}) %reduce-scatter.14.cloned.1.call-update) | async-done | bytes 1572880 | tf_op jit(solution)/shard_map/reduce_scatter | solution.py:192
  1719.5 829.1 %reduce-scatter.12.cloned.1.call-done = f32[64,12288]{1,0:T(8,128)} async-done(((f32[2048,12288]{1,0:T(8,128)}), f32[64,12288]{1,0:T(8,128)}) %reduce-scatter.12.cloned.1.call-update) | async-done | bytes 3145744 | tf_op jit(solution)/shard_map/reduce_scatter | solution.py:191
  (190 shorter events, 66.2 us)
Async XLA Ops:
  7.2 82.5 %all-gather.6.cloned.1.call-start = ((), (), s32[]{:S(2)}) async-start(), calls=%async_computation.5 | async-start | bytes 8110080 | tf_op jit(solution)/shard_map/all_gather | solution.py:104
  7.9 133.1 %all-gather.8.cloned.1.call-start = ((), (), s32[]{:S(2)}) async-start(), calls=%async_computation.6 | async-start | bytes 3276800 | tf_op jit(solution)/shard_map/all_gather | solution.py:139
  51.5 49.2 %copy-start.35 = (f32[64]{0:T(128)}, f32[64]{0:T(128)S(1)}, u32[]{:S(2)}) copy-start(f32[64]{0:T(128)S(1)} %get-tuple-element.41) | copy-start | bytes 772
  51.5 62.7 %copy-start.43 = (f32[64]{0:T(128)}, f32[64]{0:T(128)S(1)}, u32[]{:S(2)}) copy-start(f32[64]{0:T(128)S(1)} %get-tuple-element.40) | copy-start | bytes 772
  54.2 43.3 %copy-start.40 = (f32[512]{0:T(512)}, f32[512]{0:T(512)S(1)}, u32[]{:S(2)}) copy-start(f32[512]{0:T(512)S(1)} %get-tuple-element.45) | copy-start | bytes 6148
  54.2 43.3 %copy-start.32 = (f32[2048]{0:T(1024)}, f32[2048]{0:T(1024)S(1)}, u32[]{:S(2)}) copy-start(f32[2048]{0:T(1024)S(1)} %get-tuple-element.39) | copy-start | bytes 24580
  54.2 656.6 %copy-start.11 = (f32[2048]{0:T(1024)}, f32[2048]{0:T(1024)S(1)}, u32[]{:S(2)}) copy-start(f32[2048]{0:T(1024)S(1)} %get-tuple-element.38) | copy-start | bytes 24580
  54.5 60.2 %copy-start.20 = (f32[512,32]{0,1:T(8,128)}, f32[512,32]{0,1:T(8,128)S(1)}, u32[]{:S(2)}) copy-start(f32[512,32]{0,1:T(8,128)S(1)} %get-tuple-element.42) | copy-start | bytes 196612
  54.5 60.2 %copy-start.22 = (f32[512,32]{0,1:T(8,128)}, f32[512,32]{0,1:T(8,128)S(1)}, u32[]{:S(2)}) copy-start(f32[512,32]{0,1:T(8,128)S(1)} %get-tuple-element.43) | copy-start | bytes 196612
  102.6 138.0 %all-gather.10.cloned.1.call-start = ((), (), s32[]{:S(2)}) async-start(), calls=%async_computation.7 | async-start | bytes 5406720 | tf_op jit(solution)/shard_map/all_gather | solution.py:105
  103.4 383.5 %all-gather.12.cloned.1.call-start = ((), (), s32[]{:S(2)}) async-start(), calls=%async_computation.8 | async-start | bytes 51904512 | tf_op jit(solution)/shard_map/all_gather | solution.py:165
  104.0 538.6 %all-gather.14.cloned.1.call-start = ((), (), s32[]{:S(2)}) async-start(), calls=%async_computation.9 | async-start | bytes 25952256 | tf_op jit(solution)/shard_map/all_gather | solution.py:166
  104.5 779.3 %reduce-scatter.6.cloned.1.call-start = ((), (), s32[]{:S(2)}) async-start(), calls=%async_computation.10 | async-start | bytes 3276800 | tf_op jit(solution)/shard_map/reduce_scatter | solution.py:240
  146.9 31.6 %copy-start.9 = (pred[512,2048]{0,1:T(8,128)(4,1)S(1)}, pred[512,2048]{0,1:T(8,128)(4,1)}, u32[]{:S(2)}) copy-start(pred[512,2048]{0,1:T(8,128)(4,1)} %fusion.27) | copy-start | bytes 3145732
  206.0 34.7 %copy-start.6 = (bf16[1,512,2048]{2,1,0:T(8,128)(2,1)S(1)}, bf16[1,512,2048]{2,1,0:T(8,128)(2,1)}, u32[]{:S(2)}) copy-start(bf16[1,512,2048]{2,1,0:T(8,128)(2,1)} %param.8) | copy-start | bytes 6291460
  249.2 461.5 %copy-start.16 = (f32[512]{0:T(512)}, f32[512]{0:T(512)S(1)}, u32[]{:S(2)}) copy-start(f32[512]{0:T(512)S(1)} %get-tuple-element.47) | copy-start | bytes 6148
  486.9 155.6 %copy-start.18 = (bf16[1,512,2048]{2,1,0:T(8,128)(2,1)S(1)}, bf16[1,512,2048]{2,1,0:T(8,128)(2,1)}, u32[]{:S(2)}) copy-start(bf16[1,512,2048]{2,1,0:T(8,128)(2,1)} %param.15) | copy-start | bytes 6291460
  674.4 36.4 %copy-start.37 = (f32[512]{0:T(512)S(1)}, f32[512]{0:T(512)}, u32[]{:S(2)}) copy-start(f32[512]{0:T(512)} %get-tuple-element.46) | copy-start | bytes 6148
  728.0 37.8 %copy-start.10 = (pred[512,2048]{0,1:T(8,128)(4,1)S(1)}, pred[512,2048]{0,1:T(8,128)(4,1)}, u32[]{:S(2)}) copy-start(pred[512,2048]{0,1:T(8,128)(4,1)} %fusion.27) | copy-start | bytes 3145732
  765.9 48.5 %copy-start.13 = (bf16[1,512,20,32]{1,3,2,0:T(8,128)(2,1)S(1)}, bf16[1,512,20,32]{1,3,2,0:T(8,128)(2,1)}, u32[]{:S(2)}) copy-start(bf16[1,512,20,32]{1,3,2,0:T(8,128)(2,1)} %get-tuple-element.18) | copy-start | bytes 1966084
  765.9 48.5 %copy-start.14 = (bf16[1,512,20,32]{1,3,2,0:T(8,128)(2,1)S(1)}, bf16[1,512,20,32]{1,3,2,0:T(8,128)(2,1)}, u32[]{:S(2)}) copy-start(bf16[1,512,20,32]{1,3,2,0:T(8,128)(2,1)} %get-tuple-element.19) | copy-start | bytes 1966084
  834.2 269.4 %reduce-scatter.10.cloned.1.call-start = ((), (), s32[]{:S(2)}) async-start(), calls=%async_computation.12 | async-start | bytes 10813440 | tf_op jit(solution)/shard_map/reduce_scatter | solution.py:268
  843.7 438.0 %reduce-scatter.8.cloned.1.call-start = ((), (), s32[]{:S(2)}) async-start(), calls=%async_computation.11 | async-start | bytes 16220160 | tf_op jit(solution)/shard_map/reduce_scatter | solution.py:267
  849.4 17.7 copy-start.23
  900.4 819.2 %reduce-scatter.14.cloned.1.call-start = ((), (), s32[]{:S(2)}) async-start(), calls=%async_computation.14 | async-start | bytes 51904512 | tf_op jit(solution)/shard_map/reduce_scatter | solution.py:192
  924.6 1624.1 %reduce-scatter.12.cloned.1.call-start = ((), (), s32[]{:S(2)}) async-start(), calls=%async_computation.13 | async-start | bytes 103809024 | tf_op jit(solution)/shard_map/reduce_scatter | solution.py:191
  969.3 21.2 copy-start.28
  969.3 21.3 copy-start.15
  969.3 21.6 copy-start.8
  969.4 21.6 copy-start.34
  969.4 21.6 copy-start.42
  990.9 51.6 %copy-start.39 = (f32[512]{0:T(512)S(1)}, f32[512]{0:T(512)}, u32[]{:S(2)}) copy-start(f32[512]{0:T(512)} %get-tuple-element.44) | copy-start | bytes 6148
  (25 other events, 96.0 us)
Sparse Core Ops, SparseCore 0:
  10.9 78.7 all-gather.5
  102.8 38.2 all-gather.7
  143.9 65.3 all-gather.9
  212.0 274.8 all-gather.11
  489.6 152.8 all-gather.13
  834.3 37.7 reduce-scatter.5
  875.1 228.5 reduce-scatter.9
  1110.2 171.3 reduce-scatter.7
  1288.7 430.8 reduce-scatter.13
  1726.4 822.2 reduce-scatter.11
where the time goes:
time: 2560 us
  waiting for transfers between devices  1920 us (75%)
  matrix products  431 us (17%)
  blocking collectives  82.7 us (3%)
  other arithmetic  64.1 us (3%)
  local copies, waits for them, and re-layouts  43.9 us (2%)
    reduce_scatter x1, waiting for transfers between devices, body(): lax.psum_scatter(expand_term, ('dp', 'seq'), scatter_dimension=0, tiled=T...  829 us
    reduce_scatter x1, waiting for transfers between devices, body(): lax.psum_scatter(shrink_term, ('dp', 'seq'), scatter_dimension=1, tiled=T...  438 us
    all_gather x1, waiting for transfers between devices, body(): lax.all_gather(expand_weight, ('dp', 'seq'), axis=0, tiled=True)  237 us
    reduce_scatter x1, waiting for transfers between devices, body(): lax.psum_scatter(joined_term, ('dp', 'seq'), scatter_dimension=0, tiled=T...  178 us
    dot_general x8, matrix products, contract(): lax.dot_general(left, right, (((left_dim,), (right_dim,)), ((), ())), pre...  168 us
    all_gather x1, waiting for transfers between devices, body(): lax.all_gather(shrink_weight, ('dp', 'seq'), axis=1, tiled=True)  118 us
    unnamed x2, blocking collectives  82.7 us
    reduce_scatter x1, waiting for transfers between devices, body(): lax.psum_scatter(output_term, ('dp', 'seq'), scatter_dimension=1, tiled=T...  55.1 us
  transfers between devices with their start and end apart: 10, of which 8 were waited for; matrix products, arithmetic and copies ran while one was open for 13% of the time, Pallas kernels for 0%

commit v1 on v0

--- a/solution.py
+++ b/solution.py
@@ -59,7 +59,10 @@
 
 
 def document_ids(doc_lengths):
-    bounds = jnp.cumsum(doc_lengths, axis=-1)[:, :-1]
+    ends = [doc_lengths[:, :1]]
+    for index in range(1, doc_lengths.shape[1] - 1):
+        ends.append(ends[-1] + doc_lengths[:, index : index + 1])
+    bounds = jnp.concatenate(ends, axis=1)
     places = jnp.arange(ROW_LEN, dtype=jnp.int32)
     return jnp.sum((places[None, :, None] >= bounds[:, None, :]).astype(jnp.int32), axis=-1)
 
@@ -188,8 +191,8 @@
     shrink_term = contract(hidden_low, upstream_low, 0, 0)
     expand_term = contract(normed_two, grad_both, 0, 0)
     expand_gradient, shrink_gradient = (
-        lax.psum_scatter(expand_term, ("dp", "seq"), scatter_dimension=0, tiled=True),
-        lax.psum_scatter(shrink_term, ("dp", "seq"), scatter_dimension=1, tiled=True),
+        lax.psum_scatter(expand_term.astype(jnp.bfloat16), ("dp", "seq"), scatter_dimension=0, tiled=True),
+        lax.psum_scatter(shrink_term.astype(jnp.bfloat16), ("dp", "seq"), scatter_dimension=1, tiled=True),
     )
     joined_back, output_back = (
         lax.all_gather(joined_weight, ("dp", "seq"), axis=0, tiled=True),
@@ -264,17 +267,17 @@
     token_gradient = grad_residual + norm_back(grad_normed, flat, scale_one, gain_one)
     gains_term = jnp.concatenate([gain_one_grad, gain_query_grad, gain_key_grad, gain_two_grad])
     joined_gradient, output_gradient, gains_gradient = (
-        lax.psum_scatter(joined_term, ("dp", "seq"), scatter_dimension=0, tiled=True),
-        lax.psum_scatter(output_term, ("dp", "seq"), scatter_dimension=1, tiled=True),
+        lax.psum_scatter(joined_term.astype(jnp.bfloat16), ("dp", "seq"), scatter_dimension=0, tiled=True),
+        lax.psum_scatter(output_term.astype(jnp.bfloat16), ("dp", "seq"), scatter_dimension=1, tiled=True),
         lax.psum_scatter(gains_term, ("dp", "seq"), scatter_dimension=0, tiled=True),
     )
     return (
         layer_output,
         token_gradient.astype(jnp.bfloat16).reshape(row_count, local_len, width),
-        joined_gradient,
-        output_gradient,
-        expand_gradient,
-        shrink_gradient,
+        joined_gradient.astype(jnp.float32),
+        output_gradient.astype(jnp.float32),
+        expand_gradient.astype(jnp.float32),
+        shrink_gradient.astype(jnp.float32),
         gains_gradient,
     )
 

time: 2560 us -> 1850 us (0.72)
  waiting for transfers between devices: 1920 us -> 1210 us
    reduce_scatter x4, waiting for transfers between devices: 1500 us -> 792 us  [the longest x1 435 us: body(): lax.psum_scatter(expand_term.astype(jnp.bfloat16), ('dp', 'seq'), scatter...]
  transfers between devices with their start and end apart: 10 -> 10, of which waited for: 8 -> 7; matrix products, arithmetic and copies ran while one was open for 13% -> 18% of each run, Pallas kernels for 0% -> 0%
where the time goes in v1:
time: 1850 us; the launch traced here: 1840 us
  waiting for transfers between devices  1210 us (65%)
  matrix products  416 us (22%)
  blocking collectives  82 us (4%)
  other arithmetic  73.7 us (4%)
  local copies, waits for them, and re-layouts  46.9 us (3%)
    reduce_scatter x1, waiting for transfers between devices, body(): lax.psum_scatter(expand_term.astype(jnp.bfloat16), ('dp', 'seq'), scatter...  435 us
    reduce_scatter x1, waiting for transfers between devices, body(): lax.psum_scatter(shrink_term.astype(jnp.bfloat16), ('dp', 'seq'), scatter...  250 us
    all_gather x1, waiting for transfers between devices, body(): lax.all_gather(expand_weight, ('dp', 'seq'), axis=0, tiled=True)  237 us
    dot_general x8, matrix products, contract(): lax.dot_general(left, right, (((left_dim,), (right_dim,)), ((), ())), pre...  155 us
    all_gather x1, waiting for transfers between devices, body(): lax.all_gather(shrink_weight, ('dp', 'seq'), axis=1, tiled=True)  118 us
    reduce_scatter x1, waiting for transfers between devices, body(): lax.psum_scatter(joined_term.astype(jnp.bfloat16), ('dp', 'seq'), scatter...  107 us
    unnamed x2, blocking collectives  82 us
    dot_general x1, matrix products, body(): jnp.einsum('rqhgd,rkhd->rhgqk', grad_out_low, value_piece, preferred_elem...  48.5 us
  transfers between devices with their start and end apart: 10, of which 7 were waited for; matrix products, arithmetic and copies ran while one was open for 18% of the time, Pallas kernels for 0%

profile of v1, /device:TPU:0, one launch (start us, length us, event | category | flops | bytes accessed | tf_op | source)
XLA Modules:
  0.0 1843.6 jit_solution(10042636667090192097)
XLA Ops:
  8.8 42.5 %all-reduce = bf16[4224]{0:T(1024)(128)(2,1)S(1)} all-reduce(bf16[4224]{0:T(1024)(128)(2,1)S(1)} %dynamic-update-slice), channel_id=1, replica_groups=mesh['dp'=8,'seq'=4] {'dp','seq'}, use_global_device_ids=true, to_apply=%add | all-reduce | flops 4224 | bytes 16896
  54.5 35.3 %all-gather.6.cloned.1.call-done = bf16[2048,1920]{1,0:T(8,128)(2,1)} async-done(((bf16[64,1920]{1,0:T(8,128)(2,1)}), bf16[2048,1920]{1,0:T(8,128)(2,1)}) %all-gather.6.cloned.1.call-update) | async-done | bytes 7864336 | tf_op jit(solution)/shard_map/all_gather | solution.py:107
  89.7 7.7 fusion.49
  120.1 21.0 %all-gather.8.cloned.1.call-done = bf16[1,2048,640]{2,1,0:T(8,128)(2,1)} async-done(((bf16[1,512,640]{2,1,0:T(8,128)(2,1)}), bf16[1,2048,640]{2,1,0:T(8,128)(2,1)}) %all-gather.8.cloned.1.call-update) | async-done | bytes 2621456 | tf_op jit(solution)/shard_map/all_gather | solution.py:142
  146.9 31.5 %fusion.5 = (f32[5,4,512]{2,1,0:T(4,128)S(1)}, f32[5,2048,512,4]{2,1,3,0:T(8,128)}) fusion(pred[512,2048]{0,1:T(8,128)(4,1)} %fusion.26, bf16[2048,5,64,1]{0,2,3,1:T(8,128)(2,1)} %bitcast.203, bf16[512,5,4,32]{0,3,2,1:T(8,128)(2,1)} %bitcast.207, bf16[512,5,4,32]{0,3,2,1:T(8,128)(2,1)} %bitcast.205), kind=kOutput, calls=%fused_computation.10 | convolution fusion | flops 2749880320 | bytes 87597056 | tf_op jit(solution)/shard_map/rqhgd,rkhd->rhgqk/dot_general | solution.py:146
  178.5 27.6 %fusion.2 = f32[5,4,512]{2,1,0:T(4,128)S(1)} fusion(f32[5,2048,512,4]{2,1,3,0:T(8,128)} %get-tuple-element.52, f32[5,4,512]{2,1,0:T(4,128)S(1)} %broadcast_maximum_fusion, pred[512,2048]{0,1:T(8,128)(4,1)S(1)} %copy-done.8), kind=kLoop, calls=%fused_computation.6 | loop fusion | flops 104847360 | bytes 85016576 | tf_op jit(solution)/shard_map/reduce_sum | solution.py:152
  206.1 34.3 %fusion.69 = (bf16[1,512,5,4,64]{1,4,3,2,0:T(8,128)(2,1)}, f32[1,512,5,4,64]{1,4,3,2,0:T(8,128)}) fusion(f32[512,5,4]{0,2,1:T(4,128)S(1)} %bitcast.217, bf16[2048,5,64,1]{0,2,3,1:T(8,128)(2,1)} %bitcast.211, f32[5,2048,512,4]{2,1,3,0:T(8,128)} %get-tuple-element.52, f32[5,4,512]{2,1,0:T(4,128)S(1)} %broadcast_maximum_fusion, ...), kind=kOutput, calls=%fused_computation.139 | convolution fusion | flops 2790522880 | bytes 90259456 | tf_op jit(solution)/shard_map/rhgqk,rkhd->rqhgd/dot_general | solution.py:153
  240.4 7.9 multiply_reduce_fusion.2
  249.5 237.0 %all-gather.12.cloned.1.call-done = bf16[2048,12288]{1,0:T(8,128)(2,1)} async-done(((bf16[64,12288]{1,0:T(8,128)(2,1)}), bf16[2048,12288]{1,0:T(8,128)(2,1)}) %all-gather.12.cloned.1.call-update) | async-done | bytes 50331664 | tf_op jit(solution)/shard_map/all_gather | solution.py:168
  486.5 37.4 %fusion.64 = f32[512,12288]{1,0:T(8,128)} fusion(bf16[2048,12288]{1,0:T(8,128)(2,1)} %all-gather.12.cloned.1.call-done, f32[512,2048]{1,0:T(8,128)} %get-tuple-element.56, f32[2048]{0:T(1024)S(1)} %get-tuple-element.38, f32[512]{0:T(512)S(1)} %get-tuple-element.47), kind=kOutput, calls=%fused_computation.134 | convolution fusion | flops 25772949504 | bytes 79702016 | tf_op jit(solution)/shard_map/dot_general | solution.py:171
  523.9 118.2 %all-gather.14.cloned.1.call-done = bf16[6144,2048]{0,1:T(8,128)(2,1)} async-done(((bf16[6144,64]{0,1:T(8,128)(2,1)}), bf16[6144,2048]{0,1:T(8,128)(2,1)}) %all-gather.14.cloned.1.call-update) | async-done | bytes 25165840 | tf_op jit(solution)/shard_map/all_gather | solution.py:169
  642.1 31.8 %multiply_convert_fusion.1 = (bf16[512,6144]{1,0:T(8,128)(2,1)}, bf16[512,6144]{1,0:T(8,128)(2,1)}, bf16[512,6144]{1,0:T(8,128)(2,1)}) fusion(f32[512,12288]{1,0:T(8,128)} %fusion.64, bf16[6144,2048]{0,1:T(8,128)(2,1)} %all-gather.14.cloned.1.call-done, bf16[1,512,2048]{2,1,0:T(8,128)(2,1)S(1)} %copy-done.12), kind=kOutput, calls=%fused_computation.21 | convolution fusion | flops 12935233536 | bytes 71303168 | tf_op jit(solution)/shard_map/dot_general | solution.py:71
  673.9 36.6 %multiply_reduce_fusion = (f32[2048]{0:T(1024)}, f32[512]{0:T(512)S(1)}, f32[512,2048]{1,0:T(8,128)}) fusion(f32[512,2048]{1,0:T(8,128)} %get-tuple-element.56, f32[512]{0:T(512)S(1)} %get-tuple-element.47, f32[2048]{0:T(1024)S(1)} %get-tuple-element.38, bf16[2048,12288]{1,0:T(8,128)(2,1)} %all-gather.12.cloned.1.call-done, ...), kind=kOutput, calls=%fused_computation.43 | convolution fusion | flops 25801259008 | bytes 71323648 | tf_op jit(solution)/shard_map/dot_general | solution.py:71
  710.5 4.8 subtract_add_fusion
  717.3 3.9 convolution_convert_fusion.4
  727.7 37.4 %fusion.33 = bf16[5,64,2048]{2,1,0:T(8,128)(2,1)S(1)} fusion(bf16[512,5,4,64]{0,3,2,1:T(8,128)(2,1)} %bitcast.213, f32[5,2048,512,4]{2,1,3,0:T(8,128)} %get-tuple-element.52, f32[5,4,512]{2,1,0:T(4,128)S(1)} %copy-done.23, pred[512,2048]{0,1:T(8,128)(4,1)} %fusion.26), kind=kOutput, calls=%fused_computation.57 | convolution fusion | flops 2789867520 | bytes 87597056 | tf_op jit(solution)/shard_map/rhgqk,rqhgd->rkhd/dot_general | solution.py:229
  765.2 48.5 %fusion.8 = bf16[5,4,512,2048]{2,3,1,0:T(8,128)(2,1)} fusion(f32[5,2048,512,4]{2,1,3,0:T(8,128)} %get-tuple-element.52, f32[5,4,512]{2,1,0:T(4,128)S(1)} %bitcast.218, f32[5,4,512]{2,1,0:T(4,128)S(1)} %copy-done.23, pred[512,2048]{0,1:T(8,128)(4,1)S(1)} %copy-done.9, bf16[2048,5,64,1]{0,2,3,1:T(8,128)(2,1)} %bitcast.212, bf16[512,5,4,64]{0,3,2,1:T(8,128)(2,1)} %bitcast.214), kind=kOutput, calls=%fused_computation.13 | convolution fusion | flops 2831155200 | bytes 129581056 | tf_op jit(solution)/shard_map/rqhgd,rkhd->rhgqk/dot_general | solution.py:217
  813.7 18.1 fusion.32
  833.5 8.0 convolution_convert_fusion.2
  847.2 17.4 convolution_multiply_fusion
  874.5 6.8 multiply_reduce_fusion.3
  887.6 3.8 concatenate.98
  891.4 8.4 convolution_convert_fusion.3
  900.3 21.1 %convolution_convert_fusion.1 = bf16[6144,2048]{0,1:T(8,128)(2,1)} fusion(bf16[512,6144]{1,0:T(8,128)(2,1)} %get-tuple-element.13, bf16[1,512,2048]{2,1,0:T(8,128)(2,1)} %param.15), kind=kOutput, calls=%fused_computation.18 | convolution fusion | flops 12897484800 | bytes 33554432 | tf_op jit(solution)/shard_map/dot_general | solution.py:71
  922.1 34.6 %convolution_convert_fusion = bf16[2048,12288]{1,0:T(8,128)(2,1)} fusion(bf16[512,6144]{1,0:T(8,128)(2,1)} %get-tuple-element.12, bf16[512,6144]{1,0:T(8,128)(2,1)} %get-tuple-element.11, f32[512,2048]{1,0:T(8,128)} %get-tuple-element.56, f32[2048]{0:T(1024)S(1)} %copy-done.25, f32[512]{0:T(512)S(1)} %copy-done.31), kind=kOutput, calls=%fused_computation.9 | convolution fusion | flops 25823281152 | bytes 67119104 | tf_op jit(solution)/shard_map/dot_general | solution.py:71
  956.9 21.0 %fusion.31 = bf16[1,512,2048]{2,1,0:T(8,128)(2,1)} fusion(f32[512,2048]{1,0:T(8,128)} %get-tuple-element.56, bf16[512,6144]{1,0:T(8,128)(2,1)} %get-tuple-element.13, bf16[6144,2048]{0,1:T(8,128)(2,1)} %all-gather.14.cloned.1.call-done), kind=kOutput, calls=%fused_computation.55 | convolution fusion | flops 12886999040 | bytes 37748736 | tf_op jit(solution)/shard_map/dot_general | solution.py:176
  978.2 10.7 fusion.25
  989.0 39.4 %all-reduce.1 = f32[4224]{0:T(1024)S(1)} all-reduce(f32[4224]{0:T(1024)S(1)} %concatenate.99), channel_id=7, replica_groups=mesh['dp'=8,'seq'=4] {'dp','seq'}, use_global_device_ids=true, to_apply=%region_23.24.clone | all-reduce | flops 4224 | bytes 33792
  1029.0 6.3 fusion.36
  1037.0 106.5 %reduce-scatter.8.cloned.1.call-done = bf16[64,1920]{1,0:T(8,128)(2,1)} async-done(((bf16[2048,1920]{1,0:T(8,128)(2,1)}), bf16[64,1920]{1,0:T(8,128)(2,1)}) %reduce-scatter.8.cloned.1.call-update) | async-done | bytes 245776 | tf_op jit(solution)/shard_map/reduce_scatter | solution.py:270
  1145.3 250.5 %reduce-scatter.14.cloned.1.call-done = bf16[6144,64]{0,1:T(8,128)(2,1)} async-done(((bf16[6144,2048]{0,1:T(8,128)(2,1)}), bf16[6144,64]{0,1:T(8,128)(2,1)}) %reduce-scatter.14.cloned.1.call-update) | async-done | bytes 786448 | tf_op jit(solution)/shard_map/reduce_scatter | solution.py:195
  1398.1 435.1 %reduce-scatter.12.cloned.1.call-done = bf16[64,12288]{1,0:T(8,128)(2,1)} async-done(((bf16[2048,12288]{1,0:T(8,128)(2,1)}), bf16[64,12288]{1,0:T(8,128)(2,1)}) %reduce-scatter.12.cloned.1.call-update) | async-done | bytes 1572880 | tf_op jit(solution)/shard_map/reduce_scatter | solution.py:194
  (182 shorter events, 75.6 us)
Async XLA Ops:
  7.2 82.5 %all-gather.6.cloned.1.call-start = ((), (), s32[]{:S(2)}) async-start(), calls=%async_computation.5 | async-start | bytes 8110080 | tf_op jit(solution)/shard_map/all_gather | solution.py:107
  7.9 133.2 %all-gather.8.cloned.1.call-start = ((), (), s32[]{:S(2)}) async-start(), calls=%async_computation.6 | async-start | bytes 3276800 | tf_op jit(solution)/shard_map/all_gather | solution.py:142
  51.5 49.2 %copy-start.28 = (f32[64]{0:T(128)}, f32[64]{0:T(128)S(1)}, u32[]{:S(2)}) copy-start(f32[64]{0:T(128)S(1)} %get-tuple-element.41) | copy-start | bytes 772
  51.5 65.9 %copy-start.37 = (f32[64]{0:T(128)}, f32[64]{0:T(128)S(1)}, u32[]{:S(2)}) copy-start(f32[64]{0:T(128)S(1)} %get-tuple-element.40) | copy-start | bytes 772
  54.1 43.3 %copy-start.35 = (f32[512]{0:T(512)}, f32[512]{0:T(512)S(1)}, u32[]{:S(2)}) copy-start(f32[512]{0:T(512)S(1)} %get-tuple-element.45) | copy-start | bytes 6148
  54.1 43.3 %copy-start.26 = (f32[2048]{0:T(1024)}, f32[2048]{0:T(1024)S(1)}, u32[]{:S(2)}) copy-start(f32[2048]{0:T(1024)S(1)} %get-tuple-element.39) | copy-start | bytes 24580
  54.1 656.4 %copy-start.24 = (f32[2048]{0:T(1024)}, f32[2048]{0:T(1024)S(1)}, u32[]{:S(2)}) copy-start(f32[2048]{0:T(1024)S(1)} %get-tuple-element.38) | copy-start | bytes 24580
  54.4 64.1 %copy-start.13 = (f32[512,32]{0,1:T(8,128)}, f32[512,32]{0,1:T(8,128)S(1)}, u32[]{:S(2)}) copy-start(f32[512,32]{0,1:T(8,128)S(1)} %get-tuple-element.42) | copy-start | bytes 196612
  54.4 64.1 %copy-start.15 = (f32[512,32]{0,1:T(8,128)}, f32[512,32]{0,1:T(8,128)S(1)}, u32[]{:S(2)}) copy-start(f32[512,32]{0,1:T(8,128)S(1)} %get-tuple-element.43) | copy-start | bytes 196612
  102.7 137.7 %all-gather.10.cloned.1.call-start = ((), (), s32[]{:S(2)}) async-start(), calls=%async_computation.7 | async-start | bytes 5406720 | tf_op jit(solution)/shard_map/all_gather | solution.py:108
  103.4 383.0 %all-gather.12.cloned.1.call-start = ((), (), s32[]{:S(2)}) async-start(), calls=%async_computation.8 | async-start | bytes 51904512 | tf_op jit(solution)/shard_map/all_gather | solution.py:168
  104.0 538.1 %all-gather.14.cloned.1.call-start = ((), (), s32[]{:S(2)}) async-start(), calls=%async_computation.9 | async-start | bytes 25952256 | tf_op jit(solution)/shard_map/all_gather | solution.py:169
  104.6 776.7 %reduce-scatter.6.cloned.1.call-start = ((), (), s32[]{:S(2)}) async-start(), calls=%async_computation.10 | async-start | bytes 3276800 | tf_op jit(solution)/shard_map/reduce_scatter | solution.py:243
  146.9 31.6 %copy-start.8 = (pred[512,2048]{0,1:T(8,128)(4,1)S(1)}, pred[512,2048]{0,1:T(8,128)(4,1)}, u32[]{:S(2)}) copy-start(pred[512,2048]{0,1:T(8,128)(4,1)} %fusion.26) | copy-start | bytes 3145732
  206.1 34.3 %copy-start.6 = (bf16[1,512,2048]{2,1,0:T(8,128)(2,1)S(1)}, bf16[1,512,2048]{2,1,0:T(8,128)(2,1)}, u32[]{:S(2)}) copy-start(bf16[1,512,2048]{2,1,0:T(8,128)(2,1)} %param.8) | copy-start | bytes 6291460
  248.9 461.6 %copy-start.30 = (f32[512]{0:T(512)}, f32[512]{0:T(512)S(1)}, u32[]{:S(2)}) copy-start(f32[512]{0:T(512)S(1)} %get-tuple-element.47) | copy-start | bytes 6148
  486.5 155.6 %copy-start.12 = (bf16[1,512,2048]{2,1,0:T(8,128)(2,1)S(1)}, bf16[1,512,2048]{2,1,0:T(8,128)(2,1)}, u32[]{:S(2)}) copy-start(bf16[1,512,2048]{2,1,0:T(8,128)(2,1)} %param.15) | copy-start | bytes 6291460
  673.9 36.6 %copy-start.32 = (f32[512]{0:T(512)S(1)}, f32[512]{0:T(512)}, u32[]{:S(2)}) copy-start(f32[512]{0:T(512)} %get-tuple-element.46) | copy-start | bytes 6148
  727.7 37.4 %copy-start.9 = (pred[512,2048]{0,1:T(8,128)(4,1)S(1)}, pred[512,2048]{0,1:T(8,128)(4,1)}, u32[]{:S(2)}) copy-start(pred[512,2048]{0,1:T(8,128)(4,1)} %fusion.26) | copy-start | bytes 3145732
  765.1 48.5 %copy-start.10 = (bf16[1,512,20,32]{1,3,2,0:T(8,128)(2,1)S(1)}, bf16[1,512,20,32]{1,3,2,0:T(8,128)(2,1)}, u32[]{:S(2)}) copy-start(bf16[1,512,20,32]{1,3,2,0:T(8,128)(2,1)} %get-tuple-element.18) | copy-start | bytes 1966084
  765.2 48.5 %copy-start.11 = (bf16[1,512,20,32]{1,3,2,0:T(8,128)(2,1)S(1)}, bf16[1,512,20,32]{1,3,2,0:T(8,128)(2,1)}, u32[]{:S(2)}) copy-start(bf16[1,512,20,32]{1,3,2,0:T(8,128)(2,1)} %get-tuple-element.19) | copy-start | bytes 1966084
  833.5 201.8 %reduce-scatter.10.cloned.1.call-start = ((), (), s32[]{:S(2)}) async-start(), calls=%async_computation.12 | async-start | bytes 5406720 | tf_op jit(solution)/shard_map/reduce_scatter | solution.py:271
  841.5 302.0 %reduce-scatter.8.cloned.1.call-start = ((), (), s32[]{:S(2)}) async-start(), calls=%async_computation.11 | async-start | bytes 8110080 | tf_op jit(solution)/shard_map/reduce_scatter | solution.py:270
  847.2 17.4 copy-start.14
  847.2 17.4 copy-start.16
  874.5 8.9 copy-start.4
  883.6 7.9 copy-start.7
  883.6 7.9 copy-start.27
  899.9 495.9 %reduce-scatter.14.cloned.1.call-start = ((), (), s32[]{:S(2)}) async-start(), calls=%async_computation.14 | async-start | bytes 25952256 | tf_op jit(solution)/shard_map/reduce_scatter | solution.py:195
  921.4 911.9 %reduce-scatter.12.cloned.1.call-start = ((), (), s32[]{:S(2)}) async-start(), calls=%async_computation.13 | async-start | bytes 51904512 | tf_op jit(solution)/shard_map/reduce_scatter | solution.py:194
  978.2 10.7 copy-start.33
  978.2 50.8 %copy-start.34 = (f32[512]{0:T(512)S(1)}, f32[512]{0:T(512)}, u32[]{:S(2)}) copy-start(f32[512]{0:T(512)} %get-tuple-element.44) | copy-start | bytes 6148
  (19 other events, 50.7 us)
Sparse Core Ops, SparseCore 0:
  10.9 78.7 all-gather.5
  102.8 38.2 all-gather.7
  143.9 65.3 all-gather.9
  212.1 274.3 all-gather.11
  489.2 152.8 all-gather.13
  833.6 37.7 reduce-scatter.5
  873.7 143.6 reduce-scatter.9
  1023.0 120.4 reduce-scatter.7
  1151.1 244.6 reduce-scatter.13
  1402.0 431.2 reduce-scatter.11

commit v2 on v0

v2 whole, which is shorter than its diff:
```python
import functools

import jax
import jax.numpy as jnp
from jax import lax
from jax.experimental import pallas as pl
from jax.experimental.pallas import tpu as pltpu
from jax.sharding import PartitionSpec as P

D = 2048
HEADS = 20
KV_HEADS = 5
HEAD_DIM = 64
FF = 6144
ROW_LEN = 2048
GAINS = 4224
PAIR = 2 * HEAD_DIM
Q_WIDTH = HEADS * HEAD_DIM
KV_WIDTH = KV_HEADS * HEAD_DIM
QKV = Q_WIDTH + 2 * KV_WIDTH
CORES = 2

epsilon = 1e-05
f32 = jnp.float32
bf16 = jnp.bfloat16
AXES = ("dp", "seq")
NN = (((1,), (0,)), ((), ()))
NT = (((1,), (1,)), ((), ()))
TN = (((0,), (0,)), ((), ()))


def dot(left, right, dims):
    return lax.dot_general(left, right, dims, preferred_element_type=f32)


def rms_scale(values):
    return lax.rsqrt(jnp.mean(values * values, axis=-1, keepdims=True) + epsilon)


def norm_back(upstream, values, scaling, gain_vector):
    weighted = upstream * gain_vector
    average = jnp.mean(weighted * values, axis=-1, keepdims=True)
    return scaling * weighted - values * (scaling * scaling * scaling) * average


def lanes(shape):
    return lax.broadcasted_iota(jnp.int32, shape, len(shape) - 1)


def swap_halves(values):
    half = HEAD_DIM // 2
    first = lanes(values.shape) % HEAD_DIM < half
    return jnp.where(first, pltpu.roll(values, PAIR - half, axis=1), pltpu.roll(values, half, axis=1))


def head_means(values):
    low = lanes(values.shape) < HEAD_DIM
    left = jnp.sum(jnp.where(low, values, 0.0), axis=-1, keepdims=True)
    right = jnp.sum(jnp.where(low, 0.0, values), axis=-1, keepdims=True)
    return jnp.where(low, left, right) * (1.0 / HEAD_DIM)


def rope_kernel(query_pairs, projected, gains, tables, out):
    step = pl.program_id(0)
    is_query = step < query_pairs
    values = projected[...]
    plain = (lanes(values.shape) >= HEAD_DIM) & jnp.logical_not(is_query)
    gain = jnp.where(is_query, gains[0:1], gains[1:2])
    normed = values * lax.rsqrt(head_means(values * values) + epsilon) * gain
    turned = normed * tables[0] + swap_halves(normed) * tables[1]
    turned = turned * jnp.where(is_query, HEAD_DIM**-0.5, 1.0)
    out[...] = jnp.where(plain, values, turned).astype(bf16)


def rope(projected, gains, tables):
    tokens, width = projected.shape
    return pl.pallas_call(
        functools.partial(rope_kernel, Q_WIDTH // PAIR),
        grid=(width // PAIR,),
        in_specs=[
            pl.BlockSpec((tokens, PAIR), lambda i: (0, i)),
            pl.BlockSpec((2, PAIR), lambda i: (0, 0)),
            pl.BlockSpec((2, tokens, PAIR), lambda i: (0, 0, 0)),
        ],
        out_specs=pl.BlockSpec((tokens, PAIR), lambda i: (0, i)),
        out_shape=jax.ShapeDtypeStruct((tokens, width), bf16),
        cost_estimate=pl.CostEstimate(flops=40 * tokens * width, bytes_accessed=6 * tokens * width, transcendentals=0),
        name="rope",
    )(projected, gains, tables)


def rope_back_kernel(query_pairs, dq, dkv, projected, gains, tables, out, gain_sums):
    step = pl.program_id(0)
    is_query = step < query_pairs
    values = projected[...]
    upstream = jnp.where(is_query, dq[...] * HEAD_DIM**-0.5, dkv[...])
    plain = (lanes(values.shape) >= HEAD_DIM) & jnp.logical_not(is_query)
    gain = jnp.where(is_query, gains[0:1], gains[1:2])
    turned = upstream * tables[0] + swap_halves(upstream * tables[1])
    scaling = lax.rsqrt(head_means(values * values) + epsilon)
    weighted = turned * gain
    back = scaling * weighted - values * (scaling * scaling * scaling) * head_means(weighted * values)
    out[...] = jnp.where(plain, upstream, back).astype(bf16)
    sums = jnp.sum(jnp.where(plain, 0.0, turned * values * scaling), axis=0, keepdims=True)

    @pl.when(step == 0)
    def _():
        gain_sums[...] = jnp.zeros_like(gain_sums)

    row = lax.broadcasted_iota(jnp.int32, gain_sums.shape, 0)
    gain_sums[...] += jnp.where(row == jnp.where(is_query, 0, 1), sums, 0.0)


def rope_back(dq, dkv, projected, gains, tables):
    tokens, width = projected.shape
    query_pairs = Q_WIDTH // PAIR
    return pl.pallas_call(
        functools.partial(rope_back_kernel, query_pairs),
        grid=(width // PAIR,),
        in_specs=[
            pl.BlockSpec((tokens, PAIR), lambda i: (0, jnp.minimum(i, query_pairs - 1))),
            pl.BlockSpec((tokens, PAIR), lambda i: (0, jnp.maximum(i - query_pairs, 0))),
            pl.BlockSpec((tokens, PAIR), lambda i: (0, i)),
            pl.BlockSpec((2, PAIR), lambda i: (0, 0)),
            pl.BlockSpec((2, tokens, PAIR), lambda i: (0, 0, 0)),
        ],
        out_specs=[
            pl.BlockSpec((tokens, PAIR), lambda i: (0, i)),
            pl.BlockSpec((8, PAIR), lambda i: (0, 0)),
        ],
        out_shape=[
            jax.ShapeDtypeStruct((tokens, width), bf16),
            jax.ShapeDtypeStruct((8, PAIR), f32),
        ],
        cost_estimate=pl.CostEstimate(flops=60 * tokens * width, bytes_accessed=10 * tokens * width, transcendentals=0),
        name="rope_back",
    )(dq, dkv, projected, gains, tables)


def three_parts(values):
    first = values.astype(bf16).astype(f32)
    second = (values - first).astype(bf16).astype(f32)
    return first, second, values - first - second


def spread_kv(kv, key_marks, keys, vals):
    both = kv[...]
    lane = lanes(both.shape)
    keys[...] = jnp.where(lane < HEAD_DIM, both, key_marks[...])
    vals[...] = jnp.where(lane < HEAD_DIM, jnp.where(lane < 3, 1.0, 0.0).astype(bf16), both)


MARK = 8


def attend_kernel(tq, tk, offset, q, kv, key_marks, query_marks, out, q_marked, keys, vals, rows):
    local_len = q.shape[0]
    group = q.shape[1] // HEAD_DIM
    spread_kv(kv, key_marks, keys, vals)
    lane1 = lanes((tq, PAIR))
    for tile in range(local_len // tq):
        part = slice(tile * tq, (tile + 1) * tq)
        for head in range(group):
            wide = q[part, (head // 2) * PAIR : (head // 2 + 1) * PAIR].astype(f32)
            if head % 2:
                wide = pltpu.roll(wide, HEAD_DIM, axis=1)
            marked = jnp.where(lane1 < HEAD_DIM, wide, query_marks[part].astype(f32))
            rows[head * tq : (head + 1) * tq] = marked.astype(bf16)
        first = offset[0] + tile * tq

        def block(index, total, masked):
            span = pl.ds(pl.multiple_of(index * tk, tk), tk)
            expo = jnp.exp(dot(rows[...], keys[span], NT))
            if masked:
                query_pos = first + lax.broadcasted_iota(jnp.int32, (tq, tk), 0)
                key_pos = index * tk + lax.broadcasted_iota(jnp.int32, (tq, tk), 1)
                expo = jnp.where((key_pos <= query_pos)[None], expo.reshape(group, tq, tk), 0.0)
                expo = expo.reshape(group * tq, tk)
            return total + dot(expo.astype(bf16), vals[span], NN)

        full = first // tk
        end = (first + tq + tk - 1) // tk
        total = jnp.zeros((group * tq, PAIR), f32)
        total = lax.fori_loop(0, full, lambda i, t: block(i, t, False), total)
        total = lax.fori_loop(full, end, lambda i, t: block(i, t, True), total)
        denominator = total[:, 0:1]
        mixed = total / denominator
        one, two, three = three_parts(-jnp.log(denominator))
        lane = lanes(total.shape) - HEAD_DIM - MARK
        kept = rows[...].astype(f32)
        kept = jnp.where(lane == 0, one, jnp.where(lane == 1, two, jnp.where(lane == 2, three, kept)))
        kept = kept.astype(bf16)
        for head in range(group):
            q_marked[head, part] = kept[head * tq : (head + 1) * tq]
        for head in range(0, group, 2):
            even = pltpu.roll(mixed[head * tq : (head + 1) * tq], HEAD_DIM, axis=1)
            odd = mixed[(head + 1) * tq : (head + 2) * tq]
            out[part, (head // 2) * PAIR : (head // 2 + 1) * PAIR] = jnp.where(lane1 < HEAD_DIM, even, odd)


def attention_cost(tokens, products):
    pairs = HEADS * tokens * ROW_LEN
    return pl.CostEstimate(flops=products * 2 * 4 * HEAD_DIM * pairs, bytes_accessed=1 << 24, transcendentals=pairs)


def attend(offset, q, kv, key_marks, query_marks):
    tokens = q.shape[0]
    keys = kv.shape[0]
    group = HEADS // KV_HEADS
    width = group * HEAD_DIM
    tq, tk = tokens, min(512, keys)
    spec = pltpu.PrefetchScalarGridSpec(
        num_scalar_prefetch=1,
        grid=(KV_HEADS,),
        in_specs=[
            pl.BlockSpec((tokens, width), lambda g, _: (0, g)),
            pl.BlockSpec((keys, PAIR), lambda g, _: (0, g)),
            pl.BlockSpec((keys, PAIR), lambda g, _: (0, 0)),
            pl.BlockSpec((tokens, PAIR), lambda g, _: (0, 0)),
        ],
        out_specs=[
            pl.BlockSpec((tokens, width), lambda g, _: (0, g)),
            pl.BlockSpec((group, tokens, PAIR), lambda g, _: (g, 0, 0)),
        ],
        scratch_shapes=[
            pltpu.VMEM((keys, PAIR), bf16),
            pltpu.VMEM((keys, PAIR), bf16),
            pltpu.VMEM((group * tq, PAIR), bf16),
        ],
    )
    return pl.pallas_call(
        functools.partial(attend_kernel, tq, tk),
        grid_spec=spec,
        out_shape=[
            jax.ShapeDtypeStruct((tokens, Q_WIDTH), f32),
            jax.ShapeDtypeStruct((HEADS, tokens, PAIR), bf16),
        ],
        compiler_params=pltpu.CompilerParams(vmem_limit_bytes=56 << 20),
        cost_estimate=attention_cost(tokens, 2),
        name="attend",
    )(offset, q, kv, key_marks, query_marks)


def attend_back_kernel(
    tq, tk, offset, q_marked, d_out, out, kv, key_marks, dq, dkv, keys, vals, d_rows, rows, dk_sum, dv_sum
):
    local_len = d_out.shape[0]
    group = d_out.shape[1] // HEAD_DIM
    spread_kv(kv, key_marks, keys, vals)
    dk_sum[...] = jnp.zeros_like(dk_sum)
    dv_sum[...] = jnp.zeros_like(dv_sum)
    lane1 = lanes((tq, PAIR))
    for tile in range(local_len // tq):
        part = slice(tile * tq, (tile + 1) * tq)
        for head in range(group):
            pair = slice((head // 2) * PAIR, (head // 2 + 1) * PAIR)
            wide = d_out[part, pair].astype(f32)
            mine = (lane1 < HEAD_DIM) if head % 2 == 0 else (lane1 >= HEAD_DIM)
            delta = jnp.sum(jnp.where(mine, wide * out[part, pair], 0.0), axis=1, keepdims=True)
            one, two, three = three_parts(-delta)
            if head % 2 == 0:
                wide = pltpu.roll(wide, HEAD_DIM, axis=1)
            marks = jnp.where(lane1 == 0, one, jnp.where(lane1 == 1, two, jnp.where(lane1 == 2, three, 0.0)))
            d_rows[head * tq : (head + 1) * tq] = jnp.where(lane1 < HEAD_DIM, marks, wide).astype(bf16)
            rows[head * tq : (head + 1) * tq] = q_marked[head, part]
        first = offset[0] + tile * tq

        def block(index, total, masked):
            span = pl.ds(pl.multiple_of(index * tk, tk), tk)
            prob = jnp.exp(dot(keys[span], rows[...], NT))
            if masked:
                key_pos = index * tk + lax.broadcasted_iota(jnp.int32, (tk, tq), 0)
                query_pos = first + lax.broadcasted_iota(jnp.int32, (tk, tq), 1)
                prob = jnp.where(jnp.concatenate([key_pos <= query_pos] * group, axis=1), prob, 0.0)
            d_scores = (prob * dot(vals[span], d_rows[...], NT)).astype(bf16)
            dv_sum[span] += dot(prob.astype(bf16), d_rows[...], NN)
            dk_sum[span] += dot(d_scores, rows[...], NN)
            return total + dot(d_scores, keys[span], TN)

        full = first // tk
        end = (first + tq + tk - 1) // tk
        total = jnp.zeros((group * tq, PAIR), f32)
        total = lax.fori_loop(0, full, lambda i, t: block(i, t, False), total)
        total = lax.fori_loop(full, end, lambda i, t: block(i, t, True), total)
        for head in range(0, group, 2):
            even = total[head * tq : (head + 1) * tq]
            odd = pltpu.roll(total[(head + 1) * tq : (head + 2) * tq], HEAD_DIM, axis=1)
            dq[part, (head // 2) * PAIR : (head // 2 + 1) * PAIR] = jnp.where(lane1 < HEAD_DIM, even, odd)
    dkv[...] = jnp.where(lanes(dk_sum.shape) < HEAD_DIM, dk_sum[...], dv_sum[...]).astype(bf16)


def attend_back(offset, q_marked, d_out, out, kv, key_marks):
    tokens = d_out.shape[0]
    keys = kv.shape[0]
    group = HEADS // KV_HEADS
    width = group * HEAD_DIM
    tq, tk = tokens, min(512, keys)
    spec = pltpu.PrefetchScalarGridSpec(
        num_scalar_prefetch=1,
        grid=(KV_HEADS,),
        in_specs=[
            pl.BlockSpec((group, tokens, PAIR), lambda g, _: (g, 0, 0)),
            pl.BlockSpec((tokens, width), lambda g, _: (0, g)),
            pl.BlockSpec((tokens, width), lambda g, _: (0, g)),
            pl.BlockSpec((keys, PAIR), lambda g, _: (0, g)),
            pl.BlockSpec((keys, PAIR), lambda g, _: (0, 0)),
        ],
        out_specs=[
            pl.BlockSpec((tokens, width), lambda g, _: (0, g)),
            pl.BlockSpec((keys, PAIR), lambda g, _: (0, g)),
        ],
        scratch_shapes=[
            pltpu.VMEM((keys, PAIR), bf16),
            pltpu.VMEM((keys, PAIR), bf16),
            pltpu.VMEM((group * tq, PAIR), bf16),
            pltpu.VMEM((group * tq, PAIR), bf16),
            pltpu.VMEM((keys, PAIR), f32),
            pltpu.VMEM((keys, PAIR), f32),
        ],
    )
    return pl.pallas_call(
        functools.partial(attend_back_kernel, tq, tk),
        grid_spec=spec,
        out_shape=[
            jax.ShapeDtypeStruct((tokens, Q_WIDTH), f32),
            jax.ShapeDtypeStruct(kv.shape, bf16),
        ],
        compiler_params=pltpu.CompilerParams(vmem_limit_bytes=56 << 20),
        cost_estimate=attention_cost(tokens, 4),
        name="attend_back",
    )(offset, q_marked, d_out, out, kv, key_marks)


def feed_kernel(normed, upstream, weights, hidden, both, result, back):
    units = hidden.shape[1]
    values = normed[...]
    gate = dot(values, weights[:, :units], NN)
    up = dot(values, weights[:, units : 2 * units], NN)
    d_hidden = dot(upstream[...], weights[:, 2 * units :], NN)
    sigmoid = 1.0 / (1.0 + jnp.exp(-gate))
    silu = gate * sigmoid
    low = (silu * up).astype(bf16)
    hidden[...] = low
    result[...] = dot(low, weights[:, 2 * units :], NT).astype(bf16)
    d_gate = (d_hidden * up * sigmoid * (1.0 + gate * (1.0 - sigmoid))).astype(bf16)
    d_up = (d_hidden * silu).astype(bf16)
    both[:, :units] = d_gate
    both[:, units:] = d_up
    d_normed = dot(d_gate, weights[:, :units], NT) + dot(d_up, weights[:, units : 2 * units], NT)
    back[...] = d_normed.astype(bf16)


def feed(normed, upstream, weights):
    tokens = normed.shape[0]
    units = weights.shape[1] // 3
    tile = 256
    row = lambda n: pl.BlockSpec((tile, n), lambda i: (i, 0))
    out = lambda n: jax.ShapeDtypeStruct((tokens, n), bf16)
    return pl.pallas_call(
        feed_kernel,
        grid=(tokens // tile,),
        in_specs=[
            row(D),
            row(D),
            pl.BlockSpec(weights.shape, lambda i: (0, 0), pipeline_mode=pl.Buffered(1)),
        ],
        out_specs=[row(units), row(2 * units), row(D), row(D)],
        out_shape=[out(units), out(2 * units), out(D), out(D)],
        compiler_params=pltpu.CompilerParams(vmem_limit_bytes=56 << 20),
        cost_estimate=pl.CostEstimate(
            flops=20 * tokens * D * units,
            bytes_accessed=2 * (3 * D * units + tokens * (4 * D + 3 * units)),
            transcendentals=tokens * units,
        ),
        name="feed",
    )(normed, upstream, weights)


def weight_gradient_kernel(count, *refs):
    normed, upstream, both, hidden = (refs[i * count : (i + 1) * count] for i in range(4))
    out = refs[-1]
    units = hidden[0].shape[1]
    expand = shrink = None
    for j in range(count):
        one = dot(normed[j][...], both[j][...], TN)
        two = dot(upstream[j][...], hidden[j][...], TN)
        expand = one if expand is None else expand + one
        shrink = two if shrink is None else shrink + two
    out[:, : 2 * units] = expand.astype(bf16)
    out[:, 2 * units :] = shrink.astype(bf16)


def weight_gradient(normed, upstream, both, hidden):
    count = len(normed)
    units = hidden[0].shape[1]
    tile = 256
    columns = [pl.BlockSpec((a.shape[0], tile), lambda i: (0, i)) for a in normed]
    whole = lambda xs: [pl.BlockSpec(a.shape, lambda i: (0, 0), pipeline_mode=pl.Buffered(1)) for a in xs]
    tokens = sum(a.shape[0] for a in normed)
    return pl.pallas_call(
        functools.partial(weight_gradient_kernel, count),
        grid=(D // tile,),
        in_specs=columns + columns + whole(both) + whole(hidden),
        out_specs=pl.BlockSpec((tile, 3 * units), lambda i: (i, 0)),
        out_shape=jax.ShapeDtypeStruct((D, 3 * units), bf16),
        compiler_params=pltpu.CompilerParams(vmem_limit_bytes=60 << 20),
        cost_estimate=pl.CostEstimate(
            flops=8 * tokens * D * units, bytes_accessed=2 * tokens * (2 * D + 3 * units), transcendentals=0
        ),
        name="weight_gradient",
    )(*normed, *upstream, *both, *hidden)


class Links:
    def __init__(self, n_dp, n_seq):
        self.n_z = n_dp // CORES
        self.n_seq = n_seq
        self.plane = CORES * n_seq

    def place(self):
        dp = lax.axis_index("dp")
        return dp // CORES, dp % CORES, lax.axis_index("seq")

    def send(self, values, pairs_of):
        pairs = []
        for z in range(self.n_z):
            for c in range(CORES):
                for s in range(self.n_seq):
                    to = pairs_of(z, c, s)
                    if to is not None:
                        tz, tc, ts = to
                        pairs.append((((z * CORES + c) * self.n_seq + s), (tz * CORES + tc) * self.n_seq + ts))
        return lax.ppermute(values, AXES, pairs)

    def core(self, values):
        return self.send(values, lambda z, c, s: (z, 1 - c, s))

    def peer(self, values, k):
        return self.send(values, lambda z, c, s: (z, c, s ^ k))

    def up(self, values, first, last):
        return self.send(values, lambda z, c, s: (z + 1, c, s) if first <= z <= last else None)

    def down(self, values, first, last):
        return self.send(values, lambda z, c, s: (z - 1, c, s) if first <= z <= last else None)

    def seq_gather(self, values):
        if self.n_seq != 4:
            return [[values]] + [[self.peer(values, k)] for k in range(1, self.n_seq)]
        half = values.shape[0] // 2
        one, two = self.peer(values, 1), self.peer(values, 2)
        top = self.peer(one[:half], 2)
        bottom = self.peer(two[half:], 1)
        return [[values], [one], [two], [top, bottom]]

    def seq_scatter(self, parts, add):
        if self.n_seq != 4:
            return add([parts[0]] + [self.peer(parts[k], k) for k in range(1, self.n_seq)])
        half = parts[0].shape[0] // 2
        top = self.peer(parts[3][:half], 1)
        bottom = self.peer(parts[3][half:], 2)
        two = [self.peer(add([parts[2][:half], top]), 2), self.peer(parts[2][half:], 2)]
        one = [self.peer(parts[1][:half], 1), self.peer(add([parts[1][half:], bottom]), 1)]
        return [add([parts[0][:half], two[0], one[0]]), add([parts[0][half:], two[1], one[1]])]

    def line_gather(self, values):
        n = self.n_z
        z, _, _ = self.place()
        rows = values.shape[0]
        ups, downs = [values], [values]
        for k in range(1, n):
            ups.append(self.up(ups[-1], k - 1, n - 2))
            downs.append(self.down(downs[-1], 1, n - k))
        full = lax.dynamic_update_slice_in_dim(jnp.zeros((n * rows, values.shape[1]), values.dtype), values, z * rows, 0)
        for r in range(1, n):
            piece = jnp.where(z + r < n, downs[r], ups[n - r])
            full = lax.dynamic_update_slice_in_dim(full, piece, ((z + r) % n) * rows, 0)
        return full

    def line_scatter(self, full, add):
        n = self.n_z
        z, _, _ = self.place()
        rows = full.shape[0] // n
        take = lambda d: lax.dynamic_slice_in_dim(full, jnp.clip(d, 0, n - 1) * rows, rows, 0)
        above = below = None
        for k in range(1, n):
            one, two = take(z + n - k), take(z - n + k)
            one = one if above is None else add([one, above])
            two = two if below is None else add([two, below])
            above = self.up(one, 0, k - 1)
            below = self.down(two, n - k, n - 1)
        return [take(z)] + ([above, below] if n > 1 else [])


def add_low(parts):
    return functools.reduce(lambda a, b: a + b, [p.astype(f32) for p in parts]).astype(bf16)


def add_wide(parts):
    return functools.reduce(lambda a, b: a + b, [p.astype(f32) for p in parts])


def body(
    n_dp,
    n_seq,
    tokens,
    joined_weight,
    output_weight,
    expand_weight,
    shrink_weight,
    norm_gains,
    doc_lengths,
    cotangent,
):
    links = Links(n_dp, n_seq)
    n_z, plane = links.n_z, links.plane
    z, core, seq = links.place()
    me = core * n_seq + seq
    devices = n_dp * n_seq
    local_len = tokens.shape[1]
    rows = D // devices
    units = FF // plane
    own_gains = GAINS // devices
    offset = seq * local_len

    kv_columns = joined_weight[:, Q_WIDTH:].reshape(rows, 2, KV_HEADS, HEAD_DIM).transpose(0, 2, 1, 3)
    gain_block = jnp.pad(norm_gains, (0, rows * PAIR - own_gains)).reshape(rows, PAIR)
    joined_block = jnp.concatenate(
        [joined_weight[:, :Q_WIDTH], kv_columns.reshape(rows, 2 * KV_WIDTH), gain_block], axis=1
    )
    joined_all = lax.all_gather(joined_block, AXES, axis=0, tiled=True)
    output_all = lax.all_gather(output_weight.T, AXES, axis=0, tiled=True)
    gains = joined_all[:, QKV:].reshape(devices, rows * PAIR)[:, :own_gains].reshape(GAINS).astype(f32)
    joined_all = joined_all[:, :QKV]
    gain_one = gains[:D]
    gain_query = gains[D : D + HEAD_DIM]
    gain_key = gains[D + HEAD_DIM : D + PAIR]
    gain_two = gains[D + PAIR :]
    head_gains = jnp.stack([jnp.tile(gain_query, 2), jnp.tile(gain_key, 2)])

    shrink_rows = shrink_weight.T
    shares = []
    for k in range(plane):
        p = (core ^ (k // n_seq)) * n_seq + (seq ^ (k % n_seq))
        take = lambda a, start: lax.dynamic_slice_in_dim(a, start + p * units, units, 1)
        share = jnp.concatenate([take(expand_weight, 0), take(expand_weight, FF), take(shrink_rows, 0)], axis=1)
        if k:
            share = links.send(share, lambda a, c, s: (a, c ^ (k // n_seq), s ^ (k % n_seq)))
        shares.append((p, share))
    block = jnp.zeros((plane * rows, 3 * units), bf16)
    for p, share in shares:
        block = lax.dynamic_update_slice_in_dim(block, share, p * rows, 0)
    weights = links.line_gather(block)

    half = HEAD_DIM // 2
    frequency = 10000.0 ** (-jnp.arange(half, dtype=f32) / half)
    angles = (offset + jnp.arange(local_len, dtype=jnp.int32)).astype(f32)[:, None] * frequency[None, :]
    cosine, sine = jnp.cos(angles), jnp.sin(angles)
    tables = jnp.stack(
        [jnp.concatenate([cosine] * 4, axis=1), jnp.concatenate([-sine, sine, -sine, sine], axis=1)]
    )
    places = jnp.arange(ROW_LEN, dtype=jnp.int32)
    docs = jnp.zeros((ROW_LEN,), jnp.int32)
    bound = 0
    for index in range(doc_lengths.shape[1] - 1):
        bound = bound + doc_lengths[0, index]
        docs = docs + (places >= bound).astype(jnp.int32)
    mark = jnp.arange(PAIR, dtype=jnp.int32)[None] - HEAD_DIM
    same = (mark >= 0) & (mark < MARK) & (mark == docs[:, None])
    other = (mark >= 0) & (mark < MARK) & (mark != docs[:, None])
    carries = (mark >= MARK) & (mark < MARK + 3)
    key_marks = jnp.where(other, -1024.0, jnp.where(carries, 1.0, 0.0)).astype(bf16)
    query_marks = lax.dynamic_slice_in_dim(same.astype(bf16), offset, local_len, 0)
    offset_array = jnp.reshape(offset, (1,)).astype(jnp.int32)

    flat = tokens.reshape(local_len, D).astype(f32)
    scale_one = rms_scale(flat)
    normed_low = (flat * scale_one * gain_one).astype(bf16)
    projected = dot(normed_low, joined_all, NN)
    turned = rope(projected, head_gains, tables)
    own_kv = turned[:, Q_WIDTH:]
    kv = jnp.zeros((ROW_LEN, 2 * KV_WIDTH), bf16)
    for k, parts in enumerate(links.seq_gather(own_kv)):
        start = (seq ^ k) * local_len
        for part in parts:
            kv = lax.dynamic_update_slice_in_dim(kv, part, start, 0)
            start = start + part.shape[0]
    attended, q_marked = attend(offset_array, turned, kv, key_marks, query_marks)
    attended_low = attended.astype(bf16)
    residual = flat + dot(attended_low, output_all, NT)
    scale_two = rms_scale(residual)
    normed_two = (residual * scale_two * gain_two).astype(bf16)

    def plane_gather(values):
        groups = []
        for parts in links.seq_gather(values):
            parts = parts + [links.core(p) for p in parts]
            groups.append(jnp.concatenate(parts, axis=0))
        return groups

    upstream_low = cotangent.reshape(local_len, D)
    upstream_all = plane_gather(upstream_low)
    normed_all = plane_gather(normed_two)
    hidden_all, both_all, result_parts, back_parts = [], [], [], []
    for values, above in zip(normed_all, upstream_all):
        hidden, both, result, back = feed(values, above, weights)
        hidden_all.append(hidden)
        both_all.append(both)
        result_parts.append(result)
        back_parts.append(back)

    def plane_scatter(parts):
        parts = [add_low([p[:local_len], links.core(p[local_len:])]) for p in parts]
        out = links.seq_scatter(parts, add_low)
        return jnp.concatenate(out, axis=0) if isinstance(out, list) else out

    grad_normed_two = plane_scatter(back_parts).astype(f32)
    share_gradient = weight_gradient(normed_all, upstream_all, both_all, hidden_all)
    feed_result = plane_scatter(result_parts).astype(f32)
    layer_output = (residual + feed_result).astype(bf16)

    mine = add_low(links.line_scatter(share_gradient, add_low))
    expand_gradient = jnp.zeros((rows, 2 * FF), f32)
    shrink_gradient = jnp.zeros((rows, FF), f32)
    for k in range(plane):
        p = (core ^ (k // n_seq)) * n_seq + (seq ^ (k % n_seq))
        piece = lax.dynamic_slice_in_dim(mine, p * rows, rows, 0)
        if k:
            piece = links.send(piece, lambda a, c, s: (a, c ^ (k // n_seq), s ^ (k % n_seq)))
        piece = piece.astype(f32)
        put = lambda a, part, start: lax.dynamic_update_slice_in_dim(a, part, start + p * units, 1)
        expand_gradient = put(expand_gradient, piece[:, :units], 0)
        expand_gradient = put(expand_gradient, piece[:, units : 2 * units], FF)
        shrink_gradient = put(shrink_gradient, piece[:, 2 * units :], 0)
    shrink_gradient = shrink_gradient.T

    upstream = upstream_low.astype(f32)
    gain_two_grad = jnp.sum(grad_normed_two * residual * scale_two, axis=0)
    grad_residual = upstream + norm_back(grad_normed_two, residual, scale_two, gain_two)
    grad_attn_low = grad_residual.astype(bf16)
    output_term = dot(grad_attn_low, attended_low, TN).astype(bf16)
    grad_out_low = dot(grad_attn_low, output_all, NN).astype(bf16)
    grad_query, grad_kv_all = attend_back(offset_array, q_marked, grad_out_low, attended, kv, key_marks)
    kv_parts = [lax.dynamic_slice_in_dim(grad_kv_all, (seq ^ k) * local_len, local_len, 0) for k in range(n_seq)]
    grad_kv = links.seq_scatter(kv_parts, add_wide if n_seq != 4 else add_low)
    grad_kv = jnp.concatenate(grad_kv, axis=0) if isinstance(grad_kv, list) else grad_kv
    grad_projected, head_gain_sums = rope_back(grad_query, grad_kv.astype(f32), projected, head_gains, tables)
    joined_term = dot(normed_low, grad_projected, TN).astype(bf16)
    grad_normed = dot(grad_projected, joined_all, NT)
    gain_one_grad = jnp.sum(grad_normed * flat * scale_one, axis=0)
    token_gradient = grad_residual + norm_back(grad_normed, flat, scale_one, gain_one)
    gain_query_grad = head_gain_sums[0, :HEAD_DIM] + head_gain_sums[0, HEAD_DIM:]
    gain_key_grad = head_gain_sums[1, :HEAD_DIM]
    gain_grads = jnp.concatenate([gain_one_grad, gain_query_grad, gain_key_grad, gain_two_grad])
    gain_block = jnp.pad(gain_grads.reshape(devices, own_gains), ((0, 0), (0, rows * PAIR - own_gains)))
    gain_block = gain_block.reshape(devices * rows, PAIR).astype(bf16)

    def scatter_all(full):
        width = full.shape[1]
        full = full.reshape(n_z, CORES, n_seq, rows, width)
        other = links.core(lax.dynamic_index_in_dim(full, 1 - core, 1, keepdims=False))
        full = add_low([lax.dynamic_index_in_dim(full, core, 1, keepdims=False), other])
        full = full.transpose(1, 0, 2, 3).reshape(n_seq, n_z * rows, width)
        parts = [lax.dynamic_index_in_dim(full, seq ^ k, 0, keepdims=False) for k in range(n_seq)]
        out = links.seq_scatter(parts, add_low)
        out = jnp.concatenate(out, axis=0) if isinstance(out, list) else out
        return add_wide(links.line_scatter(out, add_low))

    output_gradient = scatter_all(output_term).T
    joined_sum = scatter_all(jnp.concatenate([joined_term, gain_block], axis=1))
    kv_sum = joined_sum[:, Q_WIDTH:QKV].reshape(rows, KV_HEADS, 2, HEAD_DIM).transpose(0, 2, 1, 3)
    joined_gradient = jnp.concatenate([joined_sum[:, :Q_WIDTH], kv_sum.reshape(rows, 2 * KV_WIDTH)], axis=1)
    gains_gradient = joined_sum[:, QKV:].reshape(rows * PAIR)[:own_gains]
    return (
        layer_output.reshape(1, local_len, D),
        token_gradient.astype(bf16).reshape(1, local_len, D),
        joined_gradient,
        output_gradient,
        expand_gradient,
        shrink_gradient,
        gains_gradient,
    )


def solution(mesh):
    placed = (
        P("dp", "seq", None),
        P(AXES, None),
        P(None, AXES),
        P(AXES, None),
        P(None, AXES),
        P(AXES),
        P("dp", None),
        P("dp", "seq", None),
    )
    return jax.shard_map(
        functools.partial(body, mesh.shape["dp"], mesh.shape["seq"]),
        mesh=mesh,
        in_specs=placed,
        out_specs=(
            P("dp", "seq", None),
            P("dp", "seq", None),
            P(AXES, None),
            P(None, AXES),
            P(AXES, None),
            P(None, AXES),
            P(AXES),
        ),
        check_vma=False,
    )
```

time: 2560 us -> 1190 us (0.46)
  waiting for transfers between devices: 1920 us -> 455 us
  matrix products: 431 us -> 40.8 us
  Pallas kernels: 0 us -> 228 us
  starting transfers between devices: 1.08 us -> 220 us
  blocking collectives: 82.7 us -> 0 us
  local copies, waits for them, and re-layouts: 43.9 us -> 112 us
  other arithmetic: 64.1 us -> 109 us
    reduce_scatter x5 -> x0, waiting for transfers between devices: 1500 us -> none  [the longest x1 829 us: body(): lax.psum_scatter(expand_term, ('dp', 'seq'), scatter_dimension=0, tiled=T...]
    ppermute x0 -> x100, waiting for transfers between devices: none -> 455 us  [send(): return lax.ppermute(values, AXES, pairs)]
    all_gather x5 -> x2, waiting for transfers between devices: 415 us -> 0.01 us  [the longest x1 0.01 us: body(): joined_all = lax.all_gather(joined_block, AXES, axis=0, tiled=True)]
    dot_general x18 -> x6, matrix products: 431 us -> 40.8 us  [dot(): return lax.dot_general(left, right, dims, preferred_element_type=f32)]
    pallas_call x0 -> x9, Pallas kernels: none -> 228 us  [the longest x4 104 us: feed(): pl.pallas_call(feed_kernel, grid=(tokens // tile,), in_specs=[row(D), row...]
    ppermute x0 -> x100, starting transfers between devices: none -> 219 us  [send(): return lax.ppermute(values, AXES, pairs)]
    unnamed x2 -> x0, blocking collectives: 82.7 us -> none
    convert_element_type x1 -> x44, other arithmetic: 0.01 us -> 51.9 us  [the longest x31 48.1 us: add_low(): functools.reduce(lambda a, b: a + b, [p.astype(f32) for p in parts])]
  transfers between devices with their start and end apart: 10 -> 102, of which waited for: 8 -> 32; matrix products, arithmetic and copies ran while one was open for 13% -> 20% of each run, Pallas kernels for 0% -> 19%
where the time goes in v2:
time: 1190 us; the launch traced here: 1180 us
  waiting for transfers between devices  455 us (38%)
  Pallas kernels  228 us (19%)
  starting transfers between devices  220 us (18%)
  local copies, waits for them, and re-layouts  112 us (9%)
  other arithmetic  109 us (9%)
  matrix products  40.8 us (3%)
  between operations  18.4 us (2%)
    ppermute x100, waiting for transfers between devices, send(): return lax.ppermute(values, AXES, pairs)  455 us
    ppermute x100, starting transfers between devices, send(): return lax.ppermute(values, AXES, pairs)  219 us
    pallas_call x4, Pallas kernels, feed(): pl.pallas_call(feed_kernel, grid=(tokens // tile,), in_specs=[row(D), row...  104 us
    pallas_call x1, Pallas kernels, weight_gradient(): pl.pallas_call(functools.partial(weight_gradient_kernel, count), grid=(D...  50.4 us
    convert_element_type x31, other arithmetic, add_low(): functools.reduce(lambda a, b: a + b, [p.astype(f32) for p in parts])  48.1 us
    dot_general x6, matrix products, dot(): return lax.dot_general(left, right, dims, preferred_element_type=f32)  40.8 us
    pallas_call x1, Pallas kernels, attend_back(): pl.pallas_call(functools.partial(attend_back_kernel, tq, tk), grid_spec=s...  28.1 us
    unnamed x137, local copies, waits for them, and re-layouts  27.4 us
  transfers between devices with their start and end apart: 102, of which 32 were waited for; matrix products, arithmetic and copies ran while one was open for 20% of the time, Pallas kernels for 19%

profile of v2, /device:TPU:0, one launch (start us, length us, event | category | flops | bytes accessed | tf_op | source)
XLA Modules:
  0.0 1182.7 jit_solution(9418009042819637137)
XLA Ops:
  31.7 48.1 %collective-permute-done.6 = bf16[64,2304]{1,0:T(8,128)(2,1)} collective-permute-done((bf16[64,2304]{1,0:T(8,128)(2,1)}, bf16[64,2304]{1,0:T(8,128)(2,1)}, u32[]{:S(2)}, u32[]{:S(2)}) %collective-permute-start.6) | collective-permute-done | bytes 294944 | tf_op jit(solution)/shard_map/ppermute | solution.py:433
  85.3 10.7 collective-permute-done.8
  105.8 8.2 collective-permute-done.12
  141.3 52.7 %collective-permute-done.14 = bf16[512,2304]{1,0:T(8,128)(2,1)} collective-permute-done((bf16[512,2304]{1,0:T(8,128)(2,1)S(1)}, bf16[512,2304]{1,0:T(8,128)(2,1)}, u32[]{:S(2)}, u32[]{:S(2)}) %collective-permute-start.14) | collective-permute-done | bytes 2359328 | tf_op jit(solution)/shard_map/ppermute | solution.py:433
  209.1 10.3 fusion.3.projected
  219.5 11.9 %rope.1.q = bf16[512,1920]{1,0:T(8,128)(2,1)} custom-call(f32[512,1920]{1,0:T(8,128)} %fusion.3.projected, f32[2,128]{1,0:T(2,128)} %pad_maximum_fusion.14.gains, f32[2,512,128]{2,1,0:T(8,128)} %pad_maximum_fusion.4.tables), custom_call_target="tpu_custom_call" | custom-call | flops 39321600 | bytes 5898240 | tf_op jit(solution)/shard_map/rope/pallas_call | solution.py:77
  239.8 10.5 collective-permute-done
  268.7 19.0 %attend.1 = (f32[512,1280]{1,0:T(8,128)}, bf16[20,512,128]{2,1,0:T(8,128)(2,1)}) custom-call(s32[1]{0:T(128)} %bitcast.1.offset, bf16[512,1920]{1,0:T(8,128)(2,1)} %rope.1.q, bf16[2048,640]{1,0:T(8,128)(2,1)} %copy-done.29, bf16[2048,128]{1,0:T(8,128)(2,1)} %select_convert_fusion.key_marks, bf16[512,128]{1,0:T(8,128)(2,1)} %and_convert_fusion.query_marks), custom_call_target="tpu_custom_call" | custom-call | flops 21474836480 | bytes 16777216 | tf_op jit(solution)/shard_map/attend/pallas_call | solution.py:231
  303.3 15.2 %collective-permute-start.20 = (bf16[512,2048]{1,0:T(8,128)(2,1)S(1)}, bf16[512,2048]{1,0:T(8,128)(2,1)S(1)}, u32[]{:S(2)}, u32[]{:S(2)}) collective-permute-start(bf16[512,2048]{1,0:T(8,128)(2,1)S(1)} %multiply_convert_fusion), channel_id=1, source_target_pairs={{0,2},{1,3},{2,0},{3,1},{4,6},{5,7},{6,4},{7,5},{8,10},{9,11},{10,... | collective-permute-start | bytes 6291464 | tf_op jit(solution)/shard_map/ppermute | solution.py:433
  329.4 17.6 %collective-permute-done.25 = bf16[512,2048]{1,0:T(8,128)(2,1)S(1)} collective-permute-done((bf16[512,2048]{1,0:T(8,128)(2,1)S(1)}, bf16[512,2048]{1,0:T(8,128)(2,1)S(1)}, u32[]{:S(2)}, u32[]{:S(2)}) %collective-permute-start.25) | collective-permute-done | bytes 2097184 | tf_op jit(solution)/shard_map/ppermute | solution.py:433
  348.1 16.0 %collective-permute-start.26 = (bf16[256,2048]{1,0:T(8,128)(2,1)}, bf16[256,2048]{1,0:T(8,128)(2,1)}, u32[]{:S(2)}, u32[]{:S(2)}) collective-permute-start(bf16[256,2048]{1,0:T(8,128)(2,1)} %slice.477), channel_id=1, source_target_pairs={{0,2},{1,3},{2,0},{3,1},{4,6},{5,7},{6,4},{7,5},{8,10},{9,11},{10,... | collective-permute-start | bytes 3145736 | tf_op jit(solution)/shard_map/ppermute | solution.py:433
  369.5 26.0 %feed.4 = (bf16[1024,768]{1,0:T(8,128)(2,1)}, bf16[1024,1536]{1,0:T(8,128)(2,1)}, bf16[1024,2048]{1,0:T(8,128)(2,1)}, bf16[1024,2048]{1,0:T(8,128)(2,1)}) custom-call(bf16[1024,2048]{1,0:T(8,128)(2,1)} %pad_maximum_fusion.1.normed.refs_0_, bf16[1024,2048]{1,0:T(8,128)(2,1)} %pad_maximum_fusion.2.upstream.refs_4_, ...), custom_call_target="tpu_custom_call" | custom-call | flops 32212254720 | bytes 30932992 | tf_op jit(solution)/shard_map/feed/pallas_call | solution.py:359
  411.6 25.8 %feed.7 = (bf16[1024,768]{1,0:T(8,128)(2,1)}, bf16[1024,1536]{1,0:T(8,128)(2,1)}, bf16[1024,2048]{1,0:T(8,128)(2,1)}, bf16[1024,2048]{1,0:T(8,128)(2,1)}) custom-call(bf16[1024,2048]{1,0:T(8,128)(2,1)} %constant_dynamic-update-slice_fusion.12.normed.refs_1_, bf16[1024,2048]{1,0:T(8,128)(2,1)} %copy-done.35, ...), custom_call_target="tpu_custom_call" | custom-call | flops 32212254720 | bytes 30932992 | tf_op jit(solution)/shard_map/feed/pallas_call | solution.py:359
  440.7 26.5 %feed.5 = (bf16[1024,768]{1,0:T(8,128)(2,1)}, bf16[1024,1536]{1,0:T(8,128)(2,1)}, bf16[1024,2048]{1,0:T(8,128)(2,1)}, bf16[1024,2048]{1,0:T(8,128)(2,1)}) custom-call(bf16[1024,2048]{1,0:T(8,128)(2,1)} %constant_dynamic-update-slice_fusion.normed.refs_2_, bf16[1024,2048]{1,0:T(8,128)(2,1)} %copy-done.37, ...), custom_call_target="tpu_custom_call" | custom-call | flops 32212254720 | bytes 30932992 | tf_op jit(solution)/shard_map/feed/pallas_call | solution.py:359
  489.5 25.8 %feed.6 = (bf16[1024,768]{1,0:T(8,128)(2,1)}, bf16[1024,1536]{1,0:T(8,128)(2,1)}, bf16[1024,2048]{1,0:T(8,128)(2,1)}, bf16[1024,2048]{1,0:T(8,128)(2,1)}) custom-call(bf16[1024,2048]{1,0:T(8,128)(2,1)} %constant_dynamic-update-slice_fusion.4.normed.refs_3_, bf16[1024,2048]{1,0:T(8,128)(2,1)} %constant_dynamic-update-slice_fusion.8.upstream.refs_7_, ...), custom_call_target="tpu_custom_call" | custom-call | flops 32212254720 | bytes 30932992 | tf_op jit(solution)/shard_map/feed/pallas_call | solution.py:359
  520.1 50.4 %weight_gradient.1 = bf16[2048,2304]{1,0:T(8,128)(2,1)} custom-call(bf16[1024,2048]{1,0:T(8,128)(2,1)} %pad_maximum_fusion.1.normed.refs_0_, bf16[1024,2048]{1,0:T(8,128)(2,1)} %constant_dynamic-update-slice_fusion.12.normed.refs_1_, bf16[1024,2048]{1,0:T(8,128)(2,1)} %constant_dynamic-update-slice_fusion.normed.refs_2_, ...), custom_call_target="tpu_custom_call" | custom-call | flops 51539607552 | bytes 52428800 | tf_op jit(solution)/shard_map/weight_gradient/pallas_call | solution.py:400
  600.3 34.9 %collective-permute-done.87 = bf16[512,2304]{1,0:T(8,128)(2,1)S(1)} collective-permute-done((bf16[512,2304]{1,0:T(8,128)(2,1)S(1)}, bf16[512,2304]{1,0:T(8,128)(2,1)S(1)}, u32[]{:S(2)}, u32[]{:S(2)}) %collective-permute-start.87) | collective-permute-done | bytes 2359328 | tf_op jit(solution)/shard_map/ppermute | solution.py:433
  641.9 21.8 %collective-permute-done.43 = bf16[256,2048]{1,0:T(8,128)(2,1)S(1)} collective-permute-done((bf16[256,2048]{1,0:T(8,128)(2,1)S(1)}, bf16[256,2048]{1,0:T(8,128)(2,1)S(1)}, u32[]{:S(2)}, u32[]{:S(2)}) %collective-permute-start.43) | collective-permute-done | bytes 1048608 | tf_op jit(solution)/shard_map/ppermute | solution.py:433
  670.4 13.3 %collective-permute-done.54 = bf16[256,2048]{1,0:T(8,128)(2,1)S(1)} collective-permute-done((bf16[256,2048]{1,0:T(8,128)(2,1)S(1)}, bf16[256,2048]{1,0:T(8,128)(2,1)S(1)}, u32[]{:S(2)}, u32[]{:S(2)}) %collective-permute-start.54) | collective-permute-done | bytes 1048608 | tf_op jit(solution)/shard_map/ppermute | solution.py:433
  692.7 13.5 %collective-permute-done.41 = bf16[256,2048]{1,0:T(8,128)(2,1)S(1)} collective-permute-done((bf16[256,2048]{1,0:T(8,128)(2,1)S(1)}, bf16[256,2048]{1,0:T(8,128)(2,1)S(1)}, u32[]{:S(2)}, u32[]{:S(2)}) %collective-permute-start.41) | collective-permute-done | bytes 1048608 | tf_op jit(solution)/shard_map/ppermute | solution.py:433
  712.4 14.9 %collective-permute-done.44 = bf16[256,2048]{1,0:T(8,128)(2,1)S(1)} collective-permute-done((bf16[256,2048]{1,0:T(8,128)(2,1)S(1)}, bf16[256,2048]{1,0:T(8,128)(2,1)S(1)}, u32[]{:S(2)}, u32[]{:S(2)}) %collective-permute-start.44) | collective-permute-done | bytes 1048608 | tf_op jit(solution)/shard_map/ppermute | solution.py:433
  742.7 28.1 %attend_back.1 = (f32[512,1280]{1,0:T(8,128)}, bf16[2048,640]{1,0:T(8,128)(2,1)}) custom-call(s32[1]{0:T(128)} %bitcast.1.offset, bf16[20,512,128]{2,1,0:T(8,128)(2,1)} %get-tuple-element.38.q_marked, bf16[512,1280]{1,0:T(8,128)(2,1)} %convolution_convert_fusion.2.d_out, f32[512,1280]{1,0:T(8,128)} %get-tuple-element.29.out, bf16[2048,640]{1,0:T(8,128)(2,1)} %copy-done.29, ...), custom_call_target="tpu_custom_call" | custom-call | flops 42949672960 | bytes 16777216 | tf_op jit(solution)/shard_map/attend_back/pallas_call | solution.py:321
  772.3 17.7 %collective-permute-start.55 = (bf16[256,640]{1,0:T(8,128)(2,1)S(1)}, bf16[256,640]{1,0:T(8,128)(2,1)S(1)}, u32[]{:S(2)}, u32[]{:S(2)}) collective-permute-start(bf16[256,640]{1,0:T(8,128)(2,1)S(1)} %get-tuple-element.75), channel_id=1, source_target_pairs={{0,1},{1,0},{2,3},{3,2},{4,5},{5,4},{6,7},{7,6},{8,9},{9,8},{10,11... | collective-permute-start | bytes 983048 | tf_op jit(solution)/shard_map/ppermute | solution.py:433
  793.3 31.2 %collective-permute-start.59 = (bf16[256,640]{1,0:T(8,128)(2,1)S(1)}, bf16[256,640]{1,0:T(8,128)(2,1)S(1)}, u32[]{:S(2)}, u32[]{:S(2)}) collective-permute-start(bf16[256,640]{1,0:T(8,128)(2,1)S(1)} %get-tuple-element.77), channel_id=1, source_target_pairs={{0,2},{1,3},{2,0},{3,1},{4,6},{5,7},{6,4},{7,5},{8,10},{9,11},{10,... | collective-permute-start | bytes 983048 | tf_op jit(solution)/shard_map/ppermute | solution.py:433
  851.5 14.2 %rope_back.1 = (bf16[512,1920]{1,0:T(8,128)(2,1)}, f32[8,128]{1,0:T(8,128)}) custom-call(f32[512,1280]{1,0:T(8,128)} %get-tuple-element.39.dq, f32[512,640]{1,0:T(8,128)} %maximum_convert_fusion.dkv, f32[512,1920]{1,0:T(8,128)} %fusion.3.projected, f32[2,128]{1,0:T(2,128)} %pad_maximum_fusion.14.gains, f32[2,512,128]{2,1,0:T(8,128)} %pad_maximum_fusion.4.tables), custom_call_target="tpu_custom_call" | custom-call | flops 58982400 | bytes 9830400 | tf_op jit(solution)/shard_map/rope_back/pallas_call | solution.py:117
  866.5 10.8 fusion.23
  905.9 12.3 %copy.37 = bf16[2048,2048]{1,0:T(8,128)(2,1)} copy(bf16[2048,2048]{0,1:T(8,128)(2,1)} %pad_maximum_fusion) | data formatting | bytes 16777216 | tf_op jit(solution)/shard_map/concatenate | solution.py:670
  938.2 47.9 %collective-permute-done.81 = bf16[64,1280]{1,0:T(8,128)(2,1)S(1)} collective-permute-done((bf16[64,1280]{1,0:T(8,128)(2,1)S(1)}, bf16[64,1280]{1,0:T(8,128)(2,1)S(1)}, u32[]{:S(2)}, u32[]{:S(2)}) %collective-permute-start.81) | collective-permute-done | bytes 163872 | tf_op jit(solution)/shard_map/ppermute | solution.py:433
  1005.4 47.6 %collective-permute-done.86 = bf16[64,1280]{1,0:T(8,128)(2,1)S(1)} collective-permute-done((bf16[64,1280]{1,0:T(8,128)(2,1)S(1)}, bf16[64,1280]{1,0:T(8,128)(2,1)S(1)}, u32[]{:S(2)}, u32[]{:S(2)}) %collective-permute-start.86) | collective-permute-done | bytes 163872 | tf_op jit(solution)/shard_map/ppermute | solution.py:433
  1067.6 20.9 %collective-permute-done.94 = bf16[64,2304]{1,0:T(8,128)(2,1)S(1)} collective-permute-done((bf16[64,2304]{1,0:T(8,128)(2,1)S(1)}, bf16[64,2304]{1,0:T(8,128)(2,1)S(1)}, u32[]{:S(2)}, u32[]{:S(2)}) %collective-permute-start.94) | collective-permute-done | bytes 294944 | tf_op jit(solution)/shard_map/ppermute | solution.py:433
  1091.8 18.4 %collective-permute-done.95 = bf16[64,2304]{1,0:T(8,128)(2,1)S(1)} collective-permute-done((bf16[64,2304]{1,0:T(8,128)(2,1)S(1)}, bf16[64,2304]{1,0:T(8,128)(2,1)S(1)}, u32[]{:S(2)}, u32[]{:S(2)}) %collective-permute-start.95) | collective-permute-done | bytes 294944 | tf_op jit(solution)/shard_map/ppermute | solution.py:433
  1112.5 8.4 collective-permute-done.67
  (515 shorter events, 433.6 us)
Async XLA Ops:
  7.2 199.6 %all-gather.3.cloned.1.call-start = ((), (), s32[]{:S(2)}) async-start(), calls=%async_computation | async-start | bytes 8650752 | tf_op jit(solution)/shard_map/all_gather | solution.py:531
  10.9 276.8 %all-gather.5.cloned.1.call-start = ((), (), s32[]{:S(2)}) async-start(), calls=%async_computation.1 | async-start | bytes 5406720 | tf_op jit(solution)/shard_map/all_gather | solution.py:532
  11.0 113.5 %collective-permute-start.30 = (bf16[512,2048]{1,0:T(8,128)(2,1)}, bf16[512,2048]{1,0:T(8,128)(2,1)}, u32[]{:S(2)}, u32[]{:S(2)}) collective-permute-start(bf16[512,2048]{1,0:T(8,128)(2,1)} %bitcast.150), channel_id=1, source_target_pairs={{0,1},{1,0},{2,3},{3,2},{4,5},{5,4},{6,7},{7,6},{8,9},{9,8},{10,11... | collective-permute-start | bytes 6291464 | tf_op jit(solution)/shard_map/ppermute | solution.py:433
  14.0 112.8 %collective-permute-start.22 = (bf16[512,2048]{1,0:T(8,128)(2,1)}, bf16[512,2048]{1,0:T(8,128)(2,1)}, u32[]{:S(2)}, u32[]{:S(2)}) collective-permute-start(bf16[512,2048]{1,0:T(8,128)(2,1)} %bitcast.151), channel_id=1, source_target_pairs={{0,2},{1,3},{2,0},{3,1},{4,6},{5,7},{6,4},{7,5},{8,10},{9,11},{10,... | collective-permute-start | bytes 6291464 | tf_op jit(solution)/shard_map/ppermute | solution.py:433
  15.5 121.7 %collective-permute-start.5 = (bf16[512,2048]{1,0:T(8,128)(2,1)}, bf16[512,2048]{1,0:T(8,128)(2,1)}, u32[]{:S(2)}, u32[]{:S(2)}) collective-permute-start(bf16[512,2048]{1,0:T(8,128)(2,1)} %bitcast.152), channel_id=1, source_target_pairs={{0,4},{1,5},{2,6},{3,7},{4,0},{5,1},{6,2},{7,3},{8,12},{9,13},{10,... | collective-permute-start | bytes 6291464 | tf_op jit(solution)/shard_map/ppermute | solution.py:433
  22.0 62.2 %collective-permute-start.7 = (bf16[64,2304]{1,0:T(8,128)(2,1)}, bf16[64,2304]{1,0:T(8,128)(2,1)}, u32[]{:S(2)}, u32[]{:S(2)}) collective-permute-start(bf16[64,2304]{1,0:T(8,128)(2,1)} %pad_maximum_fusion.7), channel_id=1, source_target_pairs={{0,2},{1,3},{2,0},{3,1},{4,6},{5,7},{6,4},{7,5},{8,10},{9,11},{10,... | collective-permute-start | bytes 884744 | tf_op jit(solution)/shard_map/ppermute | solution.py:433
  114.1 79.9 %collective-permute-start.14 = (bf16[512,2304]{1,0:T(8,128)(2,1)S(1)}, bf16[512,2304]{1,0:T(8,128)(2,1)}, u32[]{:S(2)}, u32[]{:S(2)}) collective-permute-start(bf16[512,2304]{1,0:T(8,128)(2,1)S(1)} %constant_dynamic-update-slice_fusion.17), channel_id=1, source_target_pairs={{0,8},{1,9},{2,10},{3,11},{4,12},{5,13},{6,14},{7,15},{8,16},{9,17... | collective-permute-start | bytes 7077896 | tf_op jit(solution)/shard_map/ppermute | solution.py:433
  119.6 79.9 %collective-permute-start.13 = (bf16[512,2304]{1,0:T(8,128)(2,1)S(1)}, bf16[512,2304]{1,0:T(8,128)(2,1)}, u32[]{:S(2)}, u32[]{:S(2)}) collective-permute-start(bf16[512,2304]{1,0:T(8,128)(2,1)S(1)} %constant_dynamic-update-slice_fusion.17), channel_id=1, source_target_pairs={{8,0},{9,1},{10,2},{11,3},{12,4},{13,5},{14,6},{15,7},{16,8},{17,9... | collective-permute-start | bytes 7077896 | tf_op jit(solution)/shard_map/ppermute | solution.py:433
  125.8 75.7 %collective-permute-start.31 = (bf16[256,2048]{1,0:T(8,128)(2,1)S(1)}, bf16[256,2048]{1,0:T(8,128)(2,1)}, u32[]{:S(2)}, u32[]{:S(2)}) collective-permute-start(bf16[256,2048]{1,0:T(8,128)(2,1)S(1)} %slice.479), channel_id=1, source_target_pairs={{0,2},{1,3},{2,0},{3,1},{4,6},{5,7},{6,4},{7,5},{8,10},{9,11},{10,... | collective-permute-start | bytes 3145736 | tf_op jit(solution)/shard_map/ppermute | solution.py:433
  128.9 76.8 %collective-permute-start.32 = (bf16[256,2048]{1,0:T(8,128)(2,1)S(1)}, bf16[256,2048]{1,0:T(8,128)(2,1)S(1)}, u32[]{:S(2)}, u32[]{:S(2)}) collective-permute-start(bf16[256,2048]{1,0:T(8,128)(2,1)S(1)} %slice.480), channel_id=1, source_target_pairs={{0,1},{1,0},{2,3},{3,2},{4,5},{5,4},{6,7},{7,6},{8,9},{9,8},{10,11... | collective-permute-start | bytes 3145736 | tf_op jit(solution)/shard_map/ppermute | solution.py:433
  137.2 98.6 %collective-permute-start.39 = (bf16[512,2048]{1,0:T(8,128)(2,1)}, bf16[512,2048]{1,0:T(8,128)(2,1)}, u32[]{:S(2)}, u32[]{:S(2)}) collective-permute-start(bf16[512,2048]{1,0:T(8,128)(2,1)} %collective-permute-done.30), channel_id=1, source_target_pairs={{0,4},{1,5},{2,6},{3,7},{4,0},{5,1},{6,2},{7,3},{8,12},{9,13},{10,... | collective-permute-start | bytes 6291464 | tf_op jit(solution)/shard_map/ppermute | solution.py:433
  251.8 66.7 %collective-permute-start.16 = (bf16[512,2304]{1,0:T(8,128)(2,1)}, bf16[512,2304]{1,0:T(8,128)(2,1)}, u32[]{:S(2)}, u32[]{:S(2)}) collective-permute-start(bf16[512,2304]{1,0:T(8,128)(2,1)} %collective-permute-done.15), channel_id=1, source_target_pairs={{16,24},{17,25},{18,26},{19,27},{20,28},{21,29},{22,30},{23,31}} | collective-permute-start | bytes 7077896 | tf_op jit(solution)/shard_map/ppermute | solution.py:433
  257.5 68.3 %collective-permute-start.18 = (bf16[512,2304]{1,0:T(8,128)(2,1)}, bf16[512,2304]{1,0:T(8,128)(2,1)}, u32[]{:S(2)}, u32[]{:S(2)}) collective-permute-start(bf16[512,2304]{1,0:T(8,128)(2,1)} %collective-permute-done.17), channel_id=1, source_target_pairs={{8,0},{9,1},{10,2},{11,3},{12,4},{13,5},{14,6},{15,7}} | collective-permute-start | bytes 7077896 | tf_op jit(solution)/shard_map/ppermute | solution.py:433
  303.3 60.8 %collective-permute-start.20 = (bf16[512,2048]{1,0:T(8,128)(2,1)S(1)}, bf16[512,2048]{1,0:T(8,128)(2,1)S(1)}, u32[]{:S(2)}, u32[]{:S(2)}) collective-permute-start(bf16[512,2048]{1,0:T(8,128)(2,1)S(1)} %multiply_convert_fusion), channel_id=1, source_target_pairs={{0,2},{1,3},{2,0},{3,1},{4,6},{5,7},{6,4},{7,5},{8,10},{9,11},{10,... | collective-permute-start | bytes 6291464 | tf_op jit(solution)/shard_map/ppermute | solution.py:433
  400.3 71.4 %collective-permute-start.45 = (bf16[512,2048]{1,0:T(8,128)(2,1)}, bf16[512,2048]{1,0:T(8,128)(2,1)}, u32[]{:S(2)}, u32[]{:S(2)}) collective-permute-start(bf16[512,2048]{1,0:T(8,128)(2,1)} %slice.387), channel_id=1, source_target_pairs={{0,4},{1,5},{2,6},{3,7},{4,0},{5,1},{6,2},{7,3},{8,12},{9,13},{10,... | collective-permute-start | bytes 6291464 | tf_op jit(solution)/shard_map/ppermute | solution.py:433
  400.8 79.6 %collective-permute-start.19 = (bf16[512,2048]{1,0:T(8,128)(2,1)}, bf16[512,2048]{1,0:T(8,128)(2,1)S(1)}, u32[]{:S(2)}, u32[]{:S(2)}) collective-permute-start(bf16[512,2048]{1,0:T(8,128)(2,1)} %slice.367), channel_id=1, source_target_pairs={{0,4},{1,5},{2,6},{3,7},{4,0},{5,1},{6,2},{7,3},{8,12},{9,13},{10,... | collective-permute-start | bytes 6291464 | tf_op jit(solution)/shard_map/ppermute | solution.py:433
  405.7 78.4 %collective-permute-start.28 = (bf16[256,2048]{1,0:T(8,128)(2,1)}, bf16[256,2048]{1,0:T(8,128)(2,1)}, u32[]{:S(2)}, u32[]{:S(2)}) collective-permute-start(bf16[256,2048]{1,0:T(8,128)(2,1)} %collective-permute-done.26), channel_id=1, source_target_pairs={{0,4},{1,5},{2,6},{3,7},{4,0},{5,1},{6,2},{7,3},{8,12},{9,13},{10,... | collective-permute-start | bytes 3145736 | tf_op jit(solution)/shard_map/ppermute | solution.py:433
  407.9 79.1 %collective-permute-start.29 = (bf16[256,2048]{1,0:T(8,128)(2,1)S(1)}, bf16[256,2048]{1,0:T(8,128)(2,1)}, u32[]{:S(2)}, u32[]{:S(2)}) collective-permute-start(bf16[256,2048]{1,0:T(8,128)(2,1)S(1)} %collective-permute-done.27), channel_id=1, source_target_pairs={{0,4},{1,5},{2,6},{3,7},{4,0},{5,1},{6,2},{7,3},{8,12},{9,13},{10,... | collective-permute-start | bytes 3145736 | tf_op jit(solution)/shard_map/ppermute | solution.py:433
  471.6 103.2 %collective-permute-start.50 = (bf16[512,2048]{1,0:T(8,128)(2,1)}, bf16[512,2048]{1,0:T(8,128)(2,1)}, u32[]{:S(2)}, u32[]{:S(2)}) collective-permute-start(bf16[512,2048]{1,0:T(8,128)(2,1)} %slice.396), channel_id=1, source_target_pairs={{0,4},{1,5},{2,6},{3,7},{4,0},{5,1},{6,2},{7,3},{8,12},{9,13},{10,... | collective-permute-start | bytes 6291464 | tf_op jit(solution)/shard_map/ppermute | solution.py:433
  471.7 106.9 %collective-permute-start.40 = (bf16[512,2048]{1,0:T(8,128)(2,1)}, bf16[512,2048]{1,0:T(8,128)(2,1)}, u32[]{:S(2)}, u32[]{:S(2)}) collective-permute-start(bf16[512,2048]{1,0:T(8,128)(2,1)} %slice.380), channel_id=1, source_target_pairs={{0,4},{1,5},{2,6},{3,7},{4,0},{5,1},{6,2},{7,3},{8,12},{9,13},{10,... | collective-permute-start | bytes 6291464 | tf_op jit(solution)/shard_map/ppermute | solution.py:433
  481.7 105.1 %collective-permute-start.46 = (bf16[512,2048]{1,0:T(8,128)(2,1)}, bf16[512,2048]{1,0:T(8,128)(2,1)}, u32[]{:S(2)}, u32[]{:S(2)}) collective-permute-start(bf16[512,2048]{1,0:T(8,128)(2,1)} %slice.390), channel_id=1, source_target_pairs={{0,4},{1,5},{2,6},{3,7},{4,0},{5,1},{6,2},{7,3},{8,12},{9,13},{10,... | collective-permute-start | bytes 6291464 | tf_op jit(solution)/shard_map/ppermute | solution.py:433
  484.2 105.8 %collective-permute-start.24 = (bf16[512,2048]{1,0:T(8,128)(2,1)}, bf16[512,2048]{1,0:T(8,128)(2,1)}, u32[]{:S(2)}, u32[]{:S(2)}) collective-permute-start(bf16[512,2048]{1,0:T(8,128)(2,1)} %slice.370), channel_id=1, source_target_pairs={{0,4},{1,5},{2,6},{3,7},{4,0},{5,1},{6,2},{7,3},{8,12},{9,13},{10,... | collective-permute-start | bytes 6291464 | tf_op jit(solution)/shard_map/ppermute | solution.py:433
  520.0 73.6 %collective-permute-start.47 = (bf16[512,2048]{1,0:T(8,128)(2,1)}, bf16[512,2048]{1,0:T(8,128)(2,1)}, u32[]{:S(2)}, u32[]{:S(2)}) collective-permute-start(bf16[512,2048]{1,0:T(8,128)(2,1)} %slice.393), channel_id=1, source_target_pairs={{0,4},{1,5},{2,6},{3,7},{4,0},{5,1},{6,2},{7,3},{8,12},{9,13},{10,... | collective-permute-start | bytes 6291464 | tf_op jit(solution)/shard_map/ppermute | solution.py:433
  586.9 80.1 %collective-permute-start.51 = (bf16[256,2048]{1,0:T(8,128)(2,1)S(1)}, bf16[256,2048]{1,0:T(8,128)(2,1)S(1)}, u32[]{:S(2)}, u32[]{:S(2)}) collective-permute-start(bf16[256,2048]{1,0:T(8,128)(2,1)S(1)} %slice.490), channel_id=1, source_target_pairs={{0,1},{1,0},{2,3},{3,2},{4,5},{5,4},{6,7},{7,6},{8,9},{9,8},{10,11... | collective-permute-start | bytes 3145736 | tf_op jit(solution)/shard_map/ppermute | solution.py:433
  590.0 78.6 %collective-permute-start.52 = (bf16[256,2048]{1,0:T(8,128)(2,1)S(1)}, bf16[256,2048]{1,0:T(8,128)(2,1)S(1)}, u32[]{:S(2)}, u32[]{:S(2)}) collective-permute-start(bf16[256,2048]{1,0:T(8,128)(2,1)S(1)} %slice.492), channel_id=1, source_target_pairs={{0,2},{1,3},{2,0},{3,1},{4,6},{5,7},{6,4},{7,5},{8,10},{9,11},{10,... | collective-permute-start | bytes 3145736 | tf_op jit(solution)/shard_map/ppermute | solution.py:433
  664.5 177.9 %collective-permute-start.90 = (bf16[512,2304]{1,0:T(8,128)(2,1)}, bf16[512,2304]{1,0:T(8,128)(2,1)}, u32[]{:S(2)}, u32[]{:S(2)}) collective-permute-start(bf16[512,2304]{1,0:T(8,128)(2,1)} %get-tuple-element.58), channel_id=1, source_target_pairs={{24,16},{25,17},{26,18},{27,19},{28,20},{29,21},{30,22},{31,23}} | collective-permute-start | bytes 7077896 | tf_op jit(solution)/shard_map/ppermute | solution.py:433
  706.2 136.1 %collective-permute-start.88 = (bf16[512,2304]{1,0:T(8,128)(2,1)}, bf16[512,2304]{1,0:T(8,128)(2,1)}, u32[]{:S(2)}, u32[]{:S(2)}) collective-permute-start(bf16[512,2304]{1,0:T(8,128)(2,1)} %add_convert_fusion.4), channel_id=1, source_target_pairs={{0,8},{1,9},{2,10},{3,11},{4,12},{5,13},{6,14},{7,15},{8,16},{9,17... | collective-permute-start | bytes 7077896 | tf_op jit(solution)/shard_map/ppermute | solution.py:433
  848.1 143.5 %collective-permute-start.91 = (bf16[512,2304]{1,0:T(8,128)(2,1)}, bf16[512,2304]{1,0:T(8,128)(2,1)}, u32[]{:S(2)}, u32[]{:S(2)}) collective-permute-start(bf16[512,2304]{1,0:T(8,128)(2,1)} %get-tuple-element.56), channel_id=1, source_target_pairs={{16,8},{17,9},{18,10},{19,11},{20,12},{21,13},{22,14},{23,15},{24,... | collective-permute-start | bytes 7077896 | tf_op jit(solution)/shard_map/ppermute | solution.py:433
  927.6 126.2 %collective-permute-start.61 = (bf16[4,4,64,2048]{3,2,1,0:T(8,128)(2,1)}, bf16[4,4,64,2048]{3,2,1,0:T(8,128)(2,1)}, u32[]{:S(2)}, u32[]{:S(2)}) collective-permute-start(bf16[4,4,64,2048]{3,2,1,0:T(8,128)(2,1)} %dynamic-slice_bitcast_fusion), channel_id=1, source_target_pairs={{0,4},{1,5},{2,6},{3,7},{4,0},{5,1},{6,2},{7,3},{8,12},{9,13},{10,... | collective-permute-start | bytes 12582920 | tf_op jit(solution)/shard_map/ppermute | solution.py:433
  927.6 133.3 %collective-permute-start.89 = (bf16[512,2304]{1,0:T(8,128)(2,1)}, bf16[512,2304]{1,0:T(8,128)(2,1)}, u32[]{:S(2)}, u32[]{:S(2)}) collective-permute-start(bf16[512,2304]{1,0:T(8,128)(2,1)} %get-tuple-element.55), channel_id=1, source_target_pairs={{0,8},{1,9},{2,10},{3,11},{4,12},{5,13},{6,14},{7,15},{8,16},{9,17... | collective-permute-start | bytes 7077896 | tf_op jit(solution)/shard_map/ppermute | solution.py:433
  995.0 65.9 %collective-permute-start.92 = (bf16[512,2304]{1,0:T(8,128)(2,1)S(1)}, bf16[512,2304]{1,0:T(8,128)(2,1)S(1)}, u32[]{:S(2)}, u32[]{:S(2)}) collective-permute-start(bf16[512,2304]{1,0:T(8,128)(2,1)S(1)} %add_convert_fusion.1), channel_id=1, source_target_pairs={{8,0},{9,1},{10,2},{11,3},{12,4},{13,5},{14,6},{15,7},{16,8},{17,9... | collective-permute-start | bytes 7077896 | tf_op jit(solution)/shard_map/ppermute | solution.py:433
  1059.7 71.4 %collective-permute-start.64 = (bf16[128,2048]{1,0:T(8,128)(2,1)S(1)}, bf16[128,2048]{1,0:T(8,128)(2,1)S(1)}, u32[]{:S(2)}, u32[]{:S(2)}) collective-permute-start(bf16[128,2048]{1,0:T(8,128)(2,1)S(1)} %get-tuple-element.62), channel_id=1, source_target_pairs={{0,1},{1,0},{2,3},{3,2},{4,5},{5,4},{6,7},{7,6},{8,9},{9,8},{10,11... | collective-permute-start | bytes 1572872 | tf_op jit(solution)/shard_map/ppermute | solution.py:433
  (133 other events, 3248.5 us)
Sparse Core Ops, SparseCore 0:
  11.4 98.6 all-gather.2
  113.0 79.6 all-gather.4

commit v3 on v2

--- a/solution.py
+++ b/solution.py
@@ -24,6 +24,9 @@
 f32 = jnp.float32
 bf16 = jnp.bfloat16
 AXES = ("dp", "seq")
+MESH = pl.DeviceIdType.MESH
+ANY = pl.BlockSpec(memory_space=pl.ANY)
+VMEM = pl.BlockSpec(memory_space=pltpu.VMEM)
 NN = (((1,), (0,)), ((), ()))
 NT = (((1,), (1,)), ((), ()))
 TN = (((0,), (0,)), ((), ()))
@@ -411,6 +414,188 @@
     )(*normed, *upstream, *both, *hidden)
 
 
+def coordinates():
+    dp = lax.axis_index("dp")
+    return dp // CORES, dp % CORES, lax.axis_index("seq")
+
+
+def device_at(place):
+    z, c, s = place
+    return z * CORES + c, s
+
+
+def greet(peers, neighbours):
+    barrier = pltpu.get_barrier_semaphore()
+    count = len(peers)
+    for device in peers:
+        pl.semaphore_signal(barrier, inc=1, device_id=device_at(device), device_id_type=MESH)
+    for condition, device in neighbours:
+
+        @pl.when(condition)
+        def _():
+            pl.semaphore_signal(barrier, inc=1, device_id=device_at(device), device_id_type=MESH)
+
+        count = count + condition.astype(jnp.int32)
+    pl.semaphore_wait(barrier, count)
+
+
+def remote(source, target, sems, slot, device):
+    send, receive = sems
+    return pltpu.make_async_remote_copy(
+        src_ref=source,
+        dst_ref=target,
+        send_sem=send.at[slot],
+        recv_sem=receive.at[slot],
+        device_id=device_at(device),
+        device_id_type=MESH,
+    )
+
+
+def first_gather_kernel(n_z, n_seq, shares, joined, out_rows, block, joined_z, out_z, local, send, receive):
+    z, c, s = coordinates()
+    plane = CORES * n_seq
+    rows = joined.shape[0]
+    me = c * n_seq + s
+    others = [(z, c ^ (k // n_seq), s ^ (k % n_seq)) for k in range(1, plane)]
+    above, below = (z + 1, c, s), (z - 1, c, s)
+    greet(others, [(z > 0, below), (z < n_z - 1, above)])
+    sems = (send, receive)
+    mine = [
+        pltpu.make_async_copy(joined, joined_z.at[z], local.at[0]),
+        pltpu.make_async_copy(out_rows, out_z.at[z], local.at[1]),
+        pltpu.make_async_copy(shares.at[me], block.at[me], local.at[2]),
+    ]
+    for copy in mine:
+        copy.start()
+    slot = 0
+    chains = []
+    for source, target in ((joined, joined_z), (out_rows, out_z)):
+        ups, downs = [], []
+        for k in range(1, n_z):
+            held = source if k == 1 else target.at[z - (k - 1)]
+            ups.append(remote(held, target.at[z - (k - 1)], sems, slot, above))
+            held = source if k == 1 else target.at[z + (k - 1)]
+            downs.append(remote(held, target.at[z + (k - 1)], sems, slot + 1, below))
+            slot += 2
+        chains.append((ups, downs))
+    for ups, downs in chains:
+        pl.when(z < n_z - 1)(ups[0].start)
+        pl.when(z > 0)(downs[0].start)
+    sent = []
+    for k, (tz, tc, ts) in enumerate(others):
+        copy = remote(shares.at[tc * n_seq + ts], block.at[me], sems, slot + k, (tz, tc, ts))
+        copy.start()
+        sent.append(copy)
+    for k in range(1, n_z):
+        for ups, downs in chains:
+            pl.when(z >= k)(ups[k - 1].wait_recv)
+            pl.when(z + k < n_z)(downs[k - 1].wait_recv)
+            if k < n_z - 1:
+                pl.when((z >= k) & (z < n_z - 1))(ups[k].start)
+                pl.when((z + k < n_z) & (z > 0))(downs[k].start)
+    for k in range(1, n_z):
+        for ups, downs in chains:
+            pl.when((z >= k - 1) & (z < n_z - 1))(ups[k - 1].wait_send)
+            pl.when((z + k - 1 < n_z) & (z > 0))(downs[k - 1].wait_send)
+    for copy in sent:
+        copy.wait()
+    for copy in mine:
+        copy.wait()
+
+
+def first_gather(n_z, n_seq, shares, joined, out_rows):
+    plane = CORES * n_seq
+    rows = joined.shape[0]
+    copies = 4 * (n_z - 1) + plane - 1
+    shape = lambda *dims: jax.ShapeDtypeStruct(dims, bf16)
+    return pl.pallas_call(
+        functools.partial(first_gather_kernel, n_z, n_seq),
+        in_specs=[VMEM] * 3,
+        out_specs=[ANY] * 3,
+        out_shape=[
+            shape(*shares.shape),
+            shape(n_z, rows, joined.shape[1]),
+            shape(n_z, rows, out_rows.shape[1]),
+        ],
+        scratch_shapes=[
+            pltpu.SemaphoreType.DMA((3,)),
+            pltpu.SemaphoreType.DMA((copies,)),
+            pltpu.SemaphoreType.DMA((copies,)),
+        ],
+        compiler_params=pltpu.CompilerParams(collective_id=0, has_side_effects=True),
+        name="first_gather",
+    )(shares, joined, out_rows)
+
+
+def plane_routes(n_seq):
+    if n_seq == 4:
+        return [(1, 0, 0, 1), (2, 0, 0, 2)], [(3, 1, 1, 2), (4, 2, 2, 1)]
+    return [(k, 0, 0, k) for k in range(1, n_seq)], []
+
+
+def spread_plane_kernel(n_z, n_seq, joined_z, out_z, joined, out_rows, local, send, receive):
+    z, c, s = coordinates()
+    direct, handed = plane_routes(n_seq)
+    count = len(direct) + len(handed) + 1
+    core_peer = (z, 1 - c, s)
+    greet([(z, c, s ^ k) for k in sorted({r[3] for r in direct + handed})] + [core_peer], [])
+    half = n_z // 2
+    parts = {0: slice(0, n_z), 1: slice(0, half), 2: slice(half, n_z)}
+    plans = []
+    own = []
+    for index, (source, target) in enumerate(((joined_z, joined), (out_z, out_rows))):
+        sems = (send.at[index], receive.at[index])
+        at = lambda k, part, target=target: target.at[parts[part], c * n_seq + (s ^ k)]
+        own.append(pltpu.make_async_copy(source, at(0, 0), local.at[index]))
+        own[-1].start()
+        first = [remote(source, at(0, 0), sems, slot, (z, c, s ^ peer)) for slot, _, _, peer in direct]
+        second = [remote(at(k, p), at(k, p), sems, slot, (z, c, s ^ peer)) for slot, k, p, peer in handed]
+        to_core = [remote(source, at(0, 0), sems, count, core_peer)]
+        held = [(k, 0) for k in range(1, n_seq)] if not handed else [(1, 0), (2, 0), (3, 1), (3, 2)]
+        to_core += [remote(at(k, p), at(k, p), sems, count + 1 + i, core_peer) for i, (k, p) in enumerate(held)]
+        plans.append((first, second, to_core))
+    for first, second, to_core in plans:
+        for copy in first + to_core[:1]:
+            copy.start()
+    for first, second, to_core in plans:
+        for i, copy in enumerate(first):
+            copy.wait_recv()
+            if second:
+                second[i].start()
+            to_core[1 + i].start()
+    for first, second, to_core in plans:
+        for i, copy in enumerate(second):
+            copy.wait_recv()
+            to_core[1 + len(first) + i].start()
+    for first, second, to_core in plans:
+        for copy in first + second:
+            copy.wait_send()
+        for copy in to_core:
+            copy.wait()
+    for copy in own:
+        copy.wait()
+
+
+def spread_plane(n_z, n_seq, joined_z, out_z):
+    rows = joined_z.shape[1]
+    direct, handed = plane_routes(n_seq)
+    slots = 2 * (len(direct) + len(handed)) + 3
+    shape = lambda a: jax.ShapeDtypeStruct((n_z, CORES * n_seq, rows, a.shape[2]), bf16)
+    return pl.pallas_call(
+        functools.partial(spread_plane_kernel, n_z, n_seq),
+        in_specs=[VMEM] * 2,
+        out_specs=[ANY] * 2,
+        out_shape=[shape(joined_z), shape(out_z)],
+        scratch_shapes=[
+            pltpu.SemaphoreType.DMA((2,)),
+            pltpu.SemaphoreType.DMA((2, slots)),
+            pltpu.SemaphoreType.DMA((2, slots)),
+        ],
+        compiler_params=pltpu.CompilerParams(collective_id=1, has_side_effects=True),
+        name="spread_plane",
+    )(joined_z, out_z)
+
+
 class Links:
     def __init__(self, n_dp, n_seq):
         self.n_z = n_dp // CORES
@@ -418,8 +603,7 @@
         self.plane = CORES * n_seq
 
     def place(self):
-        dp = lax.axis_index("dp")
-        return dp // CORES, dp % CORES, lax.axis_index("seq")
+        return coordinates()
 
     def send(self, values, pairs_of):
         pairs = []
@@ -528,8 +712,19 @@
     joined_block = jnp.concatenate(
         [joined_weight[:, :Q_WIDTH], kv_columns.reshape(rows, 2 * KV_WIDTH), gain_block], axis=1
     )
-    joined_all = lax.all_gather(joined_block, AXES, axis=0, tiled=True)
-    output_all = lax.all_gather(output_weight.T, AXES, axis=0, tiled=True)
+    shrink_rows = shrink_weight.T
+    shares = jnp.concatenate(
+        [expand_weight.reshape(rows, 2, plane, units), shrink_rows.reshape(rows, 1, plane, units)], axis=1
+    )
+    shares = shares.transpose(2, 0, 1, 3).reshape(plane, rows, 3 * units)
+    block, joined_z, output_z = first_gather(n_z, n_seq, shares, joined_block, output_weight.T)
+    lines = [[a * CORES + c for a in range(n_z)] for c in range(CORES)]
+    weights = lax.all_gather(
+        block.reshape(plane * rows, 3 * units), "dp", axis=0, tiled=True, axis_index_groups=lines
+    )
+    joined_all, output_all = spread_plane(n_z, n_seq, joined_z, output_z)
+    joined_all = joined_all.reshape(D, QKV + PAIR)
+    output_all = output_all.reshape(D, Q_WIDTH)
     gains = joined_all[:, QKV:].reshape(devices, rows * PAIR)[:, :own_gains].reshape(GAINS).astype(f32)
     joined_all = joined_all[:, :QKV]
     gain_one = gains[:D]
@@ -537,20 +732,6 @@
     gain_key = gains[D + HEAD_DIM : D + PAIR]
     gain_two = gains[D + PAIR :]
     head_gains = jnp.stack([jnp.tile(gain_query, 2), jnp.tile(gain_key, 2)])
-
-    shrink_rows = shrink_weight.T
-    shares = []
-    for k in range(plane):
-        p = (core ^ (k // n_seq)) * n_seq + (seq ^ (k % n_seq))
-        take = lambda a, start: lax.dynamic_slice_in_dim(a, start + p * units, units, 1)
-        share = jnp.concatenate([take(expand_weight, 0), take(expand_weight, FF), take(shrink_rows, 0)], axis=1)
-        if k:
-            share = links.send(share, lambda a, c, s: (a, c ^ (k // n_seq), s ^ (k % n_seq)))
-        shares.append((p, share))
-    block = jnp.zeros((plane * rows, 3 * units), bf16)
-    for p, share in shares:
-        block = lax.dynamic_update_slice_in_dim(block, share, p * rows, 0)
-    weights = links.line_gather(block)
 
     half = HEAD_DIM // 2
     frequency = 10000.0 ** (-jnp.arange(half, dtype=f32) / half)
@@ -619,7 +800,9 @@
     feed_result = plane_scatter(result_parts).astype(f32)
     layer_output = (residual + feed_result).astype(bf16)
 
-    mine = add_low(links.line_scatter(share_gradient, add_low))
+    mine = lax.psum_scatter(
+        share_gradient, "dp", scatter_dimension=0, tiled=True, axis_index_groups=lines
+    )
     expand_gradient = jnp.zeros((rows, 2 * FF), f32)
     shrink_gradient = jnp.zeros((rows, FF), f32)
     for k in range(plane):
@@ -683,28 +866,20 @@
 
 
 def solution(mesh):
-    placed = (
-        P("dp", "seq", None),
-        P(AXES, None),
-        P(None, AXES),
-        P(AXES, None),
-        P(None, AXES),
-        P(AXES),
-        P("dp", None),
-        P("dp", "seq", None),
-    )
+    token_spec, row_spec, column_spec = P("dp", "seq", None), P(AXES, None), P(None, AXES)
     return jax.shard_map(
         functools.partial(body, mesh.shape["dp"], mesh.shape["seq"]),
         mesh=mesh,
-        in_specs=placed,
-        out_specs=(
-            P("dp", "seq", None),
-            P("dp", "seq", None),
-            P(AXES, None),
-            P(None, AXES),
-            P(AXES, None),
-            P(None, AXES),
+        in_specs=(
+            token_spec,
+            row_spec,
+            column_spec,
+            row_spec,
+            column_spec,
             P(AXES),
+            P("dp", None),
+            token_spec,
         ),
+        out_specs=(token_spec, token_spec, row_spec, column_spec, row_spec, column_spec, P(AXES)),
         check_vma=False,
     )

time: 1190 us -> 1060 us (0.89)
  waiting for transfers between devices: 455 us -> 291 us
  Pallas kernels: 228 us -> 346 us
  starting transfers between devices: 220 us -> 178 us
  other arithmetic: 109 us -> 75.9 us
  local copies, waits for them, and re-layouts: 112 us -> 98.3 us
    ppermute x100 -> x81, waiting for transfers between devices: 455 us -> 291 us  [send(): return lax.ppermute(values, AXES, pairs)]
    pallas_call x0 -> x2, Pallas kernels: none -> 118 us  [the longest x1 62.3 us: spread_plane(): pl.pallas_call(functools.partial(spread_plane_kernel, n_z, n_seq), in_spe...]
    ppermute x100 -> x81, starting transfers between devices: 219 us -> 178 us  [send(): return lax.ppermute(values, AXES, pairs)]
    convert_element_type x31 -> x27, other arithmetic: 48.1 us -> 26.3 us  [add_low(): functools.reduce(lambda a, b: a + b, [p.astype(f32) for p in parts])]
    unnamed x137 -> x105, local copies, waits for them, and re-layouts: 27.4 us -> 23.3 us
  transfers between devices with their start and end apart: 102 -> 83, of which waited for: 32 -> 35; matrix products, arithmetic and copies ran while one was open for 20% -> 17% of each run, Pallas kernels for 19% -> 28%
where the time goes in v3:
time: 1060 us; the launch traced here: 1050 us
  Pallas kernels  346 us (33%)
  waiting for transfers between devices  291 us (27%)
  starting transfers between devices  178 us (17%)
  local copies, waits for them, and re-layouts  98.3 us (9%)
  other arithmetic  75.9 us (7%)
  matrix products  39.7 us (4%)
  between operations  17.7 us (2%)
    ppermute x81, waiting for transfers between devices, send(): return lax.ppermute(values, AXES, pairs)  291 us
    ppermute x81, starting transfers between devices, send(): return lax.ppermute(values, AXES, pairs)  178 us
    pallas_call x4, Pallas kernels, feed(): pl.pallas_call(feed_kernel, grid=(tokens // tile,), in_specs=[row(D), row...  104 us
    pallas_call x1, Pallas kernels, spread_plane(): pl.pallas_call(functools.partial(spread_plane_kernel, n_z, n_seq), in_spe...  62.3 us
    pallas_call x1, Pallas kernels, first_gather(): pl.pallas_call(functools.partial(first_gather_kernel, n_z, n_seq), in_spe...  55.8 us
    pallas_call x1, Pallas kernels, weight_gradient(): pl.pallas_call(functools.partial(weight_gradient_kernel, count), grid=(D...  50.6 us
    dot_general x6, matrix products, dot(): return lax.dot_general(left, right, dims, preferred_element_type=f32)  39.7 us
    pallas_call x1, Pallas kernels, attend_back(): pl.pallas_call(functools.partial(attend_back_kernel, tq, tk), grid_spec=s...  28 us
  transfers between devices with their start and end apart: 83, of which 35 were waited for; matrix products, arithmetic and copies ran while one was open for 17% of the time, Pallas kernels for 28%

profile of v3, /device:TPU:0, one launch (start us, length us, event | category | flops | bytes accessed | tf_op | source)
XLA Modules:
  0.0 1046.6 jit_solution(14993156997579353239)
XLA Ops:
  26.4 55.8 %first_gather.1 = (bf16[8,64,2304]{2,1,0:T(8,128)(2,1)}, bf16[4,64,2048]{2,1,0:T(8,128)(2,1)}, bf16[4,64,1280]{2,1,0:T(8,128)(2,1)}) custom-call(bf16[8,64,2304]{2,1,0:T(8,128)(2,1)} %reshape.215.shares, bf16[64,2048]{1,0:T(8,128)(2,1)} %pad_maximum_fusion.6.joined, bf16[64,1280]{1,0:T(8,128)(2,1)} %bitcast.159), custom_call_target="tpu_custom_call" | custom-call | tf_op jit(solution)/shard_map/first_gather/pallas_call | solution.py:511
  83.4 62.3 %spread_plane.1 = (bf16[4,8,64,2048]{3,2,1,0:T(8,128)(2,1)}, bf16[4,8,64,1280]{3,2,1,0:T(8,128)(2,1)}) custom-call(bf16[4,64,2048]{2,1,0:T(8,128)(2,1)} %get-tuple-element.34.joined_z, bf16[4,64,1280]{2,1,0:T(8,128)(2,1)} %get-tuple-element.35.out_z), custom_call_target="tpu_custom_call" | custom-call | tf_op jit(solution)/shard_map/spread_plane/pallas_call | solution.py:584
  150.3 9.7 fusion.3.projected
  160.0 12.5 %rope.1.q = bf16[512,1920]{1,0:T(8,128)(2,1)} custom-call(f32[512,1920]{1,0:T(8,128)} %fusion.3.projected, f32[2,128]{1,0:T(2,128)} %pad_maximum_fusion.7.gains, f32[2,512,128]{2,1,0:T(8,128)} %pad_maximum_fusion.4.tables), custom_call_target="tpu_custom_call" | custom-call | flops 39321600 | bytes 5898240 | tf_op jit(solution)/shard_map/rope/pallas_call | solution.py:80
  183.0 10.7 %collective-permute-done = bf16[512,640]{1,0:T(8,128)(2,1)S(1)} collective-permute-done((bf16[512,640]{1,0:T(8,128)(2,1)}, bf16[512,640]{1,0:T(8,128)(2,1)S(1)}, u32[]{:S(2)}, u32[]{:S(2)}) %collective-permute-start) | collective-permute-done | bytes 655392 | tf_op jit(solution)/shard_map/ppermute | solution.py:617
  206.5 18.9 %attend.1 = (f32[512,1280]{1,0:T(8,128)}, bf16[20,512,128]{2,1,0:T(8,128)(2,1)}) custom-call(s32[1]{0:T(128)} %bitcast.1.offset, bf16[512,1920]{1,0:T(8,128)(2,1)} %rope.1.q, bf16[2048,640]{1,0:T(8,128)(2,1)} %constant_dynamic-update-slice_fusion.16.kv, bf16[2048,128]{1,0:T(8,128)(2,1)} %select_convert_fusion.key_marks, ...), custom_call_target="tpu_custom_call" | custom-call | flops 21474836480 | bytes 16777216 | tf_op jit(solution)/shard_map/attend/pallas_call | solution.py:234
  234.2 8.1 collective-permute-start.12
  242.3 14.8 %collective-permute-start.7 = (bf16[512,2048]{1,0:T(8,128)(2,1)}, bf16[512,2048]{1,0:T(8,128)(2,1)}, u32[]{:S(2)}, u32[]{:S(2)}) collective-permute-start(bf16[512,2048]{1,0:T(8,128)(2,1)} %multiply_convert_fusion), channel_id=1, source_target_pairs={{0,2},{1,3},{2,0},{3,1},{4,6},{5,7},{6,4},{7,5},{8,10},{9,11},{10,... | collective-permute-start | bytes 6291464 | tf_op jit(solution)/shard_map/ppermute | solution.py:617
  260.4 26.5 %collective-permute-done.12 = bf16[512,2048]{1,0:T(8,128)(2,1)} collective-permute-done((bf16[512,2048]{1,0:T(8,128)(2,1)}, bf16[512,2048]{1,0:T(8,128)(2,1)}, u32[]{:S(2)}, u32[]{:S(2)}) %collective-permute-start.12) | collective-permute-done | bytes 2097184 | tf_op jit(solution)/shard_map/ppermute | solution.py:617
  291.8 15.2 %collective-permute-start.13 = (bf16[256,2048]{1,0:T(8,128)(2,1)S(1)}, bf16[256,2048]{1,0:T(8,128)(2,1)S(1)}, u32[]{:S(2)}, u32[]{:S(2)}) collective-permute-start(bf16[256,2048]{1,0:T(8,128)(2,1)S(1)} %slice.477), channel_id=1, source_target_pairs={{0,2},{1,3},{2,0},{3,1},{4,6},{5,7},{6,4},{7,5},{8,10},{9,11},{10,... | collective-permute-start | bytes 3145736 | tf_op jit(solution)/shard_map/ppermute | solution.py:617
  328.5 20.0 %collective-permute-done.13 = bf16[256,2048]{1,0:T(8,128)(2,1)S(1)} collective-permute-done((bf16[256,2048]{1,0:T(8,128)(2,1)S(1)}, bf16[256,2048]{1,0:T(8,128)(2,1)S(1)}, u32[]{:S(2)}, u32[]{:S(2)}) %collective-permute-start.13) | collective-permute-done | bytes 1048608 | tf_op jit(solution)/shard_map/ppermute | solution.py:617
  367.0 25.9 %feed.7 = (bf16[1024,768]{1,0:T(8,128)(2,1)}, bf16[1024,1536]{1,0:T(8,128)(2,1)}, bf16[1024,2048]{1,0:T(8,128)(2,1)}, bf16[1024,2048]{1,0:T(8,128)(2,1)}) custom-call(bf16[1024,2048]{1,0:T(8,128)(2,1)} %constant_dynamic-update-slice_fusion.12.normed.refs_1_, bf16[1024,2048]{1,0:T(8,128)(2,1)} %copy-done.25, ...), custom_call_target="tpu_custom_call" | custom-call | flops 32212254720 | bytes 30932992 | tf_op jit(solution)/shard_map/feed/pallas_call | solution.py:362
  398.2 26.0 %feed.6 = (bf16[1024,768]{1,0:T(8,128)(2,1)}, bf16[1024,1536]{1,0:T(8,128)(2,1)}, bf16[1024,2048]{1,0:T(8,128)(2,1)}, bf16[1024,2048]{1,0:T(8,128)(2,1)}) custom-call(bf16[1024,2048]{1,0:T(8,128)(2,1)} %copy-done.29, bf16[1024,2048]{1,0:T(8,128)(2,1)} %copy-done.28, bf16[2048,2304]{1,0:T(8,128)(2,1)} %all-gather.2.cloned.1.call-done.weights), custom_call_target="tpu_custom_call" | custom-call | flops 32212254720 | bytes 30932992 | tf_op jit(solution)/shard_map/feed/pallas_call | solution.py:362
  429.7 25.8 %feed.5 = (bf16[1024,768]{1,0:T(8,128)(2,1)}, bf16[1024,1536]{1,0:T(8,128)(2,1)}, bf16[1024,2048]{1,0:T(8,128)(2,1)}, bf16[1024,2048]{1,0:T(8,128)(2,1)}) custom-call(bf16[1024,2048]{1,0:T(8,128)(2,1)} %copy-done.26, bf16[1024,2048]{1,0:T(8,128)(2,1)} %copy-done.24, bf16[2048,2304]{1,0:T(8,128)(2,1)} %all-gather.2.cloned.1.call-done.weights), custom_call_target="tpu_custom_call" | custom-call | flops 32212254720 | bytes 30932992 | tf_op jit(solution)/shard_map/feed/pallas_call | solution.py:362
  459.0 26.2 %feed.4 = (bf16[1024,768]{1,0:T(8,128)(2,1)}, bf16[1024,1536]{1,0:T(8,128)(2,1)}, bf16[1024,2048]{1,0:T(8,128)(2,1)}, bf16[1024,2048]{1,0:T(8,128)(2,1)}) custom-call(bf16[1024,2048]{1,0:T(8,128)(2,1)} %pad_maximum_fusion.1.normed.refs_0_, bf16[1024,2048]{1,0:T(8,128)(2,1)} %pad_maximum_fusion.2.upstream.refs_4_, ...), custom_call_target="tpu_custom_call" | custom-call | flops 32212254720 | bytes 30932992 | tf_op jit(solution)/shard_map/feed/pallas_call | solution.py:362
  516.2 19.9 %collective-permute-done.40 = bf16[256,2048]{1,0:T(8,128)(2,1)S(1)} collective-permute-done((bf16[256,2048]{1,0:T(8,128)(2,1)S(1)}, bf16[256,2048]{1,0:T(8,128)(2,1)S(1)}, u32[]{:S(2)}, u32[]{:S(2)}) %collective-permute-start.40) | collective-permute-done | bytes 1048608 | tf_op jit(solution)/shard_map/ppermute | solution.py:617
  538.2 13.9 %collective-permute-done.35 = bf16[256,2048]{1,0:T(8,128)(2,1)S(1)} collective-permute-done((bf16[256,2048]{1,0:T(8,128)(2,1)S(1)}, bf16[256,2048]{1,0:T(8,128)(2,1)S(1)}, u32[]{:S(2)}, u32[]{:S(2)}) %collective-permute-start.35) | collective-permute-done | bytes 1048608 | tf_op jit(solution)/shard_map/ppermute | solution.py:617
  560.7 13.9 %collective-permute-done.23 = bf16[256,2048]{1,0:T(8,128)(2,1)S(1)} collective-permute-done((bf16[256,2048]{1,0:T(8,128)(2,1)S(1)}, bf16[256,2048]{1,0:T(8,128)(2,1)S(1)}, u32[]{:S(2)}, u32[]{:S(2)}) %collective-permute-start.23) | collective-permute-done | bytes 1048608 | tf_op jit(solution)/shard_map/ppermute | solution.py:617
  582.1 15.0 %collective-permute-done.41 = bf16[256,2048]{1,0:T(8,128)(2,1)S(1)} collective-permute-done((bf16[256,2048]{1,0:T(8,128)(2,1)S(1)}, bf16[256,2048]{1,0:T(8,128)(2,1)S(1)}, u32[]{:S(2)}, u32[]{:S(2)}) %collective-permute-start.41) | collective-permute-done | bytes 1048608 | tf_op jit(solution)/shard_map/ppermute | solution.py:617
  607.5 12.0 %collective-permute-done.28 = bf16[256,2048]{1,0:T(8,128)(2,1)S(1)} collective-permute-done((bf16[256,2048]{1,0:T(8,128)(2,1)S(1)}, bf16[256,2048]{1,0:T(8,128)(2,1)S(1)}, u32[]{:S(2)}, u32[]{:S(2)}) %collective-permute-start.28) | collective-permute-done | bytes 1048608 | tf_op jit(solution)/shard_map/ppermute | solution.py:617
  626.0 15.4 %collective-permute-done.31 = bf16[256,2048]{1,0:T(8,128)(2,1)S(1)} collective-permute-done((bf16[256,2048]{1,0:T(8,128)(2,1)S(1)}, bf16[256,2048]{1,0:T(8,128)(2,1)S(1)}, u32[]{:S(2)}, u32[]{:S(2)}) %collective-permute-start.31) | collective-permute-done | bytes 1048608 | tf_op jit(solution)/shard_map/ppermute | solution.py:617
  658.0 28.0 %attend_back.1 = (f32[512,1280]{1,0:T(8,128)}, bf16[2048,640]{1,0:T(8,128)(2,1)}) custom-call(s32[1]{0:T(128)} %bitcast.1.offset, bf16[20,512,128]{2,1,0:T(8,128)(2,1)} %get-tuple-element.48.q_marked, bf16[512,1280]{1,0:T(8,128)(2,1)} %convolution_convert_fusion.2.d_out, f32[512,1280]{1,0:T(8,128)} %get-tuple-element.37.out, ...), custom_call_target="tpu_custom_call" | custom-call | flops 42949672960 | bytes 16777216 | tf_op jit(solution)/shard_map/attend_back/pallas_call | solution.py:324
  688.3 17.0 %collective-permute-start.42 = (bf16[256,640]{1,0:T(8,128)(2,1)}, bf16[256,640]{1,0:T(8,128)(2,1)}, u32[]{:S(2)}, u32[]{:S(2)}) collective-permute-start(bf16[256,640]{1,0:T(8,128)(2,1)} %get-tuple-element.81), channel_id=1, source_target_pairs={{0,1},{1,0},{2,3},{3,2},{4,5},{5,4},{6,7},{7,6},{8,9},{9,8},{10,11... | collective-permute-start | bytes 983048 | tf_op jit(solution)/shard_map/ppermute | solution.py:617
  705.2 50.6 %weight_gradient.1 = bf16[2048,2304]{1,0:T(8,128)(2,1)} custom-call(bf16[1024,2048]{1,0:T(8,128)(2,1)} %pad_maximum_fusion.1.normed.refs_0_, bf16[1024,2048]{1,0:T(8,128)(2,1)} %constant_dynamic-update-slice_fusion.12.normed.refs_1_, bf16[1024,2048]{1,0:T(8,128)(2,1)} %copy-done.26, bf16[1024,2048]{1,0:T(8,128)(2,1)} %copy-done.29, ...), custom_call_target="tpu_custom_call" | custom-call | flops 51539607552 | bytes 52428800 | tf_op jit(solution)/shard_map/weight_gradient/pallas_call | solution.py:403
  756.0 32.3 %collective-permute-start.46 = (bf16[256,640]{1,0:T(8,128)(2,1)S(1)}, bf16[256,640]{1,0:T(8,128)(2,1)}, u32[]{:S(2)}, u32[]{:S(2)}) collective-permute-start(bf16[256,640]{1,0:T(8,128)(2,1)S(1)} %get-tuple-element.83), channel_id=1, source_target_pairs={{0,2},{1,3},{2,0},{3,1},{4,6},{5,7},{6,4},{7,5},{8,10},{9,11},{10,... | collective-permute-start | bytes 983048 | tf_op jit(solution)/shard_map/ppermute | solution.py:617
  815.9 14.1 %rope_back.1 = (bf16[512,1920]{1,0:T(8,128)(2,1)}, f32[8,128]{1,0:T(8,128)}) custom-call(f32[512,1280]{1,0:T(8,128)} %get-tuple-element.49.dq, f32[512,640]{1,0:T(8,128)} %maximum_convert_fusion.dkv, f32[512,1920]{1,0:T(8,128)} %fusion.3.projected, f32[2,128]{1,0:T(2,128)} %pad_maximum_fusion.7.gains, f32[2,512,128]{2,1,0:T(8,128)} %pad_maximum_fusion.4.tables), custom_call_target="tpu_custom_call" | custom-call | flops 58982400 | bytes 9830400 | tf_op jit(solution)/shard_map/rope_back/pallas_call | solution.py:120
  831.6 10.6 %fusion.23 = (bf16[2048]{0:T(1024)(128)(2,1)S(1)}, f32[512]{0:T(512)S(1)}, f32[512,2048]{1,0:T(8,128)}) fusion(bf16[1,512,2048]{2,1,0:T(8,128)(2,1)S(1)} %copy-done.8, f32[512]{0:T(512)S(1)} %copy-done.39, f32[2048]{0:T(1024)S(1)} %copy-done.35, bf16[512,1920]{1,0:T(8,128)(2,1)} %get-tuple-element.51, bf16[2048,2048]{1,0:T(8,128)(2,1)} %bitcast.162), kind=kOutput, calls=%fused_computation.36 | convolution fusion | flops 4033869312 | bytes 16138240 | tf_op jit(solution)/shard_map/dot_general | solution.py:36
  853.1 12.6 %copy.46 = bf16[2048,2048]{1,0:T(8,128)(2,1)} copy(bf16[2048,2048]{0,1:T(8,128)(2,1)} %pad_maximum_fusion) | data formatting | bytes 16777216 | tf_op jit(solution)/shard_map/concatenate | solution.py:853
  901.2 8.0 collective-permute-done.53
  1001.6 16.2 %collective-permute-done.74 = bf16[64,2304]{1,0:T(8,128)(2,1)S(1)} collective-permute-done((bf16[64,2304]{1,0:T(8,128)(2,1)S(1)}, bf16[64,2304]{1,0:T(8,128)(2,1)S(1)}, u32[]{:S(2)}, u32[]{:S(2)}) %collective-permute-start.74) | collective-permute-done | bytes 294944 | tf_op jit(solution)/shard_map/ppermute | solution.py:617
  1019.7 7.5 collective-permute-done.75
  1028.6 8.1 collective-permute-done.76
  (423 shorter events, 375.3 us)
Async XLA Ops:
  7.2 359.9 %all-gather.2.cloned.1.call-start = ((), (), s32[]{:S(2)}) async-start(), calls=%async_computation.1 | async-start | bytes 11796480 | tf_op jit(solution)/shard_map/all_gather | solution.py:722
  7.2 249.9 %collective-permute-start.17 = (bf16[512,2048]{1,0:T(8,128)(2,1)}, bf16[512,2048]{1,0:T(8,128)(2,1)}, u32[]{:S(2)}, u32[]{:S(2)}) collective-permute-start(bf16[512,2048]{1,0:T(8,128)(2,1)} %bitcast.145), channel_id=1, source_target_pairs={{0,1},{1,0},{2,3},{3,2},{4,5},{5,4},{6,7},{7,6},{8,9},{9,8},{10,11... | collective-permute-start | bytes 6291464 | tf_op jit(solution)/shard_map/ppermute | solution.py:617
  10.2 248.4 %collective-permute-start.9 = (bf16[512,2048]{1,0:T(8,128)(2,1)}, bf16[512,2048]{1,0:T(8,128)(2,1)}, u32[]{:S(2)}, u32[]{:S(2)}) collective-permute-start(bf16[512,2048]{1,0:T(8,128)(2,1)} %bitcast.146), channel_id=1, source_target_pairs={{0,2},{1,3},{2,0},{3,1},{4,6},{5,7},{6,4},{7,5},{8,10},{9,11},{10,... | collective-permute-start | bytes 6291464 | tf_op jit(solution)/shard_map/ppermute | solution.py:617
  82.3 912.1 %reduce-scatter.2.cloned.1.call-start = ((), (), s32[]{:S(2)}) async-start(), calls=%async_computation.2 | async-start | bytes 11796480 | tf_op jit(solution)/shard_map/reduce_scatter | solution.py:803
  234.2 52.7 %collective-permute-start.12 = (bf16[512,2048]{1,0:T(8,128)(2,1)}, bf16[512,2048]{1,0:T(8,128)(2,1)}, u32[]{:S(2)}, u32[]{:S(2)}) collective-permute-start(bf16[512,2048]{1,0:T(8,128)(2,1)} %multiply_convert_fusion), channel_id=1, source_target_pairs={{0,1},{1,0},{2,3},{3,2},{4,5},{5,4},{6,7},{7,6},{8,9},{9,8},{10,11... | collective-permute-start | bytes 6291464 | tf_op jit(solution)/shard_map/ppermute | solution.py:617
  242.3 49.5 %collective-permute-start.5 = (bf16[512,2048]{1,0:T(8,128)(2,1)S(1)}, bf16[512,2048]{1,0:T(8,128)(2,1)}, u32[]{:S(2)}, u32[]{:S(2)}) collective-permute-start(bf16[512,2048]{1,0:T(8,128)(2,1)S(1)} %bitcast.147), channel_id=1, source_target_pairs={{0,4},{1,5},{2,6},{3,7},{4,0},{5,1},{6,2},{7,3},{8,12},{9,13},{10,... | collective-permute-start | bytes 6291464 | tf_op jit(solution)/shard_map/ppermute | solution.py:617
  242.3 70.7 %collective-permute-start.7 = (bf16[512,2048]{1,0:T(8,128)(2,1)}, bf16[512,2048]{1,0:T(8,128)(2,1)}, u32[]{:S(2)}, u32[]{:S(2)}) collective-permute-start(bf16[512,2048]{1,0:T(8,128)(2,1)} %multiply_convert_fusion), channel_id=1, source_target_pairs={{0,2},{1,3},{2,0},{3,1},{4,6},{5,7},{6,4},{7,5},{8,10},{9,11},{10,... | collective-permute-start | bytes 6291464 | tf_op jit(solution)/shard_map/ppermute | solution.py:617
  257.1 57.2 %collective-permute-start.4 = (bf16[512,2048]{1,0:T(8,128)(2,1)}, bf16[512,2048]{1,0:T(8,128)(2,1)}, u32[]{:S(2)}, u32[]{:S(2)}) collective-permute-start(bf16[512,2048]{1,0:T(8,128)(2,1)} %multiply_convert_fusion), channel_id=1, source_target_pairs={{0,4},{1,5},{2,6},{3,7},{4,0},{5,1},{6,2},{7,3},{8,12},{9,13},{10,... | collective-permute-start | bytes 6291464 | tf_op jit(solution)/shard_map/ppermute | solution.py:617
  258.7 67.6 %collective-permute-start.18 = (bf16[256,2048]{1,0:T(8,128)(2,1)S(1)}, bf16[256,2048]{1,0:T(8,128)(2,1)S(1)}, u32[]{:S(2)}, u32[]{:S(2)}) collective-permute-start(bf16[256,2048]{1,0:T(8,128)(2,1)S(1)} %slice.479), channel_id=1, source_target_pairs={{0,2},{1,3},{2,0},{3,1},{4,6},{5,7},{6,4},{7,5},{8,10},{9,11},{10,... | collective-permute-start | bytes 3145736 | tf_op jit(solution)/shard_map/ppermute | solution.py:617
  286.9 39.4 %collective-permute-start.19 = (bf16[256,2048]{1,0:T(8,128)(2,1)S(1)}, bf16[256,2048]{1,0:T(8,128)(2,1)S(1)}, u32[]{:S(2)}, u32[]{:S(2)}) collective-permute-start(bf16[256,2048]{1,0:T(8,128)(2,1)S(1)} %slice.480), channel_id=1, source_target_pairs={{0,1},{1,0},{2,3},{3,2},{4,5},{5,4},{6,7},{7,6},{8,9},{9,8},{10,11... | collective-permute-start | bytes 3145736 | tf_op jit(solution)/shard_map/ppermute | solution.py:617
  291.8 56.8 %collective-permute-start.13 = (bf16[256,2048]{1,0:T(8,128)(2,1)S(1)}, bf16[256,2048]{1,0:T(8,128)(2,1)S(1)}, u32[]{:S(2)}, u32[]{:S(2)}) collective-permute-start(bf16[256,2048]{1,0:T(8,128)(2,1)S(1)} %slice.477), channel_id=1, source_target_pairs={{0,2},{1,3},{2,0},{3,1},{4,6},{5,7},{6,4},{7,5},{8,10},{9,11},{10,... | collective-permute-start | bytes 3145736 | tf_op jit(solution)/shard_map/ppermute | solution.py:617
  313.0 40.5 %collective-permute-start.10 = (bf16[512,2048]{1,0:T(8,128)(2,1)}, bf16[512,2048]{1,0:T(8,128)(2,1)S(1)}, u32[]{:S(2)}, u32[]{:S(2)}) collective-permute-start(bf16[512,2048]{1,0:T(8,128)(2,1)} %collective-permute-done.9), channel_id=1, source_target_pairs={{0,4},{1,5},{2,6},{3,7},{4,0},{5,1},{6,2},{7,3},{8,12},{9,13},{10,... | collective-permute-start | bytes 6291464 | tf_op jit(solution)/shard_map/ppermute | solution.py:617
  397.7 95.4 %collective-permute-start.37 = (bf16[512,2048]{1,0:T(8,128)(2,1)}, bf16[512,2048]{1,0:T(8,128)(2,1)}, u32[]{:S(2)}, u32[]{:S(2)}) collective-permute-start(bf16[512,2048]{1,0:T(8,128)(2,1)} %slice.396), channel_id=1, source_target_pairs={{0,4},{1,5},{2,6},{3,7},{4,0},{5,1},{6,2},{7,3},{8,12},{9,13},{10,... | collective-permute-start | bytes 6291464 | tf_op jit(solution)/shard_map/ppermute | solution.py:617
  398.1 98.8 %collective-permute-start.27 = (bf16[512,2048]{1,0:T(8,128)(2,1)}, bf16[512,2048]{1,0:T(8,128)(2,1)}, u32[]{:S(2)}, u32[]{:S(2)}) collective-permute-start(bf16[512,2048]{1,0:T(8,128)(2,1)} %slice.380), channel_id=1, source_target_pairs={{0,4},{1,5},{2,6},{3,7},{4,0},{5,1},{6,2},{7,3},{8,12},{9,13},{10,... | collective-permute-start | bytes 6291464 | tf_op jit(solution)/shard_map/ppermute | solution.py:617
  429.1 74.3 %collective-permute-start.34 = (bf16[512,2048]{1,0:T(8,128)(2,1)}, bf16[512,2048]{1,0:T(8,128)(2,1)}, u32[]{:S(2)}, u32[]{:S(2)}) collective-permute-start(bf16[512,2048]{1,0:T(8,128)(2,1)} %slice.393), channel_id=1, source_target_pairs={{0,4},{1,5},{2,6},{3,7},{4,0},{5,1},{6,2},{7,3},{8,12},{9,13},{10,... | collective-permute-start | bytes 6291464 | tf_op jit(solution)/shard_map/ppermute | solution.py:617
  429.5 80.5 %collective-permute-start.22 = (bf16[512,2048]{1,0:T(8,128)(2,1)}, bf16[512,2048]{1,0:T(8,128)(2,1)S(1)}, u32[]{:S(2)}, u32[]{:S(2)}) collective-permute-start(bf16[512,2048]{1,0:T(8,128)(2,1)} %slice.377), channel_id=1, source_target_pairs={{0,4},{1,5},{2,6},{3,7},{4,0},{5,1},{6,2},{7,3},{8,12},{9,13},{10,... | collective-permute-start | bytes 6291464 | tf_op jit(solution)/shard_map/ppermute | solution.py:617
  458.7 41.1 %collective-permute-start.33 = (bf16[512,2048]{1,0:T(8,128)(2,1)}, bf16[512,2048]{1,0:T(8,128)(2,1)}, u32[]{:S(2)}, u32[]{:S(2)}) collective-permute-start(bf16[512,2048]{1,0:T(8,128)(2,1)} %slice.390), channel_id=1, source_target_pairs={{0,4},{1,5},{2,6},{3,7},{4,0},{5,1},{6,2},{7,3},{8,12},{9,13},{10,... | collective-permute-start | bytes 6291464 | tf_op jit(solution)/shard_map/ppermute | solution.py:617
  503.5 72.5 %collective-permute-start.38 = (bf16[256,2048]{1,0:T(8,128)(2,1)}, bf16[256,2048]{1,0:T(8,128)(2,1)}, u32[]{:S(2)}, u32[]{:S(2)}) collective-permute-start(bf16[256,2048]{1,0:T(8,128)(2,1)} %slice.490), channel_id=1, source_target_pairs={{0,1},{1,0},{2,3},{3,2},{4,5},{5,4},{6,7},{7,6},{8,9},{9,8},{10,11... | collective-permute-start | bytes 3145736 | tf_op jit(solution)/shard_map/ppermute | solution.py:617
  507.1 45.1 %collective-permute-start.35 = (bf16[256,2048]{1,0:T(8,128)(2,1)S(1)}, bf16[256,2048]{1,0:T(8,128)(2,1)S(1)}, u32[]{:S(2)}, u32[]{:S(2)}) collective-permute-start(bf16[256,2048]{1,0:T(8,128)(2,1)S(1)} %get-tuple-element.95), channel_id=1, source_target_pairs={{0,1},{1,0},{2,3},{3,2},{4,5},{5,4},{6,7},{7,6},{8,9},{9,8},{10,11... | collective-permute-start | bytes 3145736 | tf_op jit(solution)/shard_map/ppermute | solution.py:617
  512.9 61.7 %collective-permute-start.23 = (bf16[256,2048]{1,0:T(8,128)(2,1)S(1)}, bf16[256,2048]{1,0:T(8,128)(2,1)S(1)}, u32[]{:S(2)}, u32[]{:S(2)}) collective-permute-start(bf16[256,2048]{1,0:T(8,128)(2,1)S(1)} %get-tuple-element.99), channel_id=1, source_target_pairs={{0,1},{1,0},{2,3},{3,2},{4,5},{5,4},{6,7},{7,6},{8,9},{9,8},{10,11... | collective-permute-start | bytes 3145736 | tf_op jit(solution)/shard_map/ppermute | solution.py:617
  514.9 43.6 %collective-permute-start.30 = (bf16[256,2048]{1,0:T(8,128)(2,1)S(1)}, bf16[256,2048]{1,0:T(8,128)(2,1)S(1)}, u32[]{:S(2)}, u32[]{:S(2)}) collective-permute-start(bf16[256,2048]{1,0:T(8,128)(2,1)S(1)} %get-tuple-element.100), channel_id=1, source_target_pairs={{0,2},{1,3},{2,0},{3,1},{4,6},{5,7},{6,4},{7,5},{8,10},{9,11},{10,... | collective-permute-start | bytes 3145736 | tf_op jit(solution)/shard_map/ppermute | solution.py:617
  536.1 44.9 %collective-permute-start.39 = (bf16[256,2048]{1,0:T(8,128)(2,1)S(1)}, bf16[256,2048]{1,0:T(8,128)(2,1)S(1)}, u32[]{:S(2)}, u32[]{:S(2)}) collective-permute-start(bf16[256,2048]{1,0:T(8,128)(2,1)S(1)} %copy-done.27), channel_id=1, source_target_pairs={{0,2},{1,3},{2,0},{3,1},{4,6},{5,7},{6,4},{7,5},{8,10},{9,11},{10,... | collective-permute-start | bytes 3145736 | tf_op jit(solution)/shard_map/ppermute | solution.py:617
  552.1 44.9 %collective-permute-start.41 = (bf16[256,2048]{1,0:T(8,128)(2,1)S(1)}, bf16[256,2048]{1,0:T(8,128)(2,1)S(1)}, u32[]{:S(2)}, u32[]{:S(2)}) collective-permute-start(bf16[256,2048]{1,0:T(8,128)(2,1)S(1)} %add_convert_fusion.10), channel_id=1, source_target_pairs={{0,1},{1,0},{2,3},{3,2},{4,5},{5,4},{6,7},{7,6},{8,9},{9,8},{10,11... | collective-permute-start | bytes 3145736 | tf_op jit(solution)/shard_map/ppermute | solution.py:617
  558.6 44.9 %collective-permute-start.36 = (bf16[256,2048]{1,0:T(8,128)(2,1)S(1)}, bf16[256,2048]{1,0:T(8,128)(2,1)S(1)}, u32[]{:S(2)}, u32[]{:S(2)}) collective-permute-start(bf16[256,2048]{1,0:T(8,128)(2,1)S(1)} %add_convert_fusion.12), channel_id=1, source_target_pairs={{0,2},{1,3},{2,0},{3,1},{4,6},{5,7},{6,4},{7,5},{8,10},{9,11},{10,... | collective-permute-start | bytes 3145736 | tf_op jit(solution)/shard_map/ppermute | solution.py:617
  574.6 44.9 %collective-permute-start.28 = (bf16[256,2048]{1,0:T(8,128)(2,1)S(1)}, bf16[256,2048]{1,0:T(8,128)(2,1)S(1)}, u32[]{:S(2)}, u32[]{:S(2)}) collective-permute-start(bf16[256,2048]{1,0:T(8,128)(2,1)S(1)} %slice.482), channel_id=1, source_target_pairs={{0,1},{1,0},{2,3},{3,2},{4,5},{5,4},{6,7},{7,6},{8,9},{9,8},{10,11... | collective-permute-start | bytes 3145736 | tf_op jit(solution)/shard_map/ppermute | solution.py:617
  576.0 50.0 %collective-permute-start.29 = (bf16[256,2048]{1,0:T(8,128)(2,1)S(1)}, bf16[256,2048]{1,0:T(8,128)(2,1)S(1)}, u32[]{:S(2)}, u32[]{:S(2)}) collective-permute-start(bf16[256,2048]{1,0:T(8,128)(2,1)S(1)} %slice.484), channel_id=1, source_target_pairs={{0,2},{1,3},{2,0},{3,1},{4,6},{5,7},{6,4},{7,5},{8,10},{9,11},{10,... | collective-permute-start | bytes 3145736 | tf_op jit(solution)/shard_map/ppermute | solution.py:617
  581.0 60.3 %collective-permute-start.31 = (bf16[256,2048]{1,0:T(8,128)(2,1)S(1)}, bf16[256,2048]{1,0:T(8,128)(2,1)S(1)}, u32[]{:S(2)}, u32[]{:S(2)}) collective-permute-start(bf16[256,2048]{1,0:T(8,128)(2,1)S(1)} %add_convert_fusion.14), channel_id=1, source_target_pairs={{0,1},{1,0},{2,3},{3,2},{4,5},{5,4},{6,7},{7,6},{8,9},{9,8},{10,11... | collective-permute-start | bytes 3145736 | tf_op jit(solution)/shard_map/ppermute | solution.py:617
  597.1 50.4 %collective-permute-start.24 = (bf16[256,2048]{1,0:T(8,128)(2,1)S(1)}, bf16[256,2048]{1,0:T(8,128)(2,1)S(1)}, u32[]{:S(2)}, u32[]{:S(2)}) collective-permute-start(bf16[256,2048]{1,0:T(8,128)(2,1)S(1)} %add_convert_fusion.16), channel_id=1, source_target_pairs={{0,2},{1,3},{2,0},{3,1},{4,6},{5,7},{6,4},{7,5},{8,10},{9,11},{10,... | collective-permute-start | bytes 3145736 | tf_op jit(solution)/shard_map/ppermute | solution.py:617
  688.3 100.1 %collective-permute-start.42 = (bf16[256,640]{1,0:T(8,128)(2,1)}, bf16[256,640]{1,0:T(8,128)(2,1)}, u32[]{:S(2)}, u32[]{:S(2)}) collective-permute-start(bf16[256,640]{1,0:T(8,128)(2,1)} %get-tuple-element.81), channel_id=1, source_target_pairs={{0,1},{1,0},{2,3},{3,2},{4,5},{5,4},{6,7},{7,6},{8,9},{9,8},{10,11... | collective-permute-start | bytes 983048 | tf_op jit(solution)/shard_map/ppermute | solution.py:617
  756.0 41.1 %collective-permute-start.46 = (bf16[256,640]{1,0:T(8,128)(2,1)S(1)}, bf16[256,640]{1,0:T(8,128)(2,1)}, u32[]{:S(2)}, u32[]{:S(2)}) collective-permute-start(bf16[256,640]{1,0:T(8,128)(2,1)S(1)} %get-tuple-element.83), channel_id=1, source_target_pairs={{0,2},{1,3},{2,0},{3,1},{4,6},{5,7},{6,4},{7,5},{8,10},{9,11},{10,... | collective-permute-start | bytes 983048 | tf_op jit(solution)/shard_map/ppermute | solution.py:617
  996.1 41.1 %collective-permute-start.80 = (bf16[64,2304]{1,0:T(8,128)(2,1)S(1)}, bf16[64,2304]{1,0:T(8,128)(2,1)S(1)}, u32[]{:S(2)}, u32[]{:S(2)}) collective-permute-start(bf16[64,2304]{1,0:T(8,128)(2,1)S(1)} %get-tuple-element.85), channel_id=1, source_target_pairs={{0,7},{1,6},{2,5},{3,4},{4,3},{5,2},{6,1},{7,0},{8,15},{9,14},{10,... | collective-permute-start | bytes 884744 | tf_op jit(solution)/shard_map/ppermute | solution.py:617
  996.2 40.9 %collective-permute-start.79 = (bf16[64,2304]{1,0:T(8,128)(2,1)S(1)}, bf16[64,2304]{1,0:T(8,128)(2,1)S(1)}, u32[]{:S(2)}, u32[]{:S(2)}) collective-permute-start(bf16[64,2304]{1,0:T(8,128)(2,1)S(1)} %get-tuple-element.86), channel_id=1, source_target_pairs={{0,6},{1,7},{2,4},{3,5},{4,2},{5,3},{6,0},{7,1},{8,14},{9,15},{10,... | collective-permute-start | bytes 884744 | tf_op jit(solution)/shard_map/ppermute | solution.py:617
  (98 other events, 1530.8 us)
Sparse Core Ops, SparseCore 0:
  82.4 167.6 all-gather.1
  756.0 192.3 reduce-scatter.1

commit v4 on v3

--- a/solution.py
+++ b/solution.py
@@ -63,48 +63,58 @@
     return jnp.where(low, left, right) * (1.0 / HEAD_DIM)
 
 
-def rope_kernel(query_pairs, projected, gains, tables, out):
-    step = pl.program_id(0)
-    is_query = step < query_pairs
-    values = projected[...]
-    plain = (lanes(values.shape) >= HEAD_DIM) & jnp.logical_not(is_query)
-    gain = jnp.where(is_query, gains[0:1], gains[1:2])
-    normed = values * lax.rsqrt(head_means(values * values) + epsilon) * gain
-    turned = normed * tables[0] + swap_halves(normed) * tables[1]
-    turned = turned * jnp.where(is_query, HEAD_DIM**-0.5, 1.0)
-    out[...] = jnp.where(plain, values, turned).astype(bf16)
+BAND = 2 * KV_WIDTH
+QUERY_BANDS = Q_WIDTH // BAND
+
+
+def rope_kernel(projected, gains, tables, out):
+    is_query = pl.program_id(0) < QUERY_BANDS
+    gain = jnp.where(is_query, gains[0:1] * HEAD_DIM**-0.5, gains[1:2])
+    direct, crossed = tables[0] * gain, tables[1]
+    for start in range(0, BAND, PAIR):
+        columns = slice(start, start + PAIR)
+        values = projected[:, columns]
+        scaling = lax.rsqrt(head_means(values * values) + epsilon)
+        turned = values * direct + swap_halves(values * gain) * crossed
+        plain = (lanes(values.shape) >= HEAD_DIM) & jnp.logical_not(is_query)
+        out[:, columns] = jnp.where(plain, values, turned * scaling).astype(bf16)
 
 
 def rope(projected, gains, tables):
     tokens, width = projected.shape
     return pl.pallas_call(
-        functools.partial(rope_kernel, Q_WIDTH // PAIR),
-        grid=(width // PAIR,),
+        rope_kernel,
+        grid=(width // BAND,),
         in_specs=[
-            pl.BlockSpec((tokens, PAIR), lambda i: (0, i)),
+            pl.BlockSpec((tokens, BAND), lambda i: (0, i)),
             pl.BlockSpec((2, PAIR), lambda i: (0, 0)),
             pl.BlockSpec((2, tokens, PAIR), lambda i: (0, 0, 0)),
         ],
-        out_specs=pl.BlockSpec((tokens, PAIR), lambda i: (0, i)),
+        out_specs=pl.BlockSpec((tokens, BAND), lambda i: (0, i)),
         out_shape=jax.ShapeDtypeStruct((tokens, width), bf16),
+        compiler_params=pltpu.CompilerParams(vmem_limit_bytes=40 << 20),
         cost_estimate=pl.CostEstimate(flops=40 * tokens * width, bytes_accessed=6 * tokens * width, transcendentals=0),
         name="rope",
     )(projected, gains, tables)
 
 
-def rope_back_kernel(query_pairs, dq, dkv, projected, gains, tables, out, gain_sums):
+def rope_back_kernel(dq, dkv, projected, gains, tables, out, gain_sums):
     step = pl.program_id(0)
-    is_query = step < query_pairs
-    values = projected[...]
-    upstream = jnp.where(is_query, dq[...] * HEAD_DIM**-0.5, dkv[...])
-    plain = (lanes(values.shape) >= HEAD_DIM) & jnp.logical_not(is_query)
+    is_query = step < QUERY_BANDS
     gain = jnp.where(is_query, gains[0:1], gains[1:2])
-    turned = upstream * tables[0] + swap_halves(upstream * tables[1])
-    scaling = lax.rsqrt(head_means(values * values) + epsilon)
-    weighted = turned * gain
-    back = scaling * weighted - values * (scaling * scaling * scaling) * head_means(weighted * values)
-    out[...] = jnp.where(plain, upstream, back).astype(bf16)
-    sums = jnp.sum(jnp.where(plain, 0.0, turned * values * scaling), axis=0, keepdims=True)
+    sums = jnp.zeros((1, PAIR), f32)
+    for start in range(0, BAND, PAIR):
+        columns = slice(start, start + PAIR)
+        values = projected[:, columns]
+        upstream = jnp.where(is_query, dq[:, columns] * HEAD_DIM**-0.5, dkv[:, columns].astype(f32))
+        plain = (lanes(values.shape) >= HEAD_DIM) & jnp.logical_not(is_query)
+        turned = upstream * tables[0] + swap_halves(upstream * tables[1])
+        scaling = lax.rsqrt(head_means(values * values) + epsilon)
+        unit = values * scaling
+        weighted = turned * gain
+        back = scaling * (weighted - unit * head_means(weighted * unit))
+        out[:, columns] = jnp.where(plain, upstream, back).astype(bf16)
+        sums = sums + jnp.sum(jnp.where(plain, 0.0, turned * unit), axis=0, keepdims=True)
 
     @pl.when(step == 0)
     def _():
@@ -116,25 +126,25 @@
 
 def rope_back(dq, dkv, projected, gains, tables):
     tokens, width = projected.shape
-    query_pairs = Q_WIDTH // PAIR
     return pl.pallas_call(
-        functools.partial(rope_back_kernel, query_pairs),
-        grid=(width // PAIR,),
+        rope_back_kernel,
+        grid=(width // BAND,),
         in_specs=[
-            pl.BlockSpec((tokens, PAIR), lambda i: (0, jnp.minimum(i, query_pairs - 1))),
-            pl.BlockSpec((tokens, PAIR), lambda i: (0, jnp.maximum(i - query_pairs, 0))),
-            pl.BlockSpec((tokens, PAIR), lambda i: (0, i)),
+            pl.BlockSpec((tokens, BAND), lambda i: (0, jnp.minimum(i, QUERY_BANDS - 1))),
+            pl.BlockSpec((tokens, BAND), lambda i: (0, 0)),
+            pl.BlockSpec((tokens, BAND), lambda i: (0, i)),
             pl.BlockSpec((2, PAIR), lambda i: (0, 0)),
             pl.BlockSpec((2, tokens, PAIR), lambda i: (0, 0, 0)),
         ],
         out_specs=[
-            pl.BlockSpec((tokens, PAIR), lambda i: (0, i)),
+            pl.BlockSpec((tokens, BAND), lambda i: (0, i)),
             pl.BlockSpec((8, PAIR), lambda i: (0, 0)),
         ],
         out_shape=[
             jax.ShapeDtypeStruct((tokens, width), bf16),
             jax.ShapeDtypeStruct((8, PAIR), f32),
         ],
+        compiler_params=pltpu.CompilerParams(vmem_limit_bytes=40 << 20),
         cost_estimate=pl.CostEstimate(flops=60 * tokens * width, bytes_accessed=10 * tokens * width, transcendentals=0),
         name="rope_back",
     )(dq, dkv, projected, gains, tables)
@@ -332,86 +342,6 @@
         cost_estimate=attention_cost(tokens, 4),
         name="attend_back",
     )(offset, q_marked, d_out, out, kv, key_marks)
-
-
-def feed_kernel(normed, upstream, weights, hidden, both, result, back):
-    units = hidden.shape[1]
-    values = normed[...]
-    gate = dot(values, weights[:, :units], NN)
-    up = dot(values, weights[:, units : 2 * units], NN)
-    d_hidden = dot(upstream[...], weights[:, 2 * units :], NN)
-    sigmoid = 1.0 / (1.0 + jnp.exp(-gate))
-    silu = gate * sigmoid
-    low = (silu * up).astype(bf16)
-    hidden[...] = low
-    result[...] = dot(low, weights[:, 2 * units :], NT).astype(bf16)
-    d_gate = (d_hidden * up * sigmoid * (1.0 + gate * (1.0 - sigmoid))).astype(bf16)
-    d_up = (d_hidden * silu).astype(bf16)
-    both[:, :units] = d_gate
-    both[:, units:] = d_up
-    d_normed = dot(d_gate, weights[:, :units], NT) + dot(d_up, weights[:, units : 2 * units], NT)
-    back[...] = d_normed.astype(bf16)
-
-
-def feed(normed, upstream, weights):
-    tokens = normed.shape[0]
-    units = weights.shape[1] // 3
-    tile = 256
-    row = lambda n: pl.BlockSpec((tile, n), lambda i: (i, 0))
-    out = lambda n: jax.ShapeDtypeStruct((tokens, n), bf16)
-    return pl.pallas_call(
-        feed_kernel,
-        grid=(tokens // tile,),
-        in_specs=[
-            row(D),
-            row(D),
-            pl.BlockSpec(weights.shape, lambda i: (0, 0), pipeline_mode=pl.Buffered(1)),
-        ],
-        out_specs=[row(units), row(2 * units), row(D), row(D)],
-        out_shape=[out(units), out(2 * units), out(D), out(D)],
-        compiler_params=pltpu.CompilerParams(vmem_limit_bytes=56 << 20),
-        cost_estimate=pl.CostEstimate(
-            flops=20 * tokens * D * units,
-            bytes_accessed=2 * (3 * D * units + tokens * (4 * D + 3 * units)),
-            transcendentals=tokens * units,
-        ),
-        name="feed",
-    )(normed, upstream, weights)
-
-
-def weight_gradient_kernel(count, *refs):
-    normed, upstream, both, hidden = (refs[i * count : (i + 1) * count] for i in range(4))
-    out = refs[-1]
-    units = hidden[0].shape[1]
-    expand = shrink = None
-    for j in range(count):
-        one = dot(normed[j][...], both[j][...], TN)
-        two = dot(upstream[j][...], hidden[j][...], TN)
-        expand = one if expand is None else expand + one
-        shrink = two if shrink is None else shrink + two
-    out[:, : 2 * units] = expand.astype(bf16)
-    out[:, 2 * units :] = shrink.astype(bf16)
-
-
-def weight_gradient(normed, upstream, both, hidden):
-    count = len(normed)
-    units = hidden[0].shape[1]
-    tile = 256
-    columns = [pl.BlockSpec((a.shape[0], tile), lambda i: (0, i)) for a in normed]
-    whole = lambda xs: [pl.BlockSpec(a.shape, lambda i: (0, 0), pipeline_mode=pl.Buffered(1)) for a in xs]
-    tokens = sum(a.shape[0] for a in normed)
-    return pl.pallas_call(
-        functools.partial(weight_gradient_kernel, count),
-        grid=(D // tile,),
-        in_specs=columns + columns + whole(both) + whole(hidden),
-        out_specs=pl.BlockSpec((tile, 3 * units), lambda i: (i, 0)),
-        out_shape=jax.ShapeDtypeStruct((D, 3 * units), bf16),
-        compiler_params=pltpu.CompilerParams(vmem_limit_bytes=60 << 20),
-        cost_estimate=pl.CostEstimate(
-            flops=8 * tokens * D * units, bytes_accessed=2 * tokens * (2 * D + 3 * units), transcendentals=0
-        ),
-        name="weight_gradient",
-    )(*normed, *upstream, *both, *hidden)
 
 
 def coordinates():
@@ -596,6 +526,354 @@
     )(joined_z, out_z)
 
 
+TILE = 256
+
+
+def chunk_of(q):
+    k = q // 2
+    return k, jnp.where(k == 0, q % 2, 1 - q % 2)
+
+
+def feed_plane_kernel(n_seq, near_count, *refs):
+    near = refs[:near_count]
+    normed, weights, n_all, d_all, y_own, y_core, back, gradient, arrived = refs[near_count : near_count + 9]
+    scratch = refs[near_count + 9 :]
+    (w, hidden, both, core_sum, own_back, t_in, n_tile, d_tile, core_out, y_out, g_out) = scratch[:11]
+    (local, tile_sem, y_sem, g_sem, n_send, n_recv, d_send, d_recv, c_send, c_recv, yc_send, yc_recv, r_send, r_recv) = scratch[11:]
+    z, c, s = coordinates()
+    length = normed.shape[0]
+    units = hidden.shape[1]
+    steps = length // TILE
+    chunks = CORES * n_seq
+    folded = (n_seq, steps) == (4, 2)
+    core_peer = (z, 1 - c, s)
+    peer = lambda k: (z, c, s ^ k)
+    neighbours = [1, 2] if folded else list(range(1, n_seq))
+    greet([peer(k) for k in neighbours] + [core_peer], [])
+    mine = lambda k: 0 if k == 0 else 2 * k + 1
+    cross = lambda k: 1 if k == 0 else 2 * k
+
+    w_copy = pltpu.make_async_copy(weights, w.at[:, : 3 * units], local.at[0])
+    w_copy.start()
+    n_here = [(0, normed)]
+    d_here = [(mine(k), near[i]) for i, k in enumerate([0] + neighbours)]
+
+    def lies(here, gathered, index):
+        for place, ref in here:
+            if place == index:
+                return ref
+        return gathered.at[index]
+
+    n_sems, d_sems = (n_send, n_recv), (d_send, d_recv)
+    n_core = [remote(normed, n_all.at[1], n_sems, 0, core_peer)]
+    d_core = [remote(near[i], d_all.at[cross(k)], d_sems, i, core_peer) for i, k in enumerate([0] + neighbours)]
+    n_direct = [remote(normed, n_all.at[mine(k)], n_sems, 1 + i, peer(k)) for i, k in enumerate(neighbours)]
+    for copy in n_core + n_direct + d_core:
+        copy.start()
+    base = 1 + len(neighbours)
+    n_core += [remote(n_all.at[mine(k)], n_all.at[cross(k)], n_sems, base + i, core_peer) for i, k in enumerate(neighbours)]
+    base_n, base_d = 2 * len(neighbours) + 1, 1 + len(neighbours)
+    if folded:
+        top, bottom = pl.ds(0, TILE), pl.ds(TILE, TILE)
+        diag = lambda ref, half: ref.at[mine(3), half]
+        n_fold = [
+            remote(n_all.at[mine(1), top], diag(n_all, top), n_sems, base_n, peer(2)),
+            remote(n_all.at[mine(2), bottom], diag(n_all, bottom), n_sems, base_n + 1, peer(1)),
+        ]
+        d_fold = [
+            remote(near[1].at[top], diag(d_all, top), d_sems, base_d, peer(2)),
+            remote(near[2].at[bottom], diag(d_all, bottom), d_sems, base_d + 1, peer(1)),
+        ]
+        n_core.append(remote(n_all.at[mine(3)], n_all.at[cross(3)], n_sems, base_n + 2, core_peer))
+        d_core.append(remote(d_all.at[mine(3)], d_all.at[cross(3)], d_sems, base_d + 2, core_peer))
+
+    def chunk_ready(q):
+        @pl.when(q == 1)
+        def _():
+            n_core[0].wait_recv()
+            d_core[0].wait_recv()
+
+        @pl.when(q == 2)
+        def _():
+            for i, copy in enumerate(n_direct):
+                copy.wait_recv()
+                n_core[1 + i].start()
+                if folded:
+                    n_fold[i].start()
+            if folded:
+                for copy in d_fold:
+                    copy.start()
+
+        for i, k in enumerate(neighbours):
+
+            pl.when(q == cross(k))(n_core[1 + i].wait_recv)
+            pl.when(q == cross(k))(d_core[1 + i].wait_recv)
+
+        if folded:
+
+            @pl.when(q == cross(3))
+            def _():
+                for copy in n_fold + d_fold:
+                    copy.wait_recv()
+                n_core[3].start()
+                d_core[3].start()
+                n_core[3].wait_recv()
+                d_core[3].wait_recv()
+
+    def tile_copies(t, step_of):
+        q, h = t // steps, t % steps
+        rows = pl.ds(pl.multiple_of(h * TILE, TILE), TILE)
+        for a, (here, gathered, tile) in enumerate(((n_here, n_all, n_tile), (d_here, d_all, d_tile))):
+            copy = lambda source: pltpu.make_async_copy(source, tile.at[t % 2], tile_sem.at[a, t % 2])
+            elsewhere = True
+            for index, ref in here:
+                pl.when(q == index)(lambda: step_of(copy(ref.at[rows])))
+                elsewhere = elsewhere & (q != index)
+            pl.when(elsewhere)(lambda: step_of(copy(gathered.at[q, rows])))
+
+    def begin(copy):
+        copy.start()
+
+    def finish(copy):
+        copy.wait()
+
+    def core_copy(k, h):
+        return remote(core_out.at[h], core_sum.at[k, h], (c_send.at[k], c_recv.at[k]), h, core_peer)
+
+    def y_local(k, h):
+        rows = pl.ds(pl.multiple_of(h * TILE, TILE), TILE)
+        return pltpu.make_async_copy(y_out.at[h], y_own.at[k, rows], y_sem.at[h])
+
+    def y_remote(k, h):
+        rows = pl.ds(pl.multiple_of(h * TILE, TILE), TILE)
+        return remote(y_out.at[h], y_core.at[k, rows], (yc_send.at[k], yc_recv.at[k]), h, core_peer)
+
+    ends = (r_send, r_recv)
+
+    def to_peer(k, h):
+        if (folded, k) == (True, 3):
+            return remote(core_sum.at[3, h], t_in.at[h], ends, h, peer(1 + h))
+        slot = (2 if folded else 0) + (k - 1) * steps + h
+        return remote(core_sum.at[k, h], arrived.at[k - 1, h], ends, slot, peer(k))
+
+    late = [(2, 0), (1, 1)] if folded else []
+    prompt = [(k, h) for k in range(1, n_seq) for h in range(steps)]
+    for pair in late:
+        prompt.remove(pair)
+
+    tile_copies(jnp.int32(0), begin)
+    w_copy.wait()
+
+    def tile_step(t, _):
+        q, h = t // steps, t % steps
+        k, other = chunk_of(q)
+        slot = t % 2
+        tile_copies(t, finish)
+        values = n_tile[slot]
+        gate = dot(values, w[:, :units], NN)
+        up = dot(values, w[:, units : 2 * units], NN)
+        d_hidden = dot(d_tile[slot], w[:, 2 * units : 3 * units], NN)
+        sigmoid = 1.0 / (1.0 + jnp.exp(-gate))
+        silu = gate * sigmoid
+        low = (silu * up).astype(bf16)
+        d_gate = (d_hidden * up * sigmoid * (1.0 + gate * (1.0 - sigmoid))).astype(bf16)
+        d_up = (d_hidden * silu).astype(bf16)
+        rows = pl.ds(pl.multiple_of(t * TILE, TILE), TILE)
+        hidden[rows] = low
+        both[rows, :units] = d_gate
+        both[rows, units:] = d_up
+
+        @pl.when(t + 1 < chunks * steps)
+        def _():
+            pl.when((t + 1) % steps == 0)(lambda: chunk_ready((t + 1) // steps))
+            tile_copies(t + 1, begin)
+
+        result = dot(low, w[:, 2 * units : 3 * units], NT).astype(bf16)
+        before = q - 1
+        k_before, other_before = chunk_of(jnp.maximum(before, 0))
+        pl.when((before >= 0) & (other_before == 0))(lambda: y_local(k_before, h).wait())
+        pl.when((before >= 0) & (other_before == 1))(lambda: y_remote(k_before, h).wait_send())
+        y_out[h] = result
+        pl.when(other == 0)(lambda: y_local(k, h).start())
+        pl.when(other == 1)(lambda: y_remote(k, h).start())
+
+        part = dot(d_gate, w[:, :units], NT) + dot(d_up, w[:, units : 2 * units], NT)
+
+        @pl.when(q == 0)
+        def _():
+            own_back[h] = part.astype(bf16)
+
+        @pl.when(other == 1)
+        def _():
+            pl.when(k > 0)(lambda: core_copy(k - 1, h).wait_send())
+            core_out[h] = part.astype(bf16)
+            core_copy(k, h).start()
+
+        @pl.when((other == 0) & (k > 0))
+        def _():
+            core_copy(k, h).wait_recv()
+            core_sum[k, h] = (part + core_sum[k, h].astype(f32)).astype(bf16)
+            for key, half in prompt:
+                pl.when((k == key) & (h == half))(to_peer(key, half).start)
+
+        return 0
+
+    lax.fori_loop(0, chunks * steps, tile_step, 0)
+
+    blocks = chunks * length // D
+    width = blocks * TILE
+
+    def column_copies(j):
+        slot = j % 2
+        columns = pl.ds(pl.multiple_of(j * TILE, TILE), TILE)
+        copies = []
+        for a, (here, gathered) in enumerate(((n_here, n_all), (d_here, d_all))):
+            for b in range(blocks):
+                for q in range(D // length):
+                    first = pl.multiple_of((slot * 2 + a) * width + b * TILE, TILE)
+                    target = w.at[pl.ds(q * length, length), pl.ds(first, TILE)]
+                    index = b * (D // length) + q
+                    source = lies(here, gathered, index)
+                    copies.append((source.at[:, columns], target, (slot, a * blocks + b, q)))
+        return [pltpu.make_async_copy(x, y, g_sem.at[i]) for x, y, i in copies]
+
+    def g_store(j):
+        rows = pl.ds(pl.multiple_of(j * TILE, TILE), TILE)
+        return pltpu.make_async_copy(g_out.at[j % 2], gradient.at[rows], local.at[j % 2])
+
+    for copy in column_copies(0):
+        copy.start()
+
+    def column_step(j, _):
+        slot = j % 2
+
+        @pl.when(j + 1 < D // TILE)
+        def _():
+            for copy in column_copies(j + 1):
+                copy.start()
+
+        for copy in column_copies(j):
+            copy.wait()
+        pl.when(j >= 2)(lambda: g_store(j - 2).wait())
+        expand = shrink = None
+        for b in range(blocks):
+            rows = slice(b * D, (b + 1) * D)
+            at = lambda a: pl.ds(pl.multiple_of((slot * 2 + a) * width + b * TILE, TILE), TILE)
+            one = dot(w[:, at(0)], both[rows], TN)
+            two = dot(w[:, at(1)], hidden[rows], TN)
+            expand = one if expand is None else expand + one
+            shrink = two if shrink is None else shrink + two
+        g_out[slot, :, : 2 * units] = expand.astype(bf16)
+        g_out[slot, :, 2 * units :] = shrink.astype(bf16)
+        g_store(j).start()
+        if folded:
+
+            @pl.when(j == 3)
+            def _():
+                for i, (key, half) in enumerate(late):
+                    to_peer(3, i).wait_recv()
+                    total = core_sum[key, half].astype(f32) + t_in[i].astype(f32)
+                    core_sum[key, half] = total.astype(bf16)
+                    to_peer(key, half).start()
+
+        return 0
+
+    lax.fori_loop(0, D // TILE, column_step, 0)
+    for j in (D // TILE - 2, D // TILE - 1):
+        g_store(j).wait()
+
+    for h in range(steps):
+        core_copy(0, h).wait_recv()
+        held = own_back[h].astype(f32) + core_sum[0, h].astype(f32)
+        for i, key in enumerate(neighbours):
+            to_peer(key, h).wait_recv()
+            incoming = pltpu.make_async_copy(arrived.at[i, h], n_tile.at[i % 2], tile_sem.at[0, i % 2])
+            incoming.start()
+            incoming.wait()
+            held = held + n_tile[i % 2].astype(f32)
+        d_tile[h % 2] = held.astype(bf16)
+        out = pltpu.make_async_copy(d_tile.at[h % 2], back.at[pl.ds(h * TILE, TILE)], tile_sem.at[1, h % 2])
+        out.start()
+        out.wait()
+
+    for copy in n_direct + n_core + d_core:
+        copy.wait_send()
+    if folded:
+        for copy in n_fold + d_fold:
+            copy.wait_send()
+    for key, half in prompt + late:
+        to_peer(key, half).wait_send()
+    for h in range(steps):
+        core_copy(n_seq - 1, h).wait_send()
+        y_local(n_seq - 1, h).wait()
+        for k in range(n_seq):
+            y_remote(k, h).wait_recv()
+
+
+def feed_plane(n_seq, normed, upstream, weights):
+    length = normed.shape[0]
+    units = weights.shape[1] // 3
+    steps = length // TILE
+    chunks = CORES * n_seq
+    tokens = chunks * length
+    near = len(upstream)
+    count = near - 1
+    copies = 2 * count + 5
+    w_columns = 3 * units if 3 * units > 4 * TILE * tokens // D else 4 * TILE * tokens // D
+    sums = 2 + near * steps
+    shape = lambda *dims: jax.ShapeDtypeStruct(dims, bf16)
+
+    outs = pl.pallas_call(
+        functools.partial(feed_plane_kernel, n_seq, near),
+        in_specs=[ANY] * (near + 2),
+        out_specs=[ANY] * 7,
+        out_shape=[
+            shape(chunks, length, D),
+            shape(chunks, length, D),
+            shape(n_seq, length, D),
+            shape(n_seq, length, D),
+            shape(length, D),
+            shape(D, 3 * units),
+            shape(count, steps, TILE, D),
+        ],
+        scratch_shapes=[
+            pltpu.VMEM((D, w_columns), bf16),
+            pltpu.VMEM((tokens, units), bf16),
+            pltpu.VMEM((tokens, 2 * units), bf16),
+            pltpu.VMEM((n_seq, steps, TILE, D), bf16),
+            pltpu.VMEM((steps, TILE, D), bf16),
+            pltpu.VMEM((2, TILE, D), bf16),
+            pltpu.VMEM((2, TILE, D), bf16),
+            pltpu.VMEM((2, TILE, D), bf16),
+            pltpu.VMEM((steps, TILE, D), bf16),
+            pltpu.VMEM((steps, TILE, D), bf16),
+            pltpu.VMEM((2, TILE, 3 * units), bf16),
+            pltpu.SemaphoreType.DMA((near + 3,)),
+            pltpu.SemaphoreType.DMA((2, 2)),
+            pltpu.SemaphoreType.DMA((steps,)),
+            pltpu.SemaphoreType.DMA((2, 2 * tokens // D, D // length)),
+            pltpu.SemaphoreType.DMA((copies,)),
+            pltpu.SemaphoreType.DMA((copies,)),
+            pltpu.SemaphoreType.DMA((copies,)),
+            pltpu.SemaphoreType.DMA((copies,)),
+            pltpu.SemaphoreType.DMA((n_seq, steps)),
+            pltpu.SemaphoreType.DMA((n_seq, steps)),
+            pltpu.SemaphoreType.DMA((n_seq, steps)),
+            pltpu.SemaphoreType.DMA((n_seq, steps)),
+            pltpu.SemaphoreType.DMA((sums,)),
+            pltpu.SemaphoreType.DMA((sums,)),
+        ],
+        compiler_params=pltpu.CompilerParams(
+            collective_id=2, has_side_effects=True, vmem_limit_bytes=60 << 20
+        ),
+        cost_estimate=pl.CostEstimate(
+            flops=20 * tokens * D * units, bytes_accessed=12 * tokens * D, transcendentals=tokens * units
+        ),
+        name="feed_plane",
+    )(*upstream, normed, weights)
+    return outs[2:6]
+
+
 class Links:
     def __init__(self, n_dp, n_seq):
         self.n_z = n_dp // CORES
@@ -646,20 +924,6 @@
         two = [self.peer(add([parts[2][:half], top]), 2), self.peer(parts[2][half:], 2)]
         one = [self.peer(parts[1][:half], 1), self.peer(add([parts[1][half:], bottom]), 1)]
         return [add([parts[0][:half], two[0], one[0]]), add([parts[0][half:], two[1], one[1]])]
-
-    def line_gather(self, values):
-        n = self.n_z
-        z, _, _ = self.place()
-        rows = values.shape[0]
-        ups, downs = [values], [values]
-        for k in range(1, n):
-            ups.append(self.up(ups[-1], k - 1, n - 2))
-            downs.append(self.down(downs[-1], 1, n - k))
-        full = lax.dynamic_update_slice_in_dim(jnp.zeros((n * rows, values.shape[1]), values.dtype), values, z * rows, 0)
-        for r in range(1, n):
-            piece = jnp.where(z + r < n, downs[r], ups[n - r])
-            full = lax.dynamic_update_slice_in_dim(full, piece, ((z + r) % n) * rows, 0)
-        return full
 
     def line_scatter(self, full, add):
         n = self.n_z
@@ -772,34 +1036,12 @@
     scale_two = rms_scale(residual)
     normed_two = (residual * scale_two * gain_two).astype(bf16)
 
-    def plane_gather(values):
-        groups = []
-        for parts in links.seq_gather(values):
-            parts = parts + [links.core(p) for p in parts]
-            groups.append(jnp.concatenate(parts, axis=0))
-        return groups
-
     upstream_low = cotangent.reshape(local_len, D)
-    upstream_all = plane_gather(upstream_low)
-    normed_all = plane_gather(normed_two)
-    hidden_all, both_all, result_parts, back_parts = [], [], [], []
-    for values, above in zip(normed_all, upstream_all):
-        hidden, both, result, back = feed(values, above, weights)
-        hidden_all.append(hidden)
-        both_all.append(both)
-        result_parts.append(result)
-        back_parts.append(back)
-
-    def plane_scatter(parts):
-        parts = [add_low([p[:local_len], links.core(p[local_len:])]) for p in parts]
-        out = links.seq_scatter(parts, add_low)
-        return jnp.concatenate(out, axis=0) if isinstance(out, list) else out
-
-    grad_normed_two = plane_scatter(back_parts).astype(f32)
-    share_gradient = weight_gradient(normed_all, upstream_all, both_all, hidden_all)
-    feed_result = plane_scatter(result_parts).astype(f32)
-    layer_output = (residual + feed_result).astype(bf16)
-
+    early, _ = lax.optimization_barrier((upstream_low, kv))
+    near = [1, 2] if (n_seq, local_len) == (4, 2 * TILE) else list(range(1, n_seq))
+    upstream_near = [upstream_low] + [links.peer(early, k) for k in near]
+    y_own, y_core, back, share_gradient = feed_plane(n_seq, normed_two, upstream_near, weights)
+    grad_normed_two = back.astype(f32)
     mine = lax.psum_scatter(
         share_gradient, "dp", scatter_dimension=0, tiled=True, axis_index_groups=lines
     )
@@ -823,11 +1065,15 @@
     grad_attn_low = grad_residual.astype(bf16)
     output_term = dot(grad_attn_low, attended_low, TN).astype(bf16)
     grad_out_low = dot(grad_attn_low, output_all, NN).astype(bf16)
+    y_own, y_core, _ = lax.optimization_barrier((y_own, y_core, grad_out_low))
+    feed_result = links.seq_scatter([add_low([y_own[k], y_core[k]]) for k in range(n_seq)], add_low)
+    feed_result = jnp.concatenate(feed_result, axis=0) if isinstance(feed_result, list) else feed_result
+    layer_output = (residual + feed_result.astype(f32)).astype(bf16)
     grad_query, grad_kv_all = attend_back(offset_array, q_marked, grad_out_low, attended, kv, key_marks)
     kv_parts = [lax.dynamic_slice_in_dim(grad_kv_all, (seq ^ k) * local_len, local_len, 0) for k in range(n_seq)]
     grad_kv = links.seq_scatter(kv_parts, add_wide if n_seq != 4 else add_low)
     grad_kv = jnp.concatenate(grad_kv, axis=0) if isinstance(grad_kv, list) else grad_kv
-    grad_projected, head_gain_sums = rope_back(grad_query, grad_kv.astype(f32), projected, head_gains, tables)
+    grad_projected, head_gain_sums = rope_back(grad_query, grad_kv, projected, head_gains, tables)
     joined_term = dot(normed_low, grad_projected, TN).astype(bf16)
     grad_normed = dot(grad_projected, joined_all, NT)
     gain_one_grad = jnp.sum(grad_normed * flat * scale_one, axis=0)

time: 1060 us -> 797 us (0.75)
  waiting for transfers between devices: 291 us -> 163 us
  starting transfers between devices: 178 us -> 110 us
  local copies, waits for them, and re-layouts: 98.3 us -> 55.2 us
  other arithmetic: 75.9 us -> 57.6 us
    ppermute x81 -> x51, waiting for transfers between devices: 291 us -> 156 us  [send(): return lax.ppermute(values, AXES, pairs)]
    ppermute x81 -> x51, starting transfers between devices: 178 us -> 110 us  [send(): return lax.ppermute(values, AXES, pairs)]
    pallas_call x7 -> x3, Pallas kernels: 181 us -> 207 us  [the longest x1 193 us: feed_plane(): pl.pallas_call(functools.partial(feed_plane_kernel, n_seq, near), in_spec...]
    pallas_call x1, Pallas kernels: 55.8 us -> 36.1 us  [first_gather(): pl.pallas_call(functools.partial(first_gather_kernel, n_z, n_seq), in_spe...]
    slice x8 -> x0, local copies, waits for them, and re-layouts: 19.1 us -> none  [plane_scatter(): parts = [add_low([p[:local_len], links.core(p[local_len:])]) for p in parts]]
    unnamed x105 -> x99, local copies, waits for them, and re-layouts: 23.3 us -> 8.55 us
    convert_element_type x27 -> x17, other arithmetic: 26.3 us -> 19.9 us  [add_low(): functools.reduce(lambda a, b: a + b, [p.astype(f32) for p in parts])]
  transfers between devices with their start and end apart: 83 -> 53, of which waited for: 35 -> 26; matrix products, arithmetic and copies ran while one was open for 17% -> 15% of each run, Pallas kernels for 28% -> 12%
where the time goes in v4:
time: 797 us; the launch traced here: 790 us
  Pallas kernels  352 us (44%)
  waiting for transfers between devices  163 us (20%)
  starting transfers between devices  110 us (14%)
  other arithmetic  57.6 us (7%)
  local copies, waits for them, and re-layouts  55.2 us (7%)
  matrix products  35.8 us (4%)
  between operations  17.6 us (2%)
    pallas_call x1, Pallas kernels, feed_plane(): pl.pallas_call(functools.partial(feed_plane_kernel, n_seq, near), in_spec...  193 us
    ppermute x51, waiting for transfers between devices, send(): return lax.ppermute(values, AXES, pairs)  156 us
    ppermute x51, starting transfers between devices, send(): return lax.ppermute(values, AXES, pairs)  110 us
    pallas_call x1, Pallas kernels, spread_plane(): pl.pallas_call(functools.partial(spread_plane_kernel, n_z, n_seq), in_spe...  61.2 us
    pallas_call x1, Pallas kernels, first_gather(): pl.pallas_call(functools.partial(first_gather_kernel, n_z, n_seq), in_spe...  36.1 us
    dot_general x6, matrix products, dot(): return lax.dot_general(left, right, dims, preferred_element_type=f32)  35.8 us
    pallas_call x1, Pallas kernels, attend_back(): pl.pallas_call(functools.partial(attend_back_kernel, tq, tk), grid_spec=s...  28.4 us
    convert_element_type x17, other arithmetic, add_low(): functools.reduce(lambda a, b: a + b, [p.astype(f32) for p in parts])  19.9 us
  transfers between devices with their start and end apart: 53, of which 26 were waited for; matrix products, arithmetic and copies ran while one was open for 15% of the time, Pallas kernels for 12%

profile of v4, /device:TPU:0, one launch (start us, length us, event | category | flops | bytes accessed | tf_op | source)
XLA Modules:
  0.0 790.1 jit_solution(10750841720088491910)
XLA Ops:
  20.8 36.1 %first_gather.1 = (bf16[8,64,2304]{2,1,0:T(8,128)(2,1)}, bf16[4,64,2048]{2,1,0:T(8,128)(2,1)}, bf16[4,64,1280]{2,1,0:T(8,128)(2,1)}) custom-call(bf16[8,64,2304]{2,1,0:T(8,128)(2,1)} %reshape.247.shares, bf16[64,2048]{1,0:T(8,128)(2,1)} %pad_maximum_fusion.4.joined, bf16[64,1280]{1,0:T(8,128)(2,1)} %bitcast.188), custom_call_target="tpu_custom_call" | custom-call | tf_op jit(solution)/shard_map/first_gather/pallas_call | solution.py:441
  57.0 61.2 %spread_plane.1 = (bf16[4,8,64,2048]{3,2,1,0:T(8,128)(2,1)}, bf16[4,8,64,1280]{3,2,1,0:T(8,128)(2,1)}) custom-call(bf16[4,64,2048]{2,1,0:T(8,128)(2,1)} %get-tuple-element.25.joined_z, bf16[4,64,1280]{2,1,0:T(8,128)(2,1)} %get-tuple-element.26.out_z), custom_call_target="tpu_custom_call" | custom-call | tf_op jit(solution)/shard_map/spread_plane/pallas_call | solution.py:514
  122.6 7.4 fusion.3.projected
  130.0 5.5 rope.1.q
  145.0 10.7 %collective-permute-done = bf16[512,640]{1,0:T(8,128)(2,1)S(1)} collective-permute-done((bf16[512,640]{1,0:T(8,128)(2,1)}, bf16[512,640]{1,0:T(8,128)(2,1)S(1)}, u32[]{:S(2)}, u32[]{:S(2)}) %collective-permute-start) | collective-permute-done | bytes 655392 | tf_op jit(solution)/shard_map/ppermute | solution.py:895
  170.6 19.1 %attend.1 = (f32[512,1280]{1,0:T(8,128)}, bf16[20,512,128]{2,1,0:T(8,128)(2,1)}) custom-call(s32[1]{0:T(128)} %bitcast.1.offset, bf16[512,1920]{1,0:T(8,128)(2,1)} %copy-done.4, bf16[2048,640]{1,0:T(8,128)(2,1)} %constant_dynamic-update-slice_fusion.kv, bf16[2048,128]{1,0:T(8,128)(2,1)} %select_convert_fusion.key_marks, ...), custom_call_target="tpu_custom_call" | custom-call | flops 21474836480 | bytes 16777216 | tf_op jit(solution)/shard_map/attend/pallas_call | solution.py:244
  189.7 6.4 multiply_reduce_fusion
  198.8 16.2 %collective-permute-done.4.refs_1_ = bf16[512,2048]{1,0:T(8,128)(2,1)S(1)} collective-permute-done((bf16[512,2048]{1,0:T(8,128)(2,1)S(1)}, bf16[512,2048]{1,0:T(8,128)(2,1)S(1)}, u32[]{:S(2)}, u32[]{:S(2)}) %collective-permute-start.4) | collective-permute-done | bytes 2097184 | tf_op jit(solution)/shard_map/ppermute | solution.py:895
  216.2 6.3 all-gather.2.cloned.1.call-done.refs_4_
  222.5 193.2 %feed_plane.1 = (bf16[8,512,2048]{2,1,0:T(8,128)(2,1)}, bf16[8,512,2048]{2,1,0:T(8,128)(2,1)}, bf16[4,512,2048]{2,1,0:T(8,128)(2,1)}, bf16[4,512,2048]{2,1,0:T(8...) custom-call(bf16[512,2048]{1,0:T(8,128)(2,1)} %bitcast.180, ...), custom_call_target="tpu_custom_call" | custom-call | flops 128849018880 | bytes 100663296 | tf_op jit(solution)/shard_map/feed_plane/pallas_call | solution.py:826
  426.1 28.4 %attend_back.1 = (f32[512,1280]{1,0:T(8,128)}, bf16[2048,640]{1,0:T(8,128)(2,1)}) custom-call(s32[1]{0:T(128)} %bitcast.1.offset, bf16[20,512,128]{2,1,0:T(8,128)(2,1)} %get-tuple-element.37.q_marked, bf16[512,1280]{1,0:T(8,128)(2,1)} %convolution_convert_fusion.2.d_out, f32[512,1280]{1,0:T(8,128)} %get-tuple-element.28.out, ...), custom_call_target="tpu_custom_call" | custom-call | flops 42949672960 | bytes 16777216 | tf_op jit(solution)/shard_map/attend_back/pallas_call | solution.py:334
  456.7 17.0 %collective-permute-start.12 = (bf16[256,640]{1,0:T(8,128)(2,1)}, bf16[256,640]{1,0:T(8,128)(2,1)}, u32[]{:S(2)}, u32[]{:S(2)}) collective-permute-start(bf16[256,640]{1,0:T(8,128)(2,1)} %get-tuple-element.65), channel_id=1, source_target_pairs={{0,1},{1,0},{2,3},{3,2},{4,5},{5,4},{6,7},{7,6},{8,9},{9,8},{10,11... | collective-permute-start | bytes 983048 | tf_op jit(solution)/shard_map/ppermute | solution.py:895
  478.4 31.1 %collective-permute-start.16 = (bf16[256,640]{1,0:T(8,128)(2,1)S(1)}, bf16[256,640]{1,0:T(8,128)(2,1)S(1)}, u32[]{:S(2)}, u32[]{:S(2)}) collective-permute-start(bf16[256,640]{1,0:T(8,128)(2,1)S(1)} %get-tuple-element.67), channel_id=1, source_target_pairs={{0,2},{1,3},{2,0},{3,1},{4,6},{5,7},{6,4},{7,5},{8,10},{9,11},{10,... | collective-permute-start | bytes 983048 | tf_op jit(solution)/shard_map/ppermute | solution.py:895
  518.2 7.0 collective-permute-done.13
  527.0 10.6 %add_convert_fusion.4 = (bf16[1,512,2048]{2,1,0:T(8,128)(2,1)}, bf16[1,512,2048]{2,1,0:T(8,128)(2,1)}, bf16[1,512,2048]{2,1,0:T(8,128)(2,1)}, bf16[1,512,2048]{2,1,0:T(8,128)(2,1)}) fusion(bf16[4,512,2048]{2,1,0:T(8,128)(2,1)} %get-tuple-element.36, bf16[4,512,2048]{2,1,0:T(8,128)(2,1)} %get-tuple-element.35), kind=kLoop, calls=%fused_computation.42 | loop fusion | flops 16777216 | bytes 25165824 | tf_op jit(solution)/shard_map/convert_element_type | solution.py:944
  539.3 8.2 %rope_back.1 = (bf16[512,1920]{1,0:T(8,128)(2,1)S(1)}, f32[8,128]{1,0:T(8,128)S(1)}) custom-call(f32[512,1280]{1,0:T(8,128)S(1)} %copy-done.5, bf16[512,640]{1,0:T(8,128)(2,1)S(1)} %pad_maximum_fusion.1.dkv, f32[512,1920]{1,0:T(8,128)S(1)} %copy-done.1, f32[2,128]{1,0:T(2,128)S(1)} %copy-done.7, f32[2,512,128]{2,1,0:T(8,128)S(1)} %copy-done.3), custom_call_target="tpu_custom_call" | custom-call | flops 58982400 | bytes 9830400 | tf_op jit(solution)/shard_map/rope_back/pallas_call | solution.py:129
  547.7 6.8 fusion.23
  555.2 6.7 convolution_convert_fusion.1
  565.9 12.5 %copy.46 = bf16[2048,2048]{1,0:T(8,128)(2,1)} copy(bf16[2048,2048]{0,1:T(8,128)(2,1)} %pad_maximum_fusion) | data formatting | bytes 16777216 | tf_op jit(solution)/shard_map/concatenate | solution.py:1099
  578.4 5.0 dynamic-slice_bitcast_fusion
  589.3 5.2 fusion.26
  594.4 15.4 %collective-permute-done.10 = bf16[256,2048]{1,0:T(8,128)(2,1)S(1)} collective-permute-done((bf16[256,2048]{1,0:T(8,128)(2,1)S(1)}, bf16[256,2048]{1,0:T(8,128)(2,1)S(1)}, u32[]{:S(2)}, u32[]{:S(2)}) %collective-permute-start.10) | collective-permute-done | bytes 1048608 | tf_op jit(solution)/shard_map/ppermute | solution.py:895
  621.7 12.9 %collective-permute-done.8 = bf16[256,2048]{1,0:T(8,128)(2,1)} collective-permute-done((bf16[256,2048]{1,0:T(8,128)(2,1)}, bf16[256,2048]{1,0:T(8,128)(2,1)}, u32[]{:S(2)}, u32[]{:S(2)}) %collective-permute-start.8) | collective-permute-done | bytes 1048608 | tf_op jit(solution)/shard_map/ppermute | solution.py:895
  636.0 20.4 %collective-permute-done.11 = bf16[256,2048]{1,0:T(8,128)(2,1)} collective-permute-done((bf16[256,2048]{1,0:T(8,128)(2,1)S(1)}, bf16[256,2048]{1,0:T(8,128)(2,1)}, u32[]{:S(2)}, u32[]{:S(2)}) %collective-permute-start.11) | collective-permute-done | bytes 1048608 | tf_op jit(solution)/shard_map/ppermute | solution.py:895
  668.6 8.0 %collective-permute-done.23 = bf16[128,2048]{1,0:T(8,128)(2,1)S(1)} collective-permute-done((bf16[128,2048]{1,0:T(8,128)(2,1)S(1)}, bf16[128,2048]{1,0:T(8,128)(2,1)S(1)}, u32[]{:S(2)}, u32[]{:S(2)}) %collective-permute-start.23) | collective-permute-done | bytes 524320 | tf_op jit(solution)/shard_map/ppermute | solution.py:895
  694.9 7.1 collective-permute-done.24
  703.8 5.2 collective-permute-done.34
  711.3 6.4 collective-permute-done.21
  730.8 4.9 collective-permute-start.40
  737.5 6.4 collective-permute-start.27
  764.7 5.5 collective-permute-done.46
  772.8 7.8 collective-permute-done.49
  (324 shorter events, 172.2 us)
Async XLA Ops:
  7.2 215.4 %all-gather.2.cloned.1.call-start = ((), (), s32[]{:S(2)}) async-start(), calls=%async_computation.1 | async-start | bytes 11796480 | tf_op jit(solution)/shard_map/all_gather | solution.py:986
  56.9 697.4 %reduce-scatter.2.cloned.1.call-start = ((), (), s32[]{:S(2)}) async-start(), calls=%async_computation.2 | async-start | bytes 11796480 | tf_op jit(solution)/shard_map/reduce_scatter | solution.py:1045
  138.6 17.2 %collective-permute-start = (bf16[512,640]{1,0:T(8,128)(2,1)}, bf16[512,640]{1,0:T(8,128)(2,1)S(1)}, u32[]{:S(2)}, u32[]{:S(2)}) collective-permute-start(bf16[512,640]{1,0:T(8,128)(2,1)} %get-tuple-element.81), channel_id=1, source_target_pairs={{0,1},{1,0},{2,3},{3,2},{4,5},{5,4},{6,7},{7,6},{8,9},{9,8},{10,11... | collective-permute-start | bytes 1966088 | tf_op jit(solution)/shard_map/ppermute | solution.py:895
  139.3 19.2 %collective-permute-start.1 = (bf16[512,640]{1,0:T(8,128)(2,1)}, bf16[512,640]{1,0:T(8,128)(2,1)S(1)}, u32[]{:S(2)}, u32[]{:S(2)}) collective-permute-start(bf16[512,640]{1,0:T(8,128)(2,1)} %get-tuple-element.81), channel_id=1, source_target_pairs={{0,2},{1,3},{2,0},{3,1},{4,6},{5,7},{6,4},{7,5},{8,10},{9,11},{10,... | collective-permute-start | bytes 1966088 | tf_op jit(solution)/shard_map/ppermute | solution.py:895
  168.6 46.3 %collective-permute-start.4 = (bf16[512,2048]{1,0:T(8,128)(2,1)S(1)}, bf16[512,2048]{1,0:T(8,128)(2,1)S(1)}, u32[]{:S(2)}, u32[]{:S(2)}) collective-permute-start(bf16[512,2048]{1,0:T(8,128)(2,1)S(1)} %bitcast.181), channel_id=1, source_target_pairs={{0,1},{1,0},{2,3},{3,2},{4,5},{5,4},{6,7},{7,6},{8,9},{9,8},{10,11... | collective-permute-start | bytes 6291464 | tf_op jit(solution)/shard_map/ppermute | solution.py:895
  169.3 46.9 %collective-permute-start.5 = (bf16[512,2048]{1,0:T(8,128)(2,1)S(1)}, bf16[512,2048]{1,0:T(8,128)(2,1)}, u32[]{:S(2)}, u32[]{:S(2)}) collective-permute-start(bf16[512,2048]{1,0:T(8,128)(2,1)S(1)} %bitcast.182), channel_id=1, source_target_pairs={{0,2},{1,3},{2,0},{3,1},{4,6},{5,7},{6,4},{7,5},{8,10},{9,11},{10,... | collective-permute-start | bytes 6291464 | tf_op jit(solution)/shard_map/ppermute | solution.py:895
  456.7 52.8 %collective-permute-start.12 = (bf16[256,640]{1,0:T(8,128)(2,1)}, bf16[256,640]{1,0:T(8,128)(2,1)}, u32[]{:S(2)}, u32[]{:S(2)}) collective-permute-start(bf16[256,640]{1,0:T(8,128)(2,1)} %get-tuple-element.65), channel_id=1, source_target_pairs={{0,1},{1,0},{2,3},{3,2},{4,5},{5,4},{6,7},{7,6},{8,9},{9,8},{10,11... | collective-permute-start | bytes 983048 | tf_op jit(solution)/shard_map/ppermute | solution.py:895
  478.3 39.8 %collective-permute-start.14 = (bf16[256,640]{1,0:T(8,128)(2,1)}, bf16[256,640]{1,0:T(8,128)(2,1)S(1)}, u32[]{:S(2)}, u32[]{:S(2)}) collective-permute-start(bf16[256,640]{1,0:T(8,128)(2,1)} %get-tuple-element.66), channel_id=1, source_target_pairs={{0,1},{1,0},{2,3},{3,2},{4,5},{5,4},{6,7},{7,6},{8,9},{9,8},{10,11... | collective-permute-start | bytes 983048 | tf_op jit(solution)/shard_map/ppermute | solution.py:895
  478.4 39.8 %collective-permute-start.16 = (bf16[256,640]{1,0:T(8,128)(2,1)S(1)}, bf16[256,640]{1,0:T(8,128)(2,1)S(1)}, u32[]{:S(2)}, u32[]{:S(2)}) collective-permute-start(bf16[256,640]{1,0:T(8,128)(2,1)S(1)} %get-tuple-element.67), channel_id=1, source_target_pairs={{0,2},{1,3},{2,0},{3,1},{4,6},{5,7},{6,4},{7,5},{8,10},{9,11},{10,... | collective-permute-start | bytes 983048 | tf_op jit(solution)/shard_map/ppermute | solution.py:895
  518.1 94.8 %collective-permute-start.31 = (bf16[4,4,64,1280]{3,2,1,0:T(8,128)(2,1)}, bf16[4,4,64,1280]{3,2,1,0:T(8,128)(2,1)}, u32[]{:S(2)}, u32[]{:S(2)}) collective-permute-start(bf16[4,4,64,1280]{3,2,1,0:T(8,128)(2,1)} %dynamic-slice_bitcast_fusion.1), channel_id=1, source_target_pairs={{0,4},{1,5},{2,6},{3,7},{4,0},{5,1},{6,2},{7,3},{8,12},{9,13},{10,... | collective-permute-start | bytes 7864328 | tf_op jit(solution)/shard_map/ppermute | solution.py:895
  518.1 19.5 %collective-permute-start.15 = (bf16[256,640]{1,0:T(8,128)(2,1)S(1)}, bf16[256,640]{1,0:T(8,128)(2,1)S(1)}, u32[]{:S(2)}, u32[]{:S(2)}) collective-permute-start(bf16[256,640]{1,0:T(8,128)(2,1)S(1)} %get-tuple-element.68), channel_id=1, source_target_pairs={{0,2},{1,3},{2,0},{3,1},{4,6},{5,7},{6,4},{7,5},{8,10},{9,11},{10,... | collective-permute-start | bytes 983048 | tf_op jit(solution)/shard_map/ppermute | solution.py:895
  583.5 33.7 %collective-permute-start.18 = (bf16[4,4,64,2048]{3,2,1,0:T(8,128)(2,1)}, bf16[4,4,64,2048]{3,2,1,0:T(8,128)(2,1)S(1)}, u32[]{:S(2)}, u32[]{:S(2)}) collective-permute-start(bf16[4,4,64,2048]{3,2,1,0:T(8,128)(2,1)} %dynamic-slice_bitcast_fusion), channel_id=1, source_target_pairs={{0,4},{1,5},{2,6},{3,7},{4,0},{5,1},{6,2},{7,3},{8,12},{9,13},{10,... | collective-permute-start | bytes 12582920 | tf_op jit(solution)/shard_map/ppermute | solution.py:895
  583.7 26.2 %collective-permute-start.10 = (bf16[256,2048]{1,0:T(8,128)(2,1)S(1)}, bf16[256,2048]{1,0:T(8,128)(2,1)S(1)}, u32[]{:S(2)}, u32[]{:S(2)}) collective-permute-start(bf16[256,2048]{1,0:T(8,128)(2,1)S(1)} %get-tuple-element.80), channel_id=1, source_target_pairs={{0,2},{1,3},{2,0},{3,1},{4,6},{5,7},{6,4},{7,5},{8,10},{9,11},{10,... | collective-permute-start | bytes 3145736 | tf_op jit(solution)/shard_map/ppermute | solution.py:895
  586.0 26.0 %collective-permute-start.6 = (bf16[256,2048]{1,0:T(8,128)(2,1)S(1)}, bf16[256,2048]{1,0:T(8,128)(2,1)S(1)}, u32[]{:S(2)}, u32[]{:S(2)}) collective-permute-start(bf16[256,2048]{1,0:T(8,128)(2,1)S(1)} %get-tuple-element.79), channel_id=1, source_target_pairs={{0,1},{1,0},{2,3},{3,2},{4,5},{5,4},{6,7},{7,6},{8,9},{9,8},{10,11... | collective-permute-start | bytes 3145736 | tf_op jit(solution)/shard_map/ppermute | solution.py:895
  587.5 47.1 %collective-permute-start.8 = (bf16[256,2048]{1,0:T(8,128)(2,1)}, bf16[256,2048]{1,0:T(8,128)(2,1)}, u32[]{:S(2)}, u32[]{:S(2)}) collective-permute-start(bf16[256,2048]{1,0:T(8,128)(2,1)} %slice_bitcast_fusion.4), channel_id=1, source_target_pairs={{0,1},{1,0},{2,3},{3,2},{4,5},{5,4},{6,7},{7,6},{8,9},{9,8},{10,11... | collective-permute-start | bytes 3145736 | tf_op jit(solution)/shard_map/ppermute | solution.py:895
  609.8 26.1 %collective-permute-start.9 = (bf16[256,2048]{1,0:T(8,128)(2,1)S(1)}, bf16[256,2048]{1,0:T(8,128)(2,1)}, u32[]{:S(2)}, u32[]{:S(2)}) collective-permute-start(bf16[256,2048]{1,0:T(8,128)(2,1)S(1)} %slice_bitcast_fusion.2), channel_id=1, source_target_pairs={{0,2},{1,3},{2,0},{3,1},{4,6},{5,7},{6,4},{7,5},{8,10},{9,11},{10,... | collective-permute-start | bytes 3145736 | tf_op jit(solution)/shard_map/ppermute | solution.py:895
  612.0 44.3 %collective-permute-start.11 = (bf16[256,2048]{1,0:T(8,128)(2,1)S(1)}, bf16[256,2048]{1,0:T(8,128)(2,1)}, u32[]{:S(2)}, u32[]{:S(2)}) collective-permute-start(bf16[256,2048]{1,0:T(8,128)(2,1)S(1)} %fusion.27), channel_id=1, source_target_pairs={{0,1},{1,0},{2,3},{3,2},{4,5},{5,4},{6,7},{7,6},{8,9},{9,8},{10,11... | collective-permute-start | bytes 3145736 | tf_op jit(solution)/shard_map/ppermute | solution.py:895
  612.9 45.5 %collective-permute-start.7 = (bf16[256,2048]{1,0:T(8,128)(2,1)S(1)}, bf16[256,2048]{1,0:T(8,128)(2,1)}, u32[]{:S(2)}, u32[]{:S(2)}) collective-permute-start(bf16[256,2048]{1,0:T(8,128)(2,1)S(1)} %fusion.30), channel_id=1, source_target_pairs={{0,2},{1,3},{2,0},{3,1},{4,6},{5,7},{6,4},{7,5},{8,10},{9,11},{10,... | collective-permute-start | bytes 3145736 | tf_op jit(solution)/shard_map/ppermute | solution.py:895
  617.2 48.3 %collective-permute-start.36 = (bf16[128,1280]{1,0:T(8,128)(2,1)}, bf16[128,1280]{1,0:T(8,128)(2,1)}, u32[]{:S(2)}, u32[]{:S(2)}) collective-permute-start(bf16[128,1280]{1,0:T(8,128)(2,1)} %get-tuple-element.62), channel_id=1, source_target_pairs={{0,2},{1,3},{2,0},{3,1},{4,6},{5,7},{6,4},{7,5},{8,10},{9,11},{10,... | collective-permute-start | bytes 983048 | tf_op jit(solution)/shard_map/ppermute | solution.py:895
  634.6 42.0 %collective-permute-start.23 = (bf16[128,2048]{1,0:T(8,128)(2,1)S(1)}, bf16[128,2048]{1,0:T(8,128)(2,1)S(1)}, u32[]{:S(2)}, u32[]{:S(2)}) collective-permute-start(bf16[128,2048]{1,0:T(8,128)(2,1)S(1)} %get-tuple-element.56), channel_id=1, source_target_pairs={{0,2},{1,3},{2,0},{3,1},{4,6},{5,7},{6,4},{7,5},{8,10},{9,11},{10,... | collective-permute-start | bytes 1572872 | tf_op jit(solution)/shard_map/ppermute | solution.py:895
  662.1 16.4 %collective-permute-start.32 = (bf16[128,1280]{1,0:T(8,128)(2,1)S(1)}, bf16[128,1280]{1,0:T(8,128)(2,1)S(1)}, u32[]{:S(2)}, u32[]{:S(2)}) collective-permute-start(bf16[128,1280]{1,0:T(8,128)(2,1)S(1)} %copy-done.30), channel_id=1, source_target_pairs={{0,1},{1,0},{2,3},{3,2},{4,5},{5,4},{6,7},{7,6},{8,9},{9,8},{10,11... | collective-permute-start | bytes 983048 | tf_op jit(solution)/shard_map/ppermute | solution.py:895
  662.6 21.0 %collective-permute-start.35 = (bf16[128,1280]{1,0:T(8,128)(2,1)S(1)}, bf16[128,1280]{1,0:T(8,128)(2,1)S(1)}, u32[]{:S(2)}, u32[]{:S(2)}) collective-permute-start(bf16[128,1280]{1,0:T(8,128)(2,1)S(1)} %copy-done.29), channel_id=1, source_target_pairs={{0,2},{1,3},{2,0},{3,1},{4,6},{5,7},{6,4},{7,5},{8,10},{9,11},{10,... | collective-permute-start | bytes 983048 | tf_op jit(solution)/shard_map/ppermute | solution.py:895
  666.5 17.5 %collective-permute-start.37 = (bf16[128,1280]{1,0:T(8,128)(2,1)S(1)}, bf16[128,1280]{1,0:T(8,128)(2,1)S(1)}, u32[]{:S(2)}, u32[]{:S(2)}) collective-permute-start(bf16[128,1280]{1,0:T(8,128)(2,1)S(1)} %fusion.41), channel_id=1, source_target_pairs={{0,1},{1,0},{2,3},{3,2},{4,5},{5,4},{6,7},{7,6},{8,9},{9,8},{10,11... | collective-permute-start | bytes 983048 | tf_op jit(solution)/shard_map/ppermute | solution.py:895
  667.2 23.5 %collective-permute-start.19 = (bf16[128,2048]{1,0:T(8,128)(2,1)S(1)}, bf16[128,2048]{1,0:T(8,128)(2,1)S(1)}, u32[]{:S(2)}, u32[]{:S(2)}) collective-permute-start(bf16[128,2048]{1,0:T(8,128)(2,1)S(1)} %get-tuple-element.55), channel_id=1, source_target_pairs={{0,1},{1,0},{2,3},{3,2},{4,5},{5,4},{6,7},{7,6},{8,9},{9,8},{10,11... | collective-permute-start | bytes 1572872 | tf_op jit(solution)/shard_map/ppermute | solution.py:895
  676.6 18.3 %collective-permute-start.22 = (bf16[128,2048]{1,0:T(8,128)(2,1)S(1)}, bf16[128,2048]{1,0:T(8,128)(2,1)S(1)}, u32[]{:S(2)}, u32[]{:S(2)}) collective-permute-start(bf16[128,2048]{1,0:T(8,128)(2,1)S(1)} %get-tuple-element.53), channel_id=1, source_target_pairs={{0,2},{1,3},{2,0},{3,1},{4,6},{5,7},{6,4},{7,5},{8,10},{9,11},{10,... | collective-permute-start | bytes 1572872 | tf_op jit(solution)/shard_map/ppermute | solution.py:895
  678.5 23.4 %collective-permute-start.24 = (bf16[128,2048]{1,0:T(8,128)(2,1)S(1)}, bf16[128,2048]{1,0:T(8,128)(2,1)S(1)}, u32[]{:S(2)}, u32[]{:S(2)}) collective-permute-start(bf16[128,2048]{1,0:T(8,128)(2,1)S(1)} %fusion.33), channel_id=1, source_target_pairs={{0,1},{1,0},{2,3},{3,2},{4,5},{5,4},{6,7},{7,6},{8,9},{9,8},{10,11... | collective-permute-start | bytes 1572872 | tf_op jit(solution)/shard_map/ppermute | solution.py:895
  683.6 25.3 %collective-permute-start.34 = (bf16[128,1280]{1,0:T(8,128)(2,1)S(1)}, bf16[128,1280]{1,0:T(8,128)(2,1)S(1)}, u32[]{:S(2)}, u32[]{:S(2)}) collective-permute-start(bf16[128,1280]{1,0:T(8,128)(2,1)S(1)} %copy-done.28), channel_id=1, source_target_pairs={{0,1},{1,0},{2,3},{3,2},{4,5},{5,4},{6,7},{7,6},{8,9},{9,8},{10,11... | collective-permute-start | bytes 983048 | tf_op jit(solution)/shard_map/ppermute | solution.py:895
  684.3 24.6 %collective-permute-start.33 = (bf16[128,1280]{1,0:T(8,128)(2,1)S(1)}, bf16[128,1280]{1,0:T(8,128)(2,1)S(1)}, u32[]{:S(2)}, u32[]{:S(2)}) collective-permute-start(bf16[128,1280]{1,0:T(8,128)(2,1)S(1)} %get-tuple-element.58), channel_id=1, source_target_pairs={{0,2},{1,3},{2,0},{3,1},{4,6},{5,7},{6,4},{7,5},{8,10},{9,11},{10,... | collective-permute-start | bytes 983048 | tf_op jit(solution)/shard_map/ppermute | solution.py:895
  690.7 27.0 %collective-permute-start.21 = (bf16[128,2048]{1,0:T(8,128)(2,1)S(1)}, bf16[128,2048]{1,0:T(8,128)(2,1)S(1)}, u32[]{:S(2)}, u32[]{:S(2)}) collective-permute-start(bf16[128,2048]{1,0:T(8,128)(2,1)S(1)} %get-tuple-element.54), channel_id=1, source_target_pairs={{0,1},{1,0},{2,3},{3,2},{4,5},{5,4},{6,7},{7,6},{8,9},{9,8},{10,11... | collective-permute-start | bytes 1572872 | tf_op jit(solution)/shard_map/ppermute | solution.py:895
  702.4 15.3 %collective-permute-start.20 = (bf16[128,2048]{1,0:T(8,128)(2,1)S(1)}, bf16[128,2048]{1,0:T(8,128)(2,1)S(1)}, u32[]{:S(2)}, u32[]{:S(2)}) collective-permute-start(bf16[128,2048]{1,0:T(8,128)(2,1)S(1)} %get-tuple-element.52), channel_id=1, source_target_pairs={{0,2},{1,3},{2,0},{3,1},{4,6},{5,7},{6,4},{7,5},{8,10},{9,11},{10,... | collective-permute-start | bytes 1572872 | tf_op jit(solution)/shard_map/ppermute | solution.py:895
  763.1 17.6 %collective-permute-start.49 = (bf16[64,2304]{1,0:T(8,128)(2,1)S(1)}, bf16[64,2304]{1,0:T(8,128)(2,1)S(1)}, u32[]{:S(2)}, u32[]{:S(2)}) collective-permute-start(bf16[64,2304]{1,0:T(8,128)(2,1)S(1)} %get-tuple-element.70), channel_id=1, source_target_pairs={{0,6},{1,7},{2,4},{3,5},{4,2},{5,3},{6,0},{7,1},{8,14},{9,15},{10,... | collective-permute-start | bytes 884744 | tf_op jit(solution)/shard_map/ppermute | solution.py:895
  763.2 17.6 %collective-permute-start.50 = (bf16[64,2304]{1,0:T(8,128)(2,1)S(1)}, bf16[64,2304]{1,0:T(8,128)(2,1)S(1)}, u32[]{:S(2)}, u32[]{:S(2)}) collective-permute-start(bf16[64,2304]{1,0:T(8,128)(2,1)S(1)} %get-tuple-element.69), channel_id=1, source_target_pairs={{0,7},{1,6},{2,5},{3,4},{4,3},{5,2},{6,1},{7,0},{8,15},{9,14},{10,... | collective-permute-start | bytes 884744 | tf_op jit(solution)/shard_map/ppermute | solution.py:895
  (71 other events, 1019.0 us)
Sparse Core Ops, SparseCore 0:
  57.1 165.4 all-gather.1
  478.5 188.1 reduce-scatter.1

commit v5 on v4

--- a/solution.py
+++ b/solution.py
@@ -179,7 +179,7 @@
                 wide = pltpu.roll(wide, HEAD_DIM, axis=1)
             marked = jnp.where(lane1 < HEAD_DIM, wide, query_marks[part].astype(f32))
             rows[head * tq : (head + 1) * tq] = marked.astype(bf16)
-        first = offset[0] + tile * tq
+        first = offset[tile]
 
         def block(index, total, masked):
             span = pl.ds(pl.multiple_of(index * tk, tk), tk)
@@ -254,9 +254,59 @@
     )(offset, q, kv, key_marks, query_marks)
 
 
+def carry_sums(n_seq, parts, sides, folds, held, local, send, receive):
+    z, c, s = coordinates()
+    step = pl.program_id(0)
+    half = parts.shape[1] // 2
+    peer = lambda k: (z, c, s ^ k)
+    part = lambda k, i: parts.at[k, pl.ds(i * half, half)]
+    sems = (send, receive)
+    to_side = lambda source, k, i: remote(source, sides.at[k - 1, i], sems, 2 * (k - 1) + i, peer(k))
+    folded = n_seq == 4
+    direct = [(1, 0), (2, 1)] if folded else [(k, i) for k in range(1, n_seq) for i in range(2)]
+    fold = lambda i: remote(part(3, i), folds.at[i], sems, 4 + i, peer(1 + i))
+    load = lambda i: pltpu.make_async_copy(part(2 - i, i), held.at[i], local.at[i])
+    later = lambda i: to_side(folds.at[i], 2 - i, i)
+
+    @pl.when(step == 0)
+    def _():
+        greet([peer(k) for k in ((1, 2) if folded else range(1, n_seq))], [])
+        if folded:
+            for i in range(2):
+                fold(i).start()
+                load(i).start()
+
+    @pl.when(step == 1)
+    def _():
+        for k, i in direct:
+            to_side(part(k, i), k, i).start()
+
+    if folded:
+
+        @pl.when(step == 2)
+        def _():
+            for i in range(2):
+                load(i).wait()
+                fold(i).wait_recv()
+                folds[i] = (folds[i].astype(f32) + held[i].astype(f32)).astype(bf16)
+                later(i).start()
+
+    @pl.when(step == KV_HEADS - 1)
+    def _():
+        for k, i in direct:
+            to_side(part(k, i), k, i).wait()
+        if folded:
+            for i in range(2):
+                fold(i).wait_send()
+                later(i).wait()
+
+
 def attend_back_kernel(
-    tq, tk, offset, q_marked, d_out, out, kv, key_marks, dq, dkv, keys, vals, d_rows, rows, dk_sum, dv_sum
+    n_seq, tq, tk, q_marked, d_out, out, kv, key_marks, parts, dq, dkv, sides,
+    keys, vals, d_rows, rows, dk_sum, dv_sum, folds, held, local, send, receive,
 ):
+    carry_sums(n_seq, parts, sides, folds, held, local, send, receive)
+    offset = lax.axis_index("seq") * d_out.shape[0]
     local_len = d_out.shape[0]
     group = d_out.shape[1] // HEAD_DIM
     spread_kv(kv, key_marks, keys, vals)
@@ -276,7 +326,7 @@
             marks = jnp.where(lane1 == 0, one, jnp.where(lane1 == 1, two, jnp.where(lane1 == 2, three, 0.0)))
             d_rows[head * tq : (head + 1) * tq] = jnp.where(lane1 < HEAD_DIM, marks, wide).astype(bf16)
             rows[head * tq : (head + 1) * tq] = q_marked[head, part]
-        first = offset[0] + tile * tq
+        first = offset + tile * tq
 
         def block(index, total, masked):
             span = pl.ds(pl.multiple_of(index * tk, tk), tk)
@@ -302,25 +352,29 @@
     dkv[...] = jnp.where(lanes(dk_sum.shape) < HEAD_DIM, dk_sum[...], dv_sum[...]).astype(bf16)
 
 
-def attend_back(offset, q_marked, d_out, out, kv, key_marks):
+def attend_back(n_seq, q_marked, d_out, out, kv, key_marks, parts):
     tokens = d_out.shape[0]
+    side_count = 2 if n_seq == 4 else n_seq - 1
+    slots = 2 * side_count + 2
     keys = kv.shape[0]
     group = HEADS // KV_HEADS
     width = group * HEAD_DIM
     tq, tk = tokens, min(512, keys)
-    spec = pltpu.PrefetchScalarGridSpec(
-        num_scalar_prefetch=1,
+    return pl.pallas_call(
+        functools.partial(attend_back_kernel, n_seq, tq, tk),
         grid=(KV_HEADS,),
         in_specs=[
-            pl.BlockSpec((group, tokens, PAIR), lambda g, _: (g, 0, 0)),
-            pl.BlockSpec((tokens, width), lambda g, _: (0, g)),
-            pl.BlockSpec((tokens, width), lambda g, _: (0, g)),
-            pl.BlockSpec((keys, PAIR), lambda g, _: (0, g)),
-            pl.BlockSpec((keys, PAIR), lambda g, _: (0, 0)),
+            pl.BlockSpec((group, tokens, PAIR), lambda g: (g, 0, 0)),
+            pl.BlockSpec((tokens, width), lambda g: (0, g)),
+            pl.BlockSpec((tokens, width), lambda g: (0, g)),
+            pl.BlockSpec((keys, PAIR), lambda g: (0, g)),
+            pl.BlockSpec((keys, PAIR), lambda g: (0, 0)),
+            ANY,
         ],
         out_specs=[
-            pl.BlockSpec((tokens, width), lambda g, _: (0, g)),
-            pl.BlockSpec((keys, PAIR), lambda g, _: (0, g)),
+            pl.BlockSpec((tokens, width), lambda g: (0, g)),
+            pl.BlockSpec((keys, PAIR), lambda g: (0, g)),
+            ANY,
         ],
         scratch_shapes=[
             pltpu.VMEM((keys, PAIR), bf16),
@@ -329,19 +383,23 @@
             pltpu.VMEM((group * tq, PAIR), bf16),
             pltpu.VMEM((keys, PAIR), f32),
             pltpu.VMEM((keys, PAIR), f32),
-        ],
-    )
-    return pl.pallas_call(
-        functools.partial(attend_back_kernel, tq, tk),
-        grid_spec=spec,
+            pltpu.VMEM((2, tokens // 2, D), bf16),
+            pltpu.VMEM((2, tokens // 2, D), bf16),
+            pltpu.SemaphoreType.DMA((2,)),
+            pltpu.SemaphoreType.DMA((slots,)),
+            pltpu.SemaphoreType.DMA((slots,)),
+        ],
         out_shape=[
             jax.ShapeDtypeStruct((tokens, Q_WIDTH), f32),
             jax.ShapeDtypeStruct(kv.shape, bf16),
-        ],
-        compiler_params=pltpu.CompilerParams(vmem_limit_bytes=56 << 20),
+            jax.ShapeDtypeStruct((side_count, 2, tokens // 2, D), bf16),
+        ],
+        compiler_params=pltpu.CompilerParams(
+            collective_id=6, has_side_effects=True, vmem_limit_bytes=56 << 20
+        ),
         cost_estimate=attention_cost(tokens, 4),
         name="attend_back",
-    )(offset, q_marked, d_out, out, kv, key_marks)
+    )(q_marked, d_out, out, kv, key_marks, parts)
 
 
 def coordinates():
@@ -381,7 +439,7 @@
     )
 
 
-def first_gather_kernel(n_z, n_seq, shares, joined, out_rows, block, joined_z, out_z, local, send, receive):
+def first_gather_kernel(n_z, n_seq, expand, shrink, joined, out_rows, block, joined_z, out_z, local, send, receive):
     z, c, s = coordinates()
     plane = CORES * n_seq
     rows = joined.shape[0]
@@ -393,8 +451,17 @@
     mine = [
         pltpu.make_async_copy(joined, joined_z.at[z], local.at[0]),
         pltpu.make_async_copy(out_rows, out_z.at[z], local.at[1]),
-        pltpu.make_async_copy(shares.at[me], block.at[me], local.at[2]),
     ]
+    units = block.shape[2] // 3
+    half = expand.shape[1] // 2
+
+    def share(p):
+        start = pl.multiple_of(p * units, units)
+        other = pl.multiple_of(half + p * units, units)
+        sources = (expand.at[:, pl.ds(start, units)], expand.at[:, pl.ds(other, units)], shrink.at[:, pl.ds(start, units)])
+        return [(a, block.at[me, :, pl.ds(i * units, units)]) for i, a in enumerate(sources)]
+
+    mine += [pltpu.make_async_copy(a, b, local.at[2 + i]) for i, (a, b) in enumerate(share(me))]
     for copy in mine:
         copy.start()
     slot = 0
@@ -402,10 +469,10 @@
     for source, target in ((joined, joined_z), (out_rows, out_z)):
         ups, downs = [], []
         for k in range(1, n_z):
-            held = source if k == 1 else target.at[z - (k - 1)]
-            ups.append(remote(held, target.at[z - (k - 1)], sems, slot, above))
-            held = source if k == 1 else target.at[z + (k - 1)]
-            downs.append(remote(held, target.at[z + (k - 1)], sems, slot + 1, below))
+            held = source if k == 1 else target.at[(z + n_z - k + 1) % n_z]
+            ups.append(remote(held, target.at[(z + n_z - k + 1) % n_z], sems, slot, above))
+            held = source if k == 1 else target.at[(z + k - 1) % n_z]
+            downs.append(remote(held, target.at[(z + k - 1) % n_z], sems, slot + 1, below))
             slot += 2
         chains.append((ups, downs))
     for ups, downs in chains:
@@ -413,9 +480,10 @@
         pl.when(z > 0)(downs[0].start)
     sent = []
     for k, (tz, tc, ts) in enumerate(others):
-        copy = remote(shares.at[tc * n_seq + ts], block.at[me], sems, slot + k, (tz, tc, ts))
-        copy.start()
-        sent.append(copy)
+        for i, (a, b) in enumerate(share(tc * n_seq + ts)):
+            copy = remote(a, b, sems, slot + 3 * k + i, (tz, tc, ts))
+            copy.start()
+            sent.append(copy)
     for k in range(1, n_z):
         for ups, downs in chains:
             pl.when(z >= k)(ups[k - 1].wait_recv)
@@ -433,28 +501,29 @@
         copy.wait()
 
 
-def first_gather(n_z, n_seq, shares, joined, out_rows):
+def first_gather(n_z, n_seq, expand, shrink, joined, out_rows):
     plane = CORES * n_seq
     rows = joined.shape[0]
-    copies = 4 * (n_z - 1) + plane - 1
+    copies = 4 * (n_z - 1) + 3 * (plane - 1)
+    units = shrink.shape[1] // plane
     shape = lambda *dims: jax.ShapeDtypeStruct(dims, bf16)
     return pl.pallas_call(
         functools.partial(first_gather_kernel, n_z, n_seq),
-        in_specs=[VMEM] * 3,
+        in_specs=[VMEM] * 4,
         out_specs=[ANY] * 3,
         out_shape=[
-            shape(*shares.shape),
+            shape(plane, rows, 3 * units),
             shape(n_z, rows, joined.shape[1]),
             shape(n_z, rows, out_rows.shape[1]),
         ],
         scratch_shapes=[
-            pltpu.SemaphoreType.DMA((3,)),
+            pltpu.SemaphoreType.DMA((5,)),
             pltpu.SemaphoreType.DMA((copies,)),
             pltpu.SemaphoreType.DMA((copies,)),
         ],
         compiler_params=pltpu.CompilerParams(collective_id=0, has_side_effects=True),
         name="first_gather",
-    )(shares, joined, out_rows)
+    )(expand, shrink, joined, out_rows)
 
 
 def plane_routes(n_seq):
@@ -555,80 +624,104 @@
 
     w_copy = pltpu.make_async_copy(weights, w.at[:, : 3 * units], local.at[0])
     w_copy.start()
-    n_here = [(0, normed)]
-    d_here = [(mine(k), near[i]) for i, k in enumerate([0] + neighbours)]
-
-    def lies(here, gathered, index):
-        for place, ref in here:
-            if place == index:
+    tile_rows = [pl.ds(h * TILE, TILE) for h in range(steps)]
+    piece = lambda k, h: near[0].at[tile_rows[h]] if k == 0 else near[1 + (k - 1) * steps + h]
+    n_here = [(0, h, normed.at[tile_rows[h]]) for h in range(steps)]
+    d_here = [(mine(k), h, piece(k, h)) for k in range(n_seq) for h in range(steps)]
+
+    def lies(here, gathered, index, h):
+        for place, part, ref in here:
+            if (place, part) == (index, h):
                 return ref
-        return gathered.at[index]
+        return gathered.at[index, tile_rows[h]]
 
     n_sems, d_sems = (n_send, n_recv), (d_send, d_recv)
-    n_core = [remote(normed, n_all.at[1], n_sems, 0, core_peer)]
-    d_core = [remote(near[i], d_all.at[cross(k)], d_sems, i, core_peer) for i, k in enumerate([0] + neighbours)]
-    n_direct = [remote(normed, n_all.at[mine(k)], n_sems, 1 + i, peer(k)) for i, k in enumerate(neighbours)]
-    for copy in n_core + n_direct + d_core:
-        copy.start()
-    base = 1 + len(neighbours)
-    n_core += [remote(n_all.at[mine(k)], n_all.at[cross(k)], n_sems, base + i, core_peer) for i, k in enumerate(neighbours)]
-    base_n, base_d = 2 * len(neighbours) + 1, 1 + len(neighbours)
+    parts = [pl.ds(h * TILE, TILE) for h in range(2)] if folded else [pl.ds(0, length)]
+    count = len(neighbours) * len(parts)
+    n_own = remote(normed, n_all.at[1], n_sems, 0, core_peer)
+    d_core = [
+        [remote(piece(k, h), d_all.at[cross(k), tile_rows[h]], d_sems, k * steps + h, core_peer) for h in range(steps)]
+        for k in range(n_seq)
+    ]
+    n_direct, n_core = [], []
+    for h, part in enumerate(parts):
+        slots = [1 + h * len(neighbours) + i for i in range(len(neighbours))]
+        n_direct.append(
+            [remote(normed.at[part], n_all.at[mine(k), part], n_sems, i, peer(k)) for i, k in zip(slots, neighbours)]
+        )
+        n_core.append(
+            [
+                remote(n_all.at[mine(k), part], n_all.at[cross(k), part], n_sems, count + i, core_peer)
+                for i, k in zip(slots, neighbours)
+            ]
+        )
+    n_own.start()
+    for copies in n_direct + d_core:
+        for copy in copies:
+            copy.start()
+    n_fold, n_last = [], []
     if folded:
-        top, bottom = pl.ds(0, TILE), pl.ds(TILE, TILE)
-        diag = lambda ref, half: ref.at[mine(3), half]
-        n_fold = [
-            remote(n_all.at[mine(1), top], diag(n_all, top), n_sems, base_n, peer(2)),
-            remote(n_all.at[mine(2), bottom], diag(n_all, bottom), n_sems, base_n + 1, peer(1)),
-        ]
-        d_fold = [
-            remote(near[1].at[top], diag(d_all, top), d_sems, base_d, peer(2)),
-            remote(near[2].at[bottom], diag(d_all, bottom), d_sems, base_d + 1, peer(1)),
-        ]
-        n_core.append(remote(n_all.at[mine(3)], n_all.at[cross(3)], n_sems, base_n + 2, core_peer))
-        d_core.append(remote(d_all.at[mine(3)], d_all.at[cross(3)], d_sems, base_d + 2, core_peer))
-
-    def chunk_ready(q):
-        @pl.when(q == 1)
+        for h, part in enumerate(parts):
+            source, slot = n_all.at[mine(1 + h), part], 2 * count + 1 + h
+            n_fold.append(remote(source, n_all.at[mine(3), part], n_sems, slot, peer(2 - h)))
+            n_last.append(remote(n_all.at[mine(3), part], n_all.at[cross(3), part], n_sems, slot + 2, core_peer))
+
+    def tile_place(t):
+        if not folded:
+            return t // steps, t % steps
+        turn, j = t // 4, t % 4
+        middle = ((turn + 1) // 2) % 2
+        ends = 1 - middle
+        q = middle * (2 + j) + ends * ((turn // 3) * 6 + j % 2)
+        return q, middle * (turn // 2) + ends * (j // 2)
+
+    def d_came(k):
+        for copy in d_core[k]:
+            copy.wait_recv()
+
+    def part_came(h):
+        for copy in n_direct[h]:
+            copy.wait_recv()
+        for copy in n_core[h]:
+            copy.start()
+        if folded:
+            n_fold[h].start()
+
+    def tile_ready(t):
+        @pl.when(t == 1 if folded else t == steps)
         def _():
-            n_core[0].wait_recv()
-            d_core[0].wait_recv()
-
-        @pl.when(q == 2)
-        def _():
-            for i, copy in enumerate(n_direct):
-                copy.wait_recv()
-                n_core[1 + i].start()
-                if folded:
-                    n_fold[i].start()
-            if folded:
-                for copy in d_fold:
-                    copy.start()
-
-        for i, k in enumerate(neighbours):
-
-            pl.when(q == cross(k))(n_core[1 + i].wait_recv)
-            pl.when(q == cross(k))(d_core[1 + i].wait_recv)
-
+            n_own.wait_recv()
+            d_came(0)
+
+        for h in range(len(parts)):
+            first = 4 + 4 * h if folded else 2 * steps
+            pl.when(t == first)(lambda: part_came(h))
+            for i, k in enumerate(neighbours):
+                when = t == (first + 2 * i if folded else cross(k) * steps)
+                pl.when(when)(n_core[h][i].wait_recv)
+                if h == 0:
+                    pl.when(when)(lambda: d_came(k))
         if folded:
 
-            @pl.when(q == cross(3))
+            @pl.when(t == 12)
             def _():
-                for copy in n_fold + d_fold:
-                    copy.wait_recv()
-                n_core[3].start()
-                d_core[3].start()
-                n_core[3].wait_recv()
-                d_core[3].wait_recv()
+                for h in range(2):
+                    n_fold[h].wait_recv()
+                    n_last[h].start()
+                for h in range(2):
+                    n_last[h].wait_recv()
+                d_came(3)
 
     def tile_copies(t, step_of):
-        q, h = t // steps, t % steps
+        q, h = tile_place(t)
         rows = pl.ds(pl.multiple_of(h * TILE, TILE), TILE)
         for a, (here, gathered, tile) in enumerate(((n_here, n_all, n_tile), (d_here, d_all, d_tile))):
             copy = lambda source: pltpu.make_async_copy(source, tile.at[t % 2], tile_sem.at[a, t % 2])
             elsewhere = True
-            for index, ref in here:
-                pl.when(q == index)(lambda: step_of(copy(ref.at[rows])))
-                elsewhere = elsewhere & (q != index)
+            for index, part, ref in here:
+                pl.when((q == index) & (h == part))(lambda: step_of(copy(ref)))
+                if part == 0:
+                    elsewhere = elsewhere & (q != index)
             pl.when(elsewhere)(lambda: step_of(copy(gathered.at[q, rows])))
 
     def begin(copy):
@@ -665,7 +758,7 @@
     w_copy.wait()
 
     def tile_step(t, _):
-        q, h = t // steps, t % steps
+        q, h = tile_place(t)
         k, other = chunk_of(q)
         slot = t % 2
         tile_copies(t, finish)
@@ -678,14 +771,14 @@
         low = (silu * up).astype(bf16)
         d_gate = (d_hidden * up * sigmoid * (1.0 + gate * (1.0 - sigmoid))).astype(bf16)
         d_up = (d_hidden * silu).astype(bf16)
-        rows = pl.ds(pl.multiple_of(t * TILE, TILE), TILE)
+        rows = pl.ds(pl.multiple_of((q * steps + h) * TILE, TILE), TILE)
         hidden[rows] = low
         both[rows, :units] = d_gate
         both[rows, units:] = d_up
 
         @pl.when(t + 1 < chunks * steps)
         def _():
-            pl.when((t + 1) % steps == 0)(lambda: chunk_ready((t + 1) // steps))
+            tile_ready(t + 1)
             tile_copies(t + 1, begin)
 
         result = dot(low, w[:, 2 * units : 3 * units], NT).astype(bf16)
@@ -731,10 +824,10 @@
             for b in range(blocks):
                 for q in range(D // length):
                     first = pl.multiple_of((slot * 2 + a) * width + b * TILE, TILE)
-                    target = w.at[pl.ds(q * length, length), pl.ds(first, TILE)]
-                    index = b * (D // length) + q
-                    source = lies(here, gathered, index)
-                    copies.append((source.at[:, columns], target, (slot, a * blocks + b, q)))
+                    for h in range(steps):
+                        target = w.at[pl.ds(q * length + h * TILE, TILE), pl.ds(first, TILE)]
+                        source = lies(here, gathered, b * (D // length) + q, h)
+                        copies.append((source.at[:, columns], target, (slot, a * blocks + b, q * steps + h)))
         return [pltpu.make_async_copy(x, y, g_sem.at[i]) for x, y, i in copies]
 
     def g_store(j):
@@ -796,10 +889,9 @@
         out.start()
         out.wait()
 
-    for copy in n_direct + n_core + d_core:
-        copy.wait_send()
-    if folded:
-        for copy in n_fold + d_fold:
+    n_own.wait_send()
+    for copies in n_direct + n_core + d_core + [n_fold, n_last]:
+        for copy in copies:
             copy.wait_send()
     for key, half in prompt + late:
         to_peer(key, half).wait_send()
@@ -817,10 +909,11 @@
     chunks = CORES * n_seq
     tokens = chunks * length
     near = len(upstream)
-    count = near - 1
-    copies = 2 * count + 5
+    folded = (n_seq, steps) == (4, 2)
+    count = 2 if folded else n_seq - 1
+    copies = 13 if folded else 2 * count + 1
     w_columns = 3 * units if 3 * units > 4 * TILE * tokens // D else 4 * TILE * tokens // D
-    sums = 2 + near * steps
+    sums = 2 + count * steps
     shape = lambda *dims: jax.ShapeDtypeStruct(dims, bf16)
 
     outs = pl.pallas_call(
@@ -851,7 +944,7 @@
             pltpu.SemaphoreType.DMA((near + 3,)),
             pltpu.SemaphoreType.DMA((2, 2)),
             pltpu.SemaphoreType.DMA((steps,)),
-            pltpu.SemaphoreType.DMA((2, 2 * tokens // D, D // length)),
+            pltpu.SemaphoreType.DMA((2, 2 * tokens // D, D // TILE)),
             pltpu.SemaphoreType.DMA((copies,)),
             pltpu.SemaphoreType.DMA((copies,)),
             pltpu.SemaphoreType.DMA((copies,)),
@@ -874,6 +967,349 @@
     return outs[2:6]
 
 
+def last_sums_kernel(n_z, n_seq, out_term, joined_term, gain_term, shares, out_sum, joined_sum, exchanged, *scratch):
+    terms, core_sums, folds, sides, ups, downs = (scratch[2 * i : 2 * i + 2] for i in range(6))
+    out_parts, local, a_send, a_recv, c_send, c_recv, p_send, p_recv, u_send, u_recv, v_send, v_recv = scratch[12:]
+    z, c, s = coordinates()
+    plane = CORES * n_seq
+    me = c * n_seq + s
+    others = [(z, c ^ (k // n_seq), s ^ (k % n_seq)) for k in range(1, plane)]
+    core_peer, above, below = (z, 1 - c, s), (z + 1, c, s), (z - 1, c, s)
+    peer = lambda k: (z, c, s ^ k)
+    folded = n_seq == 4
+    half = n_z // 2
+    first, second = pl.ds(0, half), pl.ds(half, n_z - half)
+    width = joined_term.shape[4]
+    fetch = [
+        pltpu.make_async_copy(joined_term, terms[0].at[:, :, :, :, pl.ds(0, width)], local.at[0]),
+        pltpu.make_async_copy(gain_term, terms[0].at[:, :, :, :, pl.ds(width, PAIR)], local.at[1]),
+        pltpu.make_async_copy(out_term, terms[1], local.at[2]),
+    ]
+    for copy in fetch:
+        copy.start()
+    greet(others, [(z > 0, below), (z < n_z - 1, above)])
+    units = shares.shape[2] // 3
+    hidden_units = exchanged.shape[1] // 3
+
+    def piece(p, i):
+        start = pl.multiple_of(i * hidden_units + me * units, units)
+        return shares.at[p, :, pl.ds(i * units, units)], exchanged.at[:, pl.ds(start, units)]
+
+    kept = [pltpu.make_async_copy(*piece(me, i), local.at[3 + i]) for i in range(3)]
+    for copy in kept:
+        copy.start()
+    exchange = []
+    for k, (tz, tc, ts) in enumerate(others):
+        for i in range(3):
+            a, b = piece(tc * n_seq + ts, i)
+            exchange.append(remote(a, b, (a_send, a_recv), 3 * k + i, (tz, tc, ts)))
+
+    order = list(range(n_seq - 1, -1, -1))
+    to_core = lambda g, k: remote(
+        terms[g].at[:, 1 - c, s ^ k], core_sums[g].at[k], (c_send.at[g], c_recv.at[g]), k, core_peer
+    )
+
+    rows = out_parts.shape[1]
+    wholes = (pl.ds(0, n_z), pl.ds(0, rows))
+    halves = ((first, second), (pl.ds(0, rows // 2), pl.ds(rows // 2, rows // 2)))
+    held = (core_sums[0], out_parts)
+
+    def to_side(g, k, part, slot):
+        sems = (p_send.at[g], p_recv.at[g])
+        return remote(held[g].at[k, part], sides[g].at[k - 1, part], sems, slot, peer(k))
+
+    def to_fold(g, i):
+        sems = (p_send.at[g], p_recv.at[g])
+        return remote(held[g].at[3, halves[g][i]], folds[g].at[i], sems, 4 + i, peer(1 + i))
+
+    def prompt_copies(g):
+        if folded:
+            return [to_side(g, 1, halves[g][0], 0), to_side(g, 2, halves[g][1], 1)]
+        return [to_side(g, k, wholes[g], k - 1) for k in range(1, n_seq)]
+
+    def later_copies(g):
+        return [to_side(g, 2, halves[g][0], 2), to_side(g, 1, halves[g][1], 3)] if folded else []
+
+    def add_folds(g):
+        if folded:
+            later = later_copies(g)
+            for i in range(2):
+                k, part = 2 - i, halves[g][i]
+                to_fold(g, i).wait_recv()
+                held[g][k, part] = plus(held[g][k, part], folds[g][i])
+                later[i].start()
+
+    def side_total(g):
+        for copy in prompt_copies(g) + later_copies(g):
+            copy.wait_recv()
+        total = held[g][0].astype(f32)
+        for k in range(sides[g].shape[0]):
+            total = total + sides[g][k].astype(f32)
+        return total
+
+    def plus(one, two):
+        return (one.astype(f32) + two.astype(f32)).astype(bf16)
+
+    block = lambda g, d: core_sums[0].at[0, d] if g == 0 else core_sums[1].at[:, d]
+    up_copy = lambda g, k: remote(
+        block(g, (z + n_z - k) % n_z), ups[g].at[k - 1], (u_send.at[g], u_recv.at[g]), k - 1, above
+    )
+    down_copy = lambda g, k: remote(
+        block(g, (z + k) % n_z), downs[g].at[k - 1], (v_send.at[g], v_recv.at[g]), k - 1, below
+    )
+
+    def line_step(g, k):
+        if k > 1:
+
+            @pl.when((z >= 1) & (z <= k - 1))
+            def _():
+                up_copy(g, k - 1).wait_recv()
+
+            @pl.when((z >= 1) & (z <= k - 1) & (z < n_z - 1))
+            def _():
+                target = block(g, (z + n_z - k) % n_z)
+                target[...] = plus(target[...], ups[g][k - 2])
+
+            @pl.when((z < n_z - 1) & (z >= n_z - k))
+            def _():
+                down_copy(g, k - 1).wait_recv()
+
+            @pl.when((z < n_z - 1) & (z >= n_z - k) & (z > 0))
+            def _():
+                target = block(g, (z + k) % n_z)
+                target[...] = plus(target[...], downs[g][k - 2])
+
+        pl.when((z <= k - 1) & (z < n_z - 1))(lambda: up_copy(g, k).start())
+        pl.when((z >= n_z - k) & (z > 0))(lambda: down_copy(g, k).start())
+
+    def line_total(g, target):
+        own = block(g, z)
+        target[...] = own[...].astype(target.dtype)
+        if n_z > 1:
+
+            @pl.when(z >= 1)
+            def _():
+                up_copy(g, n_z - 1).wait_recv()
+                target[...] = (target[...].astype(f32) + ups[g][n_z - 2].astype(f32)).astype(target.dtype)
+
+            @pl.when(z < n_z - 1)
+            def _():
+                down_copy(g, n_z - 1).wait_recv()
+                target[...] = (target[...].astype(f32) + downs[g][n_z - 2].astype(f32)).astype(target.dtype)
+
+    for g in (1, 0):
+        for copy in fetch[2 * g : 2 + g]:
+            copy.wait()
+        for k in order:
+            to_core(g, k).start()
+    for copy in exchange[: len(exchange) // 2]:
+        copy.start()
+    for k in order:
+        to_core(1, k).wait_recv()
+        core_sums[1][k] = plus(terms[1][:, c, s ^ k], core_sums[1][k])
+    if n_z > 1:
+        line_step(1, 1)
+    prompt = prompt_copies(0)
+    for k in order:
+        to_core(0, k).wait_recv()
+        core_sums[0][k] = plus(terms[0][:, c, s ^ k], core_sums[0][k])
+        if (folded, k) == (True, 3):
+            to_fold(0, 0).start()
+            to_fold(0, 1).start()
+        elif k:
+            prompt[k - 1].start()
+    if n_z > 2:
+        line_step(1, 2)
+    add_folds(0)
+    for copy in exchange[len(exchange) // 2 :]:
+        copy.start()
+    for k in range(3, n_z):
+        line_step(1, k)
+    core_sums[0][0] = side_total(0).astype(bf16)
+    if n_z > 1:
+        line_step(0, 1)
+    line_total(1, out_parts)
+    if folded:
+        to_fold(1, 0).start()
+        to_fold(1, 1).start()
+    for copy in prompt_copies(1):
+        copy.start()
+    if n_z > 2:
+        line_step(0, 2)
+    add_folds(1)
+    for k in range(3, n_z):
+        line_step(0, k)
+    out_sum[...] = side_total(1)
+    line_total(0, joined_sum)
+
+    for g in range(2):
+        for k in order:
+            to_core(g, k).wait_send()
+        for copy in prompt_copies(g) + later_copies(g):
+            copy.wait_send()
+        if folded:
+            to_fold(g, 0).wait_send()
+            to_fold(g, 1).wait_send()
+        for k in range(1, n_z):
+            pl.when((z <= k - 1) & (z < n_z - 1))(lambda: up_copy(g, k).wait_send())
+            pl.when((z >= n_z - k) & (z > 0))(lambda: down_copy(g, k).wait_send())
+    for copy in exchange:
+        copy.wait()
+    for copy in kept:
+        copy.wait()
+
+
+def last_sums(n_z, n_seq, out_term, joined_term, gain_term, shares):
+    rows = out_term.shape[3]
+    widths = (joined_term.shape[4] + PAIR, out_term.shape[4])
+    half = n_z - n_z // 2
+    sides = 2 if n_seq == 4 else n_seq - 1
+    line = n_z - 1 if n_z > 1 else 1
+    buffers = lambda *lead: [pltpu.VMEM((*lead, rows, w), bf16) for w in widths]
+    line_buffers = [pltpu.VMEM((line, rows, widths[0]), bf16), pltpu.VMEM((line, n_seq, rows, widths[1]), bf16)]
+    sems = lambda *dims: [pltpu.SemaphoreType.DMA(dims), pltpu.SemaphoreType.DMA(dims)]
+    return pl.pallas_call(
+        functools.partial(last_sums_kernel, n_z, n_seq),
+        in_specs=[ANY, ANY, ANY, VMEM],
+        out_specs=[VMEM, VMEM, ANY],
+        out_shape=[
+            jax.ShapeDtypeStruct((rows, widths[1]), f32),
+            jax.ShapeDtypeStruct((rows, widths[0]), f32),
+            jax.ShapeDtypeStruct((rows, shares.shape[0] * shares.shape[2]), bf16),
+        ],
+        scratch_shapes=[
+            *buffers(n_z, CORES, n_seq),
+            *buffers(n_seq, n_z),
+            pltpu.VMEM((2, half, rows, widths[0]), bf16),
+            pltpu.VMEM((2, rows // 2, widths[1]), bf16),
+            pltpu.VMEM((sides, n_z, rows, widths[0]), bf16),
+            pltpu.VMEM((sides, rows, widths[1]), bf16),
+            *line_buffers,
+            *line_buffers,
+            pltpu.VMEM((n_seq, rows, widths[1]), bf16),
+            pltpu.SemaphoreType.DMA((6,)),
+            *sems(3 * (CORES * n_seq - 1)),
+            *sems(2, n_seq),
+            *sems(2, n_seq + 2),
+            *sems(2, line),
+            *sems(2, line),
+        ],
+        compiler_params=pltpu.CompilerParams(collective_id=3, has_side_effects=True, vmem_limit_bytes=56 << 20),
+        cost_estimate=pl.CostEstimate(flops=1 << 24, bytes_accessed=1 << 26, transcendentals=0),
+        name="last_sums",
+    )(out_term, joined_term, gain_term, shares)
+
+
+def kv_routes(n_seq):
+    if n_seq == 4:
+        return [(1, 0), (1, 1), (2, 0), (2, 1)], [(2, 1, 0), (1, 2, 1)]
+    return [(k, i) for k in range(1, n_seq) for i in range(2)], []
+
+
+def half_rows(half, s, i):
+    return pl.ds(pl.multiple_of((2 * s + i) * half, half), half)
+
+
+def kv_gather_kernel(n_seq, own, kv, local, send, receive):
+    z, c, s = coordinates()
+    half = own.shape[0] // 2
+    prompt, handed = kv_routes(n_seq)
+    peer = lambda k: (z, c, s ^ k)
+    greet([peer(k) for k in sorted({r[0] for r in prompt})], [])
+    rows = lambda k, i: kv.at[half_rows(half, s ^ k, i)]
+    mine = lambda i: own.at[pl.ds(i * half, half)]
+    sems = (send, receive)
+    copies = [remote(mine(i), rows(0, i), sems, slot, peer(k)) for slot, (k, i) in enumerate(prompt)]
+    later = [
+        remote(rows(k, i), rows(k, i), sems, len(prompt) + slot, peer(to)) for slot, (to, k, i) in enumerate(handed)
+    ]
+    for copy in copies:
+        copy.start()
+    kept = [pltpu.make_async_copy(mine(i), rows(0, i), local.at[i]) for i in range(2)]
+    for copy in kept:
+        copy.start()
+    for copy in copies:
+        copy.wait_recv()
+    for copy in later:
+        copy.start()
+    for copy in copies:
+        copy.wait_send()
+    for copy in later + kept:
+        copy.wait()
+
+
+def kv_gather(n_seq, own):
+    prompt, handed = kv_routes(n_seq)
+    count = len(prompt) + len(handed)
+    return pl.pallas_call(
+        functools.partial(kv_gather_kernel, n_seq),
+        in_specs=[VMEM],
+        out_specs=ANY,
+        out_shape=jax.ShapeDtypeStruct((n_seq * own.shape[0], own.shape[1]), bf16),
+        scratch_shapes=[
+            pltpu.SemaphoreType.DMA((2,)),
+            pltpu.SemaphoreType.DMA((count,)),
+            pltpu.SemaphoreType.DMA((count,)),
+        ],
+        compiler_params=pltpu.CompilerParams(collective_id=4, has_side_effects=True),
+        name="kv_gather",
+    )(own)
+
+
+def sum_kv_kernel(n_seq, parts, out, folds, sides, send, receive):
+    z, c, s = coordinates()
+    half = out.shape[0] // 2
+    peer = lambda k: (z, c, s ^ k)
+    part = lambda k, i: parts.at[half_rows(half, s ^ k, i)]
+    sems = (send, receive)
+    to_side = lambda source, k, i: remote(source, sides.at[k - 1, i], sems, 2 * (k - 1) + i, peer(k))
+    greet([peer(k) for k in ((1, 2) if n_seq == 4 else range(1, n_seq))], [])
+    if n_seq == 4:
+        fold = [remote(part(3, i), folds.at[i], sems, 4 + i, peer(1 + i)) for i in range(2)]
+        prompt = [to_side(part(1, 0), 1, 0), to_side(part(2, 1), 2, 1)]
+        later = [to_side(folds.at[0], 2, 0), to_side(folds.at[1], 1, 1)]
+        for copy in fold + prompt:
+            copy.start()
+        for i in range(2):
+            fold[i].wait_recv()
+            total = folds[i].astype(f32) + part(2 - i, i)[...].astype(f32)
+            folds[i] = total.astype(bf16)
+            later[i].start()
+        copies = prompt + later
+        for copy in fold:
+            copy.wait_send()
+    else:
+        copies = [to_side(part(k, i), k, i) for k in range(1, n_seq) for i in range(2)]
+        for copy in copies:
+            copy.start()
+    for copy in copies:
+        copy.wait()
+    for i in range(2):
+        total = part(0, i)[...].astype(f32)
+        for k in range(sides.shape[0]):
+            total = total + sides[k, i].astype(f32)
+        out[pl.ds(i * half, half)] = total
+
+
+def sum_kv(n_seq, parts):
+    length, width = parts.shape[0] // n_seq, parts.shape[1]
+    sides = 2 if n_seq == 4 else n_seq - 1
+    return pl.pallas_call(
+        functools.partial(sum_kv_kernel, n_seq),
+        in_specs=[VMEM],
+        out_specs=VMEM,
+        out_shape=jax.ShapeDtypeStruct((length, width), f32),
+        scratch_shapes=[
+            pltpu.VMEM((2, length // 2, width), bf16),
+            pltpu.VMEM((sides, 2, length // 2, width), bf16),
+            pltpu.SemaphoreType.DMA((2 * sides + 2,)),
+            pltpu.SemaphoreType.DMA((2 * sides + 2,)),
+        ],
+        compiler_params=pltpu.CompilerParams(collective_id=5, has_side_effects=True, vmem_limit_bytes=32 << 20),
+        name="sum_kv",
+    )(parts)
+
+
 class Links:
     def __init__(self, n_dp, n_seq):
         self.n_z = n_dp // CORES
@@ -905,47 +1341,6 @@
 
     def down(self, values, first, last):
         return self.send(values, lambda z, c, s: (z - 1, c, s) if first <= z <= last else None)
-
-    def seq_gather(self, values):
-        if self.n_seq != 4:
-            return [[values]] + [[self.peer(values, k)] for k in range(1, self.n_seq)]
-        half = values.shape[0] // 2
-        one, two = self.peer(values, 1), self.peer(values, 2)
-        top = self.peer(one[:half], 2)
-        bottom = self.peer(two[half:], 1)
-        return [[values], [one], [two], [top, bottom]]
-
-    def seq_scatter(self, parts, add):
-        if self.n_seq != 4:
-            return add([parts[0]] + [self.peer(parts[k], k) for k in range(1, self.n_seq)])
-        half = parts[0].shape[0] // 2
-        top = self.peer(parts[3][:half], 1)
-        bottom = self.peer(parts[3][half:], 2)
-        two = [self.peer(add([parts[2][:half], top]), 2), self.peer(parts[2][half:], 2)]
-        one = [self.peer(parts[1][:half], 1), self.peer(add([parts[1][half:], bottom]), 1)]
-        return [add([parts[0][:half], two[0], one[0]]), add([parts[0][half:], two[1], one[1]])]
-
-    def line_scatter(self, full, add):
-        n = self.n_z
-        z, _, _ = self.place()
-        rows = full.shape[0] // n
-        take = lambda d: lax.dynamic_slice_in_dim(full, jnp.clip(d, 0, n - 1) * rows, rows, 0)
-        above = below = None
-        for k in range(1, n):
-            one, two = take(z + n - k), take(z - n + k)
-            one = one if above is None else add([one, above])
-            two = two if below is None else add([two, below])
-            above = self.up(one, 0, k - 1)
-            below = self.down(two, n - k, n - 1)
-        return [take(z)] + ([above, below] if n > 1 else [])
-
-
-def add_low(parts):
-    return functools.reduce(lambda a, b: a + b, [p.astype(f32) for p in parts]).astype(bf16)
-
-
-def add_wide(parts):
-    return functools.reduce(lambda a, b: a + b, [p.astype(f32) for p in parts])
 
 
 def body(
@@ -969,24 +1364,23 @@
     rows = D // devices
     units = FF // plane
     own_gains = GAINS // devices
-    offset = seq * local_len
 
     kv_columns = joined_weight[:, Q_WIDTH:].reshape(rows, 2, KV_HEADS, HEAD_DIM).transpose(0, 2, 1, 3)
     gain_block = jnp.pad(norm_gains, (0, rows * PAIR - own_gains)).reshape(rows, PAIR)
     joined_block = jnp.concatenate(
         [joined_weight[:, :Q_WIDTH], kv_columns.reshape(rows, 2 * KV_WIDTH), gain_block], axis=1
     )
-    shrink_rows = shrink_weight.T
-    shares = jnp.concatenate(
-        [expand_weight.reshape(rows, 2, plane, units), shrink_rows.reshape(rows, 1, plane, units)], axis=1
+    block, joined_z, output_z = first_gather(
+        n_z, n_seq, expand_weight, shrink_weight.T, joined_block, output_weight.T
     )
-    shares = shares.transpose(2, 0, 1, 3).reshape(plane, rows, 3 * units)
-    block, joined_z, output_z = first_gather(n_z, n_seq, shares, joined_block, output_weight.T)
     lines = [[a * CORES + c for a in range(n_z)] for c in range(CORES)]
     weights = lax.all_gather(
         block.reshape(plane * rows, 3 * units), "dp", axis=0, tiled=True, axis_index_groups=lines
     )
     joined_all, output_all = spread_plane(n_z, n_seq, joined_z, output_z)
+    cot = cotangent.reshape(local_len, D)
+    top, bottom = cot[:TILE], cot[TILE:]
+    early_top, early_bottom, joined_all = lax.optimization_barrier((top, bottom, joined_all))
     joined_all = joined_all.reshape(D, QKV + PAIR)
     output_all = output_all.reshape(D, Q_WIDTH)
     gains = joined_all[:, QKV:].reshape(devices, rows * PAIR)[:, :own_gains].reshape(GAINS).astype(f32)
@@ -999,7 +1393,9 @@
 
     half = HEAD_DIM // 2
     frequency = 10000.0 ** (-jnp.arange(half, dtype=f32) / half)
-    angles = (offset + jnp.arange(local_len, dtype=jnp.int32)).astype(f32)[:, None] * frequency[None, :]
+    offset = seq * local_len
+    positions = offset + jnp.arange(local_len, dtype=jnp.int32)
+    angles = positions.astype(f32)[:, None] * frequency[None, :]
     cosine, sine = jnp.cos(angles), jnp.sin(angles)
     tables = jnp.stack(
         [jnp.concatenate([cosine] * 4, axis=1), jnp.concatenate([-sine, sine, -sine, sine], axis=1)]
@@ -1016,63 +1412,48 @@
     carries = (mark >= MARK) & (mark < MARK + 3)
     key_marks = jnp.where(other, -1024.0, jnp.where(carries, 1.0, 0.0)).astype(bf16)
     query_marks = lax.dynamic_slice_in_dim(same.astype(bf16), offset, local_len, 0)
-    offset_array = jnp.reshape(offset, (1,)).astype(jnp.int32)
+    starts = jnp.reshape(offset, (1,)).astype(jnp.int32)
 
     flat = tokens.reshape(local_len, D).astype(f32)
     scale_one = rms_scale(flat)
     normed_low = (flat * scale_one * gain_one).astype(bf16)
     projected = dot(normed_low, joined_all, NN)
     turned = rope(projected, head_gains, tables)
-    own_kv = turned[:, Q_WIDTH:]
-    kv = jnp.zeros((ROW_LEN, 2 * KV_WIDTH), bf16)
-    for k, parts in enumerate(links.seq_gather(own_kv)):
-        start = (seq ^ k) * local_len
-        for part in parts:
-            kv = lax.dynamic_update_slice_in_dim(kv, part, start, 0)
-            start = start + part.shape[0]
-    attended, q_marked = attend(offset_array, turned, kv, key_marks, query_marks)
+    kv = kv_gather(n_seq, turned[:, Q_WIDTH:])
+    upstream_low = cotangent.reshape(local_len, D)
+    upstream_near = [upstream_low]
+    if (n_seq, local_len) == (4, 2 * TILE):
+        late_top, late_bottom, kv = lax.optimization_barrier((top, bottom, kv))
+        one, two = links.peer(early_top, 1), links.peer(early_bottom, 2)
+        one_late, two_late = links.peer(late_bottom, 1), links.peer(late_top, 2)
+        kv, one, two = lax.optimization_barrier((kv, one, two))
+        upstream_near += [one, one_late, two_late, two, links.peer(one, 2), links.peer(two, 1)]
+    else:
+        upstream_near += [links.peer(upstream_low, k) for k in range(1, n_seq)]
+    attended, q_marked = attend(starts, turned, kv, key_marks, query_marks)
     attended_low = attended.astype(bf16)
     residual = flat + dot(attended_low, output_all, NT)
     scale_two = rms_scale(residual)
     normed_two = (residual * scale_two * gain_two).astype(bf16)
 
-    upstream_low = cotangent.reshape(local_len, D)
-    early, _ = lax.optimization_barrier((upstream_low, kv))
-    near = [1, 2] if (n_seq, local_len) == (4, 2 * TILE) else list(range(1, n_seq))
-    upstream_near = [upstream_low] + [links.peer(early, k) for k in near]
     y_own, y_core, back, share_gradient = feed_plane(n_seq, normed_two, upstream_near, weights)
     grad_normed_two = back.astype(f32)
     mine = lax.psum_scatter(
         share_gradient, "dp", scatter_dimension=0, tiled=True, axis_index_groups=lines
     )
-    expand_gradient = jnp.zeros((rows, 2 * FF), f32)
-    shrink_gradient = jnp.zeros((rows, FF), f32)
-    for k in range(plane):
-        p = (core ^ (k // n_seq)) * n_seq + (seq ^ (k % n_seq))
-        piece = lax.dynamic_slice_in_dim(mine, p * rows, rows, 0)
-        if k:
-            piece = links.send(piece, lambda a, c, s: (a, c ^ (k // n_seq), s ^ (k % n_seq)))
-        piece = piece.astype(f32)
-        put = lambda a, part, start: lax.dynamic_update_slice_in_dim(a, part, start + p * units, 1)
-        expand_gradient = put(expand_gradient, piece[:, :units], 0)
-        expand_gradient = put(expand_gradient, piece[:, units : 2 * units], FF)
-        shrink_gradient = put(shrink_gradient, piece[:, 2 * units :], 0)
-    shrink_gradient = shrink_gradient.T
-
     upstream = upstream_low.astype(f32)
     gain_two_grad = jnp.sum(grad_normed_two * residual * scale_two, axis=0)
     grad_residual = upstream + norm_back(grad_normed_two, residual, scale_two, gain_two)
     grad_attn_low = grad_residual.astype(bf16)
     output_term = dot(grad_attn_low, attended_low, TN).astype(bf16)
     grad_out_low = dot(grad_attn_low, output_all, NN).astype(bf16)
-    y_own, y_core, _ = lax.optimization_barrier((y_own, y_core, grad_out_low))
-    feed_result = links.seq_scatter([add_low([y_own[k], y_core[k]]) for k in range(n_seq)], add_low)
-    feed_result = jnp.concatenate(feed_result, axis=0) if isinstance(feed_result, list) else feed_result
-    layer_output = (residual + feed_result.astype(f32)).astype(bf16)
-    grad_query, grad_kv_all = attend_back(offset_array, q_marked, grad_out_low, attended, kv, key_marks)
-    kv_parts = [lax.dynamic_slice_in_dim(grad_kv_all, (seq ^ k) * local_len, local_len, 0) for k in range(n_seq)]
-    grad_kv = links.seq_scatter(kv_parts, add_wide if n_seq != 4 else add_low)
-    grad_kv = jnp.concatenate(grad_kv, axis=0) if isinstance(grad_kv, list) else grad_kv
+    feed_parts = (y_own.astype(f32) + y_core.astype(f32)).astype(bf16)
+    grad_query, grad_kv_all, feed_sides = attend_back(
+        n_seq, q_marked, grad_out_low, attended, kv, key_marks, feed_parts
+    )
+    feed_result = feed_parts[0].astype(f32) + jnp.sum(feed_sides.astype(f32), axis=0).reshape(local_len, D)
+    layer_output = (residual + feed_result).astype(bf16)
+    grad_kv = sum_kv(n_seq, grad_kv_all)
     grad_projected, head_gain_sums = rope_back(grad_query, grad_kv, projected, head_gains, tables)
     joined_term = dot(normed_low, grad_projected, TN).astype(bf16)
     grad_normed = dot(grad_projected, joined_all, NT)
@@ -1082,21 +1463,18 @@
     gain_key_grad = head_gain_sums[1, :HEAD_DIM]
     gain_grads = jnp.concatenate([gain_one_grad, gain_query_grad, gain_key_grad, gain_two_grad])
     gain_block = jnp.pad(gain_grads.reshape(devices, own_gains), ((0, 0), (0, rows * PAIR - own_gains)))
-    gain_block = gain_block.reshape(devices * rows, PAIR).astype(bf16)
-
-    def scatter_all(full):
-        width = full.shape[1]
-        full = full.reshape(n_z, CORES, n_seq, rows, width)
-        other = links.core(lax.dynamic_index_in_dim(full, 1 - core, 1, keepdims=False))
-        full = add_low([lax.dynamic_index_in_dim(full, core, 1, keepdims=False), other])
-        full = full.transpose(1, 0, 2, 3).reshape(n_seq, n_z * rows, width)
-        parts = [lax.dynamic_index_in_dim(full, seq ^ k, 0, keepdims=False) for k in range(n_seq)]
-        out = links.seq_scatter(parts, add_low)
-        out = jnp.concatenate(out, axis=0) if isinstance(out, list) else out
-        return add_wide(links.line_scatter(out, add_low))
-
-    output_gradient = scatter_all(output_term).T
-    joined_sum = scatter_all(jnp.concatenate([joined_term, gain_block], axis=1))
+    by_owner = lambda a: a.astype(bf16).reshape(n_z, CORES, n_seq, rows, -1)
+    output_sum, joined_sum, exchanged = last_sums(
+        n_z,
+        n_seq,
+        by_owner(output_term),
+        by_owner(joined_term),
+        by_owner(gain_block.reshape(D, PAIR)),
+        mine.reshape(plane, rows, 3 * units),
+    )
+    output_gradient = output_sum.T
+    expand_gradient = exchanged[:, : 2 * FF].astype(f32)
+    shrink_gradient = exchanged[:, 2 * FF :].T.astype(f32)
     kv_sum = joined_sum[:, Q_WIDTH:QKV].reshape(rows, KV_HEADS, 2, HEAD_DIM).transpose(0, 2, 1, 3)
     joined_gradient = jnp.concatenate([joined_sum[:, :Q_WIDTH], kv_sum.reshape(rows, 2 * KV_WIDTH)], axis=1)
     gains_gradient = joined_sum[:, QKV:].reshape(rows * PAIR)[:own_gains]

time: 797 us -> 678 us (0.85)
  Pallas kernels: 352 us -> 533 us
  waiting for transfers between devices: 163 us -> 16.4 us
  starting transfers between devices: 110 us -> 6.24 us
  local copies, waits for them, and re-layouts: 55.2 us -> 23.9 us
  other arithmetic: 57.6 us -> 33.8 us
  matrix products: 35.8 us -> 43.8 us
    pallas_call x1 -> x4, Pallas kernels: 28.4 us -> 216 us  [the longest x1 79 us: last_sums(): pl.pallas_call(functools.partial(last_sums_kernel, n_z, n_seq), in_specs=...]
    ppermute x51 -> x6, waiting for transfers between devices: 156 us -> 9.73 us  [send(): return lax.ppermute(values, AXES, pairs)]
    ppermute x51 -> x6, starting transfers between devices: 110 us -> 6.16 us  [send(): return lax.ppermute(values, AXES, pairs)]
    concatenate x1 -> x0, local copies, waits for them, and re-layouts: 12.5 us -> none  [body(): joined_sum = scatter_all(jnp.concatenate([joined_term, gain_block], axis=1))]
    transpose x4 -> x0, other arithmetic: 9.09 us -> none  [the longest x2 4.94 us: scatter_all(): full = full.transpose(1, 0, 2, 3).reshape(n_seq, n_z * rows, width)]
    squeeze x2 -> x0, local copies, waits for them, and re-layouts: 8.66 us -> none  [scatter_all(): lax.dynamic_index_in_dim(full, 1 - core, 1, keepdims=False)]
    dot_general x6, matrix products: 35.8 us -> 43.8 us  [dot(): return lax.dot_general(left, right, dims, preferred_element_type=f32)]
    convert_element_type x25 -> x5, other arithmetic: 20.2 us -> 13.6 us  [the longest x1 5.09 us: body(): feed_parts = (y_own.astype(f32) + y_core.astype(f32)).astype(bf16)]
  transfers between devices with their start and end apart: 53 -> 8, of which waited for: 26 -> 2; matrix products, arithmetic and copies ran while one was open for 15% -> 12% of each run, Pallas kernels for 12% -> 34%
where the time goes in v5:
time: 678 us; the launch traced here: 674 us
  Pallas kernels  533 us (79%)
  matrix products  43.8 us (6%)
  other arithmetic  33.8 us (5%)
  local copies, waits for them, and re-layouts  23.9 us (4%)
  between operations  16.8 us (2%)
  waiting for transfers between devices  16.4 us (2%)
    pallas_call x1, Pallas kernels, feed_plane(): pl.pallas_call(functools.partial(feed_plane_kernel, n_seq, near), in_spec...  186 us
    pallas_call x1, Pallas kernels, last_sums(): pl.pallas_call(functools.partial(last_sums_kernel, n_z, n_seq), in_specs=...  79 us
    pallas_call x1, Pallas kernels, attend_back(): pl.pallas_call(functools.partial(attend_back_kernel, n_seq, tq, tk), grid...  78.4 us
    pallas_call x1, Pallas kernels, spread_plane(): pl.pallas_call(functools.partial(spread_plane_kernel, n_z, n_seq), in_spe...  61 us
    dot_general x6, matrix products, dot(): return lax.dot_general(left, right, dims, preferred_element_type=f32)  43.8 us
    pallas_call x1, Pallas kernels, first_gather(): pl.pallas_call(functools.partial(first_gather_kernel, n_z, n_seq), in_spe...  36.4 us
    pallas_call x1, Pallas kernels, sum_kv(): pl.pallas_call(functools.partial(sum_kv_kernel, n_seq), in_specs=[VMEM],...  32.5 us
    pallas_call x1, Pallas kernels, kv_gather(): pl.pallas_call(functools.partial(kv_gather_kernel, n_seq), in_specs=[VMEM...  26 us
  transfers between devices with their start and end apart: 8, of which 2 were waited for; matrix products, arithmetic and copies ran while one was open for 12% of the time, Pallas kernels for 34%

profile of v5, /device:TPU:0, one launch (start us, length us, event | category | flops | bytes accessed | tf_op | source)
XLA Modules:
  0.0 673.6 jit_solution(14340845549359391365)
XLA Ops:
  11.1 36.4 %first_gather.1 = (bf16[8,64,2304]{2,1,0:T(8,128)(2,1)}, bf16[4,64,2048]{2,1,0:T(8,128)(2,1)}, bf16[4,64,1280]{2,1,0:T(8,128)(2,1)}) custom-call(bf16[64,12288]{1,0:T(8,128)(2,1)} %expand.1, bf16[64,6144]{1,0:T(8,128)(2,1)} %bitcast.79, bf16[64,2048]{1,0:T(8,128)(2,1)} %pad_maximum_fusion.2.joined, bf16[64,1280]{1,0:T(8,128)(2,1)} %bitcast.82), custom_call_target="tpu_custom_call" | custom-call | tf_op jit(solution)/shard_map/first_gather/pallas_call | solution.py:510
  47.5 61.0 %spread_plane.1 = (bf16[4,8,64,2048]{3,2,1,0:T(8,128)(2,1)}, bf16[4,8,64,1280]{3,2,1,0:T(8,128)(2,1)}) custom-call(bf16[4,64,2048]{2,1,0:T(8,128)(2,1)} %get-tuple-element.35.joined_z, bf16[4,64,1280]{2,1,0:T(8,128)(2,1)} %get-tuple-element.36.out_z), custom_call_target="tpu_custom_call" | custom-call | tf_op jit(solution)/shard_map/spread_plane/pallas_call | solution.py:583
  117.1 7.3 %fusion.2.projected = f32[512,1920]{1,0:T(8,128)S(1)} fusion(bf16[2048,2048]{1,0:T(8,128)(2,1)} %bitcast.84, bf16[1,512,2048]{2,1,0:T(8,128)(2,1)S(1)} %copy-done.17, f32[2048]{0:T(1024)S(1)} %get-tuple-element.70, f32[512]{0:T(512)S(1)} %get-tuple-element.77), kind=kOutput, calls=%fused_computation.12 | convolution fusion | flops 4030726144 | bytes 13903872 | tf_op jit(solution)/shard_map/dot_general | solution.py:36
  124.4 5.5 rope.1.q
  129.9 1.9 copy-done
  132.8 26.0 %kv_gather.1.kv = bf16[2048,640]{1,0:T(8,128)(2,1)} custom-call(bf16[512,640]{1,0:T(8,128)(2,1)} %slice.115.own), custom_call_target="tpu_custom_call" | custom-call | tf_op jit(solution)/shard_map/kv_gather/pallas_call | solution.py:1244
  158.8 1.5 collective-permute-start.2
  168.2 19.0 %attend.1 = (f32[512,1280]{1,0:T(8,128)}, bf16[20,512,128]{2,1,0:T(8,128)(2,1)}) custom-call(s32[1]{0:T(128)} %bitcast.1.offset, bf16[512,1920]{1,0:T(8,128)(2,1)} %copy-done.4, bf16[2048,640]{1,0:T(8,128)(2,1)} %kv_gather.1.kv, bf16[2048,128]{1,0:T(8,128)(2,1)} %select_convert_fusion.key_marks, bf16[512,128]{1,0:T(8,128)(2,1)} %and_convert_fusion.query_marks), custom_call_target="tpu_custom_call" | custom-call | flops 21474836480 | bytes 16777216 | tf_op jit(solution)/shard_map/attend/pallas_call | solution.py:244
  187.2 5.9 multiply_reduce_fusion
  193.1 1.9 copy-done.9
  195.0 1.7 multiply_convert_fusion.refs_7_
  196.7 9.7 %collective-permute-done.4.refs_5_ = bf16[256,2048]{1,0:T(8,128)(2,1)} collective-permute-done((bf16[256,2048]{1,0:T(8,128)(2,1)}, bf16[256,2048]{1,0:T(8,128)(2,1)}, u32[]{:S(2)}, u32[]{:S(2)}) %collective-permute-start.4) | collective-permute-done | bytes 1048608 | tf_op jit(solution)/shard_map/ppermute | solution.py:1331
  206.5 6.6 all-gather.2.cloned.1.call-done.refs_8_
  213.1 186.2 %feed_plane.1 = (bf16[8,512,2048]{2,1,0:T(8,128)(2,1)}, bf16[8,512,2048]{2,1,0:T(8,128)(2,1)}, bf16[4,512,2048]{2,1,0:T(8,128)(2,1)}, bf16[4,512,2048]{2,1,0:T(8...) custom-call(bf16[512,2048]{1,0:T(8,128)(2,1)} %bitcast.71, ...), custom_call_target="tpu_custom_call" | custom-call | flops 128849018880 | bytes 100663296 | tf_op jit(solution)/shard_map/feed_plane/pallas_call | solution.py:919
  399.4 1.5 copy-done.14
  400.9 4.3 fusion.10
  406.5 8.6 %convolution_convert_fusion.2.d_out = bf16[512,1280]{1,0:T(8,128)(2,1)} fusion(bf16[2048,1280]{1,0:T(8,128)(2,1)} %bitcast.87, f32[512,2048]{1,0:T(8,128)S(1)} %fusion.7), kind=kOutput, calls=%fused_computation.38 | convolution fusion | flops 2686058496 | bytes 10747904 | tf_op jit(solution)/shard_map/dot_general | solution.py:36
  415.1 5.1 add_convert_fusion.parts
  420.2 78.4 %attend_back.1 = (f32[512,1280]{1,0:T(8,128)}, bf16[2048,640]{1,0:T(8,128)(2,1)}, bf16[2,2,256,2048]{3,2,1,0:T(8,128)(2,1)}) custom-call(bf16[20,512,128]{2,1,0:T(8,128)(2,1)} %get-tuple-element.52.q_marked, bf16[512,1280]{1,0:T(8,128)(2,1)} %convolution_convert_fusion.2.d_out, f32[512,1280]{1,0:T(8,128)} %get-tuple-element.43.out, ...), custom_call_target="tpu_custom_call" | custom-call | flops 42949672960 | bytes 16777216 | tf_op jit(solution)/shard_map/attend_back/pallas_call | solution.py:363
  498.7 1.9 copy-done.6
  500.6 32.5 %sum_kv.1.dkv = f32[512,640]{1,0:T(8,128)S(1)} custom-call(bf16[2048,640]{1,0:T(8,128)(2,1)S(1)} %copy-done.6), custom_call_target="tpu_custom_call" | custom-call | tf_op jit(solution)/shard_map/sum_kv/pallas_call | solution.py:1297
  533.1 1.7 copy-done.5
  534.8 8.6 %rope_back.1 = (bf16[512,1920]{1,0:T(8,128)(2,1)S(1)}, f32[8,128]{1,0:T(8,128)S(1)}) custom-call(f32[512,1280]{1,0:T(8,128)S(1)} %copy-done.5, f32[512,640]{1,0:T(8,128)S(1)} %sum_kv.1.dkv, f32[512,1920]{1,0:T(8,128)S(1)} %copy-done.1, f32[2,128]{1,0:T(2,128)S(1)} %copy-done.8, f32[2,512,128]{2,1,0:T(8,128)S(1)} %copy-done.3), custom_call_target="tpu_custom_call" | custom-call | flops 58982400 | bytes 9830400 | tf_op jit(solution)/shard_map/rope_back/pallas_call | solution.py:129
  543.5 10.1 %fusion.20 = (bf16[2048]{0:T(1024)(128)(2,1)S(1)}, f32[512]{0:T(512)S(1)}, f32[512,2048]{1,0:T(8,128)}) fusion(bf16[1,512,2048]{2,1,0:T(8,128)(2,1)S(1)} %copy-done.19, f32[512]{0:T(512)S(1)} %copy-done.27, f32[2048]{0:T(1024)S(1)} %copy-done.25, bf16[512,1920]{1,0:T(8,128)(2,1)S(1)} %get-tuple-element.57, bf16[2048,2048]{1,0:T(8,128)(2,1)} %bitcast.85), kind=kOutput, calls=%fused_computation.32 | convolution fusion | flops 4033869312 | bytes 16138240 | tf_op jit(solution)/shard_map/dot_general | solution.py:36
  554.8 3.7 convert_reduce_fusion
  559.1 4.8 convolution_convert_fusion
  563.9 4.2 fusion.22
  568.1 2.5 fusion.23
  570.5 7.1 %convolution_convert_fusion.1 = bf16[2048,1920]{1,0:T(8,128)(2,1)} fusion(bf16[512,1920]{1,0:T(8,128)(2,1)S(1)} %get-tuple-element.57, bf16[1,512,2048]{2,1,0:T(8,128)(2,1)S(1)} %copy-done.20, f32[2048]{0:T(1024)S(1)} %copy-done.25, f32[512]{0:T(512)S(1)} %copy-done.27), kind=kOutput, calls=%fused_computation.9 | convolution fusion | flops 4034658304 | bytes 11937792 | tf_op jit(solution)/shard_map/dot_general | solution.py:36
  577.7 79.0 %last_sums.1 = (f32[64,1280]{1,0:T(8,128)}, f32[64,2048]{1,0:T(8,128)}, bf16[64,18432]{1,0:T(8,128)(2,1)}) custom-call(bf16[4,2,4,64,1280]{4,3,2,1,0:T(8,128)(2,1)} %bitcast.73, bf16[4,2,4,64,1920]{4,3,2,1,0:T(8,128)(2,1)} %bitcast.72, bf16[4,2,4,64,128]{4,3,2,1,0:T(8,128)(2,1)} %bitcast.76, bf16[8,64,2304]{2,1,0:T(8,128)(2,1)} %bitcast.75), custom_call_target="tpu_custom_call" | custom-call | flops 16777216 | bytes 67108864 | tf_op jit(solution)/shard_map/last_sums/pallas_call | solution.py:1171
  659.5 2.4 convert_bitcast_fusion
  661.9 1.9 slice_convert_fusion
  (139 shorter events, 27.9 us)
Async XLA Ops:
  7.2 205.9 %all-gather.2.cloned.1.call-start = ((), (), s32[]{:S(2)}) async-start(), calls=%async_computation.1 | async-start | bytes 11796480 | tf_op jit(solution)/shard_map/all_gather | solution.py:1377
  9.0 99.5 %copy-start.15 = (bf16[1,512,2048]{2,1,0:T(8,128)(2,1)S(1)}, bf16[1,512,2048]{2,1,0:T(8,128)(2,1)}, u32[]{:S(2)}) copy-start(bf16[1,512,2048]{2,1,0:T(8,128)(2,1)} %param.15) | copy-start | bytes 6291460
  47.5 530.2 %reduce-scatter.2.cloned.1.call-start = ((), (), s32[]{:S(2)}) async-start(), calls=%async_computation.2 | async-start | bytes 11796480 | tf_op jit(solution)/shard_map/reduce_scatter | solution.py:1441
  110.0 5.3 copy-start.17
  110.0 56.1 %collective-permute-start = (bf16[256,2048]{1,0:T(8,128)(2,1)}, bf16[256,2048]{1,0:T(8,128)(2,1)}, u32[]{:S(2)}, u32[]{:S(2)}) collective-permute-start(bf16[256,2048]{1,0:T(8,128)(2,1)} %get-tuple-element.47), channel_id=1, source_target_pairs={{0,1},{1,0},{2,3},{3,2},{4,5},{5,4},{6,7},{7,6},{8,9},{9,8},{10,11... | collective-permute-start | bytes 3145736 | tf_op jit(solution)/shard_map/ppermute | solution.py:1331
  110.7 55.4 %collective-permute-start.1 = (bf16[256,2048]{1,0:T(8,128)(2,1)}, bf16[256,2048]{1,0:T(8,128)(2,1)}, u32[]{:S(2)}, u32[]{:S(2)}) collective-permute-start(bf16[256,2048]{1,0:T(8,128)(2,1)} %get-tuple-element.46), channel_id=1, source_target_pairs={{0,2},{1,3},{2,0},{3,1},{4,6},{5,7},{6,4},{7,5},{8,10},{9,11},{10,... | collective-permute-start | bytes 3145736 | tf_op jit(solution)/shard_map/ppermute | solution.py:1331
  113.8 10.6 %copy-start.7 = (f32[2,128]{1,0:T(2,128)}, f32[2,128]{1,0:T(2,128)S(1)}, u32[]{:S(2)}) copy-start(f32[2,128]{1,0:T(2,128)S(1)} %pad_maximum_fusion.3.gains) | copy-start | bytes 3076
  115.3 9.0 %copy-start.2 = (f32[2,512,128]{2,1,0:T(8,128)}, f32[2,512,128]{2,1,0:T(8,128)S(1)}, u32[]{:S(2)}) copy-start(f32[2,512,128]{2,1,0:T(8,128)S(1)} %pad_maximum_fusion.tables) | copy-start | bytes 1572868
  124.4 36.5 %copy-start.29 = (s32[1,4]{1,0:T(1,128)S(1)}, s32[1,4]{1,0:T(1,128)}, u32[]{:S(2)}) copy-start(s32[1,4]{1,0:T(1,128)} %param.14) | copy-start | bytes 52
  131.8 36.3 %copy-start.4 = (bf16[512,1920]{1,0:T(8,128)(2,1)}, bf16[512,1920]{1,0:T(8,128)(2,1)S(1)}, u32[]{:S(2)}) copy-start(bf16[512,1920]{1,0:T(8,128)(2,1)S(1)} %rope.1.q) | copy-start | bytes 5898244
  158.8 37.9 %collective-permute-start.2 = (bf16[256,2048]{1,0:T(8,128)(2,1)}, bf16[256,2048]{1,0:T(8,128)(2,1)S(1)}, u32[]{:S(2)}, u32[]{:S(2)}) collective-permute-start(bf16[256,2048]{1,0:T(8,128)(2,1)} %get-tuple-element.46), channel_id=1, source_target_pairs={{0,1},{1,0},{2,3},{3,2},{4,5},{5,4},{6,7},{7,6},{8,9},{9,8},{10,11... | collective-permute-start | bytes 3145736 | tf_op jit(solution)/shard_map/ppermute | solution.py:1331
  160.3 36.4 %collective-permute-start.3 = (bf16[256,2048]{1,0:T(8,128)(2,1)}, bf16[256,2048]{1,0:T(8,128)(2,1)}, u32[]{:S(2)}, u32[]{:S(2)}) collective-permute-start(bf16[256,2048]{1,0:T(8,128)(2,1)} %get-tuple-element.47), channel_id=1, source_target_pairs={{0,2},{1,3},{2,0},{3,1},{4,6},{5,7},{6,4},{7,5},{8,10},{9,11},{10,... | collective-permute-start | bytes 3145736 | tf_op jit(solution)/shard_map/ppermute | solution.py:1331
  166.1 40.3 %collective-permute-start.4 = (bf16[256,2048]{1,0:T(8,128)(2,1)}, bf16[256,2048]{1,0:T(8,128)(2,1)}, u32[]{:S(2)}, u32[]{:S(2)}) collective-permute-start(bf16[256,2048]{1,0:T(8,128)(2,1)} %collective-permute-done.refs_1_), channel_id=1, source_target_pairs={{0,2},{1,3},{2,0},{3,1},{4,6},{5,7},{6,4},{7,5},{8,10},{9,11},{10,... | collective-permute-start | bytes 3145736 | tf_op jit(solution)/shard_map/ppermute | solution.py:1331
  167.6 38.9 %collective-permute-start.5 = (bf16[256,2048]{1,0:T(8,128)(2,1)}, bf16[256,2048]{1,0:T(8,128)(2,1)}, u32[]{:S(2)}, u32[]{:S(2)}) collective-permute-start(bf16[256,2048]{1,0:T(8,128)(2,1)} %collective-permute-done.1.refs_4_), channel_id=1, source_target_pairs={{0,1},{1,0},{2,3},{3,2},{4,5},{5,4},{6,7},{7,6},{8,9},{9,8},{10,11... | collective-permute-start | bytes 3145736 | tf_op jit(solution)/shard_map/ppermute | solution.py:1331
  168.2 19.0 %copy-start.18 = (bf16[1,512,2048]{2,1,0:T(8,128)(2,1)S(1)}, bf16[1,512,2048]{2,1,0:T(8,128)(2,1)}, u32[]{:S(2)}) copy-start(bf16[1,512,2048]{2,1,0:T(8,128)(2,1)} %param.8) | copy-start | bytes 6291460
  196.7 16.4 %copy-start.30 = (bf16[256,2048]{1,0:T(8,128)(2,1)}, bf16[256,2048]{1,0:T(8,128)(2,1)S(1)}, u32[]{:S(2)}) copy-start(bf16[256,2048]{1,0:T(8,128)(2,1)S(1)} %collective-permute-done.2.refs_2_) | copy-start | bytes 3145732
  399.3 5.8 copy-start.10
  399.3 5.8 copy-start.16
  405.2 9.9 %slice-start = ((s8[8388608]{0:T(1024)(128)(4,1)}), s8[4194304]{0:T(1024)(128)(4,1)S(1)}, s32[]{:S(2)}) async-start(s8[8388608]{0:T(1024)(128)(4,1)} %bitcast.67), calls=%async_computation.3 | async-start | bytes 8388608
  405.2 9.9 %slice-start.2 = ((s8[8388608]{0:T(1024)(128)(4,1)}), s8[4194304]{0:T(1024)(128)(4,1)S(1)}, s32[]{:S(2)}) async-start(s8[8388608]{0:T(1024)(128)(4,1)} %bitcast.69), calls=%async_computation.5 | async-start | bytes 8388608
  406.4 8.6 %copy-start.12 = (f32[512,2048]{1,0:T(8,128)}, f32[512,2048]{1,0:T(8,128)S(1)}, u32[]{:S(2)}) copy-start(f32[512,2048]{1,0:T(8,128)S(1)} %fusion.7) | copy-start | bytes 12582916
  406.5 8.6 %slice-start.1 = ((s8[8388608]{0:T(1024)(128)(4,1)}), s8[4194304]{0:T(1024)(128)(4,1)S(1)}, s32[]{:S(2)}) async-start(s8[8388608]{0:T(1024)(128)(4,1)} %bitcast.67), calls=%async_computation.4 | async-start | bytes 8388608
  406.5 8.6 %slice-start.3 = ((s8[8388608]{0:T(1024)(128)(4,1)}), s8[4194304]{0:T(1024)(128)(4,1)S(1)}, s32[]{:S(2)}) async-start(s8[8388608]{0:T(1024)(128)(4,1)} %bitcast.69), calls=%async_computation.6 | async-start | bytes 8388608
  420.2 112.8 %copy-start.3 = (f32[2,512,128]{2,1,0:T(8,128)S(1)}, f32[2,512,128]{2,1,0:T(8,128)}, u32[]{:S(2)}) copy-start(f32[2,512,128]{2,1,0:T(8,128)} %copy-done.2) | copy-start | bytes 1572868
  420.2 112.8 %copy-start.8 = (f32[2,128]{1,0:T(2,128)S(1)}, f32[2,128]{1,0:T(2,128)}, u32[]{:S(2)}) copy-start(f32[2,128]{1,0:T(2,128)} %copy-done.7) | copy-start | bytes 3076
  498.6 34.4 %copy-start.1 = (f32[512,1920]{1,0:T(8,128)S(1)}, f32[512,1920]{1,0:T(8,128)}, u32[]{:S(2)}) copy-start(f32[512,1920]{1,0:T(8,128)} %copy-done) | copy-start | bytes 11796484
  534.8 8.7 %copy-start.19 = (bf16[1,512,2048]{2,1,0:T(8,128)(2,1)S(1)}, bf16[1,512,2048]{2,1,0:T(8,128)(2,1)}, u32[]{:S(2)}) copy-start(bf16[1,512,2048]{2,1,0:T(8,128)(2,1)} %param.8) | copy-start | bytes 6291460
  534.8 8.7 %copy-start.25 = (f32[2048]{0:T(1024)S(1)}, f32[2048]{0:T(1024)}, u32[]{:S(2)}) copy-start(f32[2048]{0:T(1024)} %copy-done.24) | copy-start | bytes 24580
  534.8 8.7 %copy-start.27 = (f32[512]{0:T(512)S(1)}, f32[512]{0:T(512)}, u32[]{:S(2)}) copy-start(f32[512]{0:T(512)} %copy-done.26) | copy-start | bytes 6148
  554.8 4.3 copy-start.31
  559.1 4.8 copy-start.11
  656.7 5.2 copy-start.22
  (12 other events, 30.4 us)
Sparse Core Ops, SparseCore 0:
  47.6 165.4 all-gather.1
  399.5 160.1 reduce-scatter.1
